TPU v7x, 32 devices: a whole 2x2x4 slice. The times are simulated.
32 devices in a mesh: grp: 4 (over y, x), tile: 8 (over z, core).
Axes of the slice: x: 2, y: 2, z: 4, core: 2. Of those that a mesh axis runs over, the one named last changes fastest.
Arguments:
- features: bfloat16 [8192, 128], P(('grp', 'tile')), may hold values from -6 to 6
- source_rows: int32 [27, 64, 128], P(None, ('grp', 'tile')), may hold values from -1 to 127, as said below
- target_codes: int32 [27, 64], P(None, ('grp', 'tile')), may hold values from 0 to 5, as said below
- block_count: int32 [32], P(('grp', 'tile')), may hold values from 1 to 2, as said below
- weight_one: bfloat16 [27, 128, 128], replicated, may hold values from -0.125 to 0.125
- weight_two: bfloat16 [27, 128, 128], replicated, may hold values from -0.125 to 0.125
- out_cotangent: bfloat16 [8192, 128], P(('grp', 'tile')), may hold values from -6 to 6
Outputs:
- block_out: bfloat16 [8192, 128], P(('grp', 'tile'))
- input_grad: bfloat16 [8192, 128], P(('grp', 'tile'))
- wgrad_one: float32 [3456, 128], P('grp')
- wgrad_two: float32 [3456, 128], P('grp')
Inputs may be any that keep to these rules, and one draw needn't show every extreme that they name: `source_rows`: entry [k, j, r] is the row of source block j that reaches row r of its target block under offset k, or -1 for none. `target_codes`: a code s * 2 + b names block b of tile t - 1 + s of the same group, t being the source block's tile; offset k = 9 (dx + 1) + 3 (dy + 1) + (dz + 1); s = 1 except s = 0 for offsets with dz = -1 from block 0 of a tile, and s = 2 for offsets with dz = +1 from the last active block of a tile. Blocks of a tile from block_count on are empty.
All inputs are finite; a program needn't handle non-finite values.
Results may differ from a plain program's by a relative error of at most 0.025.
Values may be sent and summed in bfloat16 or wider, within the bound.
No kernel may reach another device: no remote copies, remote signals or barrier semaphores. Data moves between devices by JAX's collectives and lax.ppermute only.
A program may use at most 64 MiB of HBM per device.

v0:
```python
import jax
import jax.numpy as jnp
from jax import lax
from jax.sharding import PartitionSpec as P


def passed_along(value, axis, by):
    count = lax.axis_size(axis)
    pairs = [(i, i + by) for i in range(count) if 0 <= i + by < count]
    return lax.ppermute(value, axis, pairs)


def silu_grad(values):
    sigma = jax.nn.sigmoid(values)
    return sigma * (1.0 + values * (1.0 - sigma))


def gather_rows(field, selector):
    offsets, blocks_dev, block_rows, _ = selector.shape
    blocked = field.reshape(blocks_dev, block_rows, field.shape[1])
    picked = jnp.einsum("kbrs,bsc->kbrc", selector, blocked, preferred_element_type=jnp.float32)
    return picked.astype(jnp.bfloat16).reshape(offsets, blocks_dev * block_rows, field.shape[1])


def spread_terms(picked, weights, codes):
    offsets, total_rows, channels = picked.shape
    blocks_dev = codes.shape[1]
    block_rows = total_rows // blocks_dev
    partial_value = jnp.einsum("kmc,kcd->kmd", picked, weights, preferred_element_type=jnp.float32)
    one_hot = (
        codes[:, :, None] == jnp.arange(3 * blocks_dev, dtype=jnp.int32)[None, None, :]
    ).astype(jnp.float32)
    buffer = jnp.einsum(
        "kis,kirc->src",
        one_hot,
        partial_value.reshape(offsets, blocks_dev, block_rows, -1),
        precision=lax.Precision.HIGHEST,
    )
    return buffer.reshape(3, blocks_dev * block_rows, -1)


def join_partials(buffer):
    from_next = passed_along(buffer[0], "tile", -1)
    from_prev = passed_along(buffer[2], "tile", 1)
    return buffer[1] + from_next + from_prev


def neighbor_rows(grads):
    before = passed_along(grads, "tile", 1)
    after = passed_along(grads, "tile", -1)
    return jnp.concatenate([before, grads, after], axis=0)


def pull_back(stacked, codes, picked, selector_wide, weights):
    offsets, total_rows, channels = picked.shape
    blocks_dev = codes.shape[1]
    block_rows = total_rows // blocks_dev
    grid_blocks = stacked.reshape(3 * blocks_dev, block_rows, -1)
    grad_rows = jnp.take(grid_blocks, codes.reshape(-1), axis=0).reshape(offsets, total_rows, -1)
    wgrad = jnp.einsum("kmc,kmd->kcd", picked, grad_rows, preferred_element_type=jnp.float32)
    grad_pick = jnp.einsum("kmd,kcd->kmc", grad_rows, weights, preferred_element_type=jnp.float32)
    grad_pick = grad_pick.reshape(offsets, blocks_dev, block_rows, channels)
    grad_in = jnp.einsum(
        "kbrs,kbrc->bsc", selector_wide, grad_pick, precision=lax.Precision.HIGHEST
    )
    return (wgrad, grad_in.reshape(total_rows, channels))


def on_device(
    features, source_rows, target_codes, block_count, weight_one, weight_two, out_cotangent
):
    offsets, blocks_dev, block_rows = source_rows.shape
    channels = features.shape[1]
    active = jnp.arange(blocks_dev, dtype=jnp.int32) < block_count[0]
    row_mask = jnp.repeat(active, block_rows).astype(jnp.float32)[:, None]
    valid_rows = (source_rows >= 0) & active[None, :, None]
    matches = (
        source_rows[:, :, :, None] == jnp.arange(block_rows, dtype=jnp.int32)[None, None, None, :]
    ) & valid_rows[:, :, :, None]
    selector = matches.astype(jnp.bfloat16)
    selector_wide = matches.astype(jnp.float32)
    pick_in = gather_rows(features, selector)
    pre_one = join_partials(spread_terms(pick_in, weight_one, target_codes))
    hidden = (jax.nn.silu(pre_one) * row_mask).astype(jnp.bfloat16)
    pick_mid = gather_rows(hidden, selector)
    total = join_partials(spread_terms(pick_mid, weight_two, target_codes)) + features.astype(
        jnp.float32
    )
    result = (jax.nn.silu(total) * row_mask).astype(jnp.bfloat16)
    grad_sum = (out_cotangent.astype(jnp.float32) * silu_grad(total) * row_mask).astype(
        jnp.bfloat16
    )
    wgrad_two, grad_mid = pull_back(
        neighbor_rows(grad_sum), target_codes, pick_mid, selector_wide, weight_two
    )
    grad_pre = (grad_mid * silu_grad(pre_one) * row_mask).astype(jnp.bfloat16)
    wgrad_one, grad_conv = pull_back(
        neighbor_rows(grad_pre), target_codes, pick_in, selector_wide, weight_one
    )
    input_grad = (grad_conv + grad_sum.astype(jnp.float32)).astype(jnp.bfloat16)
    stacked = jnp.stack([wgrad_one, wgrad_two]).reshape(2, offsets * channels, channels)
    whole_sum = lax.psum(stacked.astype(jnp.bfloat16), "tile")
    owned = lax.psum_scatter(whole_sum, "grp", scatter_dimension=1, tiled=True).astype(jnp.float32)
    voxel_total = lax.axis_size("grp") * lax.axis_size("tile") * blocks_dev * block_rows
    scale = float(voxel_total) ** (-0.5)
    owned = owned * scale
    return (result, input_grad, owned[0], owned[1])


def solution(mesh):
    in_specs = (
        P(("grp", "tile"), None),
        P(None, ("grp", "tile"), None),
        P(None, ("grp", "tile")),
        P(("grp", "tile")),
        P(),
        P(),
        P(("grp", "tile"), None),
    )
    out_specs = (P(("grp", "tile"), None), P(("grp", "tile"), None), P("grp", None), P("grp", None))
    return jax.shard_map(
        on_device, mesh=mesh, in_specs=in_specs, out_specs=out_specs, check_vma=False
    )
```

profile of v0, /device:TPU:1, one launch (start us, length us, event | category | flops | bytes accessed | tf_op | source)
XLA Modules:
  0.0 169.4 jit_solution(8273669962971659891)
XLA Ops:
  8.0 0.8 copy.22
  8.7 0.8 compare_and_fusion
  9.6 1.9 %convert_bitcast_fusion.1 = bf16[27,2,128,128]{3,2,0,1:T(8,128)(2,1)S(1)} fusion(bf16[2,128,128,1]{2,1,3,0:T(8,128)(2,1)} %bitcast.115, s32[27,2,128]{2,0,1:T(8,128)S(1)} %copy.22, pred[27,2,128]{2,0,1:T(8,128)(4,1)S(1)} %copy.23), kind=kOutput, calls=%fused_computation.16 | convolution fusion | flops 229146624 | bytes 1869568 | tf_op jit(solution)/shard_map/kbrs,bsc->kbrc/dot_general | solution.py:21
  11.5 0.1 copy.25
  11.6 1.0 copy-done.5
  12.7 0.6 fusion.48
  13.4 3.4 %fusion.27 = f32[6,128,128]{2,0,1:T(8,128)S(1)} fusion(f32[27,2,128,128]{3,2,1,0:T(8,128)S(1)} %bitcast.96, s32[27,2]{0,1:T(2,128)S(1)} %copy-done.14), kind=kOutput, calls=%fused_computation.29 | convolution fusion | flops 63701316 | bytes 3932376 | tf_op jit(solution)/shard_map/kis,kirc->src/dot_general | solution.py:33
  16.8 0.1 fusion.47
  16.9 2.0 %collective-permute-start = (f32[256,128]{1,0:T(8,128)S(1)}, f32[256,128]{1,0:T(8,128)S(1)}, u32[]{:S(2)}, u32[]{:S(2)}) collective-permute-start(f32[256,128]{1,0:T(8,128)S(1)} %bitcast.110), channel_id=1, source_target_pairs={{1,0},{2,1},{3,2},{4,3},{5,4},{6,5},{7,6},{9,8},{10,9},{11,10},{12... | collective-permute-start | bytes 393224 | tf_op jit(solution)/shard_map/ppermute | solution.py:10
  18.9 4.5 %collective-permute-start.1 = (f32[256,128]{1,0:T(8,128)S(1)}, f32[256,128]{1,0:T(8,128)S(1)}, u32[]{:S(2)}, u32[]{:S(2)}) collective-permute-start(f32[256,128]{1,0:T(8,128)S(1)} %bitcast.111), channel_id=1, source_target_pairs={{0,1},{1,2},{2,3},{3,4},{4,5},{5,6},{6,7},{8,9},{9,10},{10,11},{11... | collective-permute-start | bytes 393224 | tf_op jit(solution)/shard_map/ppermute | solution.py:10
  23.8 0.5 compare_and_fusion.1
  24.3 1.1 collective-permute-done.1
  25.5 1.1 convert_bitcast_fusion
  26.6 0.2 copy.31
  26.8 0.6 fusion.49
  27.4 0.6 copy-done.1
  28.0 3.4 %fusion.30 = f32[6,128,128]{2,0,1:T(8,128)S(1)} fusion(f32[27,2,128,128]{3,2,1,0:T(8,128)S(1)} %bitcast.97, s32[27,2]{0,1:T(2,128)S(1)} %copy-done.14), kind=kOutput, calls=%fused_computation.30 | convolution fusion | flops 63701316 | bytes 3932376 | tf_op jit(solution)/shard_map/kis,kirc->src/dot_general | solution.py:33
  31.4 0.1 fusion.46
  31.6 1.9 %collective-permute-start.2 = (f32[256,128]{1,0:T(8,128)S(1)}, f32[256,128]{1,0:T(8,128)S(1)}, u32[]{:S(2)}, u32[]{:S(2)}) collective-permute-start(f32[256,128]{1,0:T(8,128)S(1)} %bitcast.113), channel_id=1, source_target_pairs={{1,0},{2,1},{3,2},{4,3},{5,4},{6,5},{7,6},{9,8},{10,9},{11,10},{12... | collective-permute-start | bytes 393224 | tf_op jit(solution)/shard_map/ppermute | solution.py:10
  33.5 4.4 %collective-permute-start.3 = (f32[256,128]{1,0:T(8,128)S(1)}, f32[256,128]{1,0:T(8,128)S(1)}, u32[]{:S(2)}, u32[]{:S(2)}) collective-permute-start(f32[256,128]{1,0:T(8,128)S(1)} %bitcast.112), channel_id=1, source_target_pairs={{0,1},{1,2},{2,3},{3,4},{4,5},{5,6},{6,7},{8,9},{9,10},{10,11},{11... | collective-permute-start | bytes 393224 | tf_op jit(solution)/shard_map/ppermute | solution.py:10
  37.9 0.7 collective-permute-done.2
  38.6 1.2 collective-permute-done.3
  40.0 1.9 %collective-permute-start.5 = (bf16[256,128]{1,0:T(8,128)(2,1)S(1)}, bf16[256,128]{1,0:T(8,128)(2,1)S(1)}, u32[]{:S(2)}, u32[]{:S(2)}) collective-permute-start(bf16[256,128]{1,0:T(8,128)(2,1)S(1)} %get-tuple-element.5), channel_id=1, source_target_pairs={{1,0},{2,1},{3,2},{4,3},{5,4},{6,5},{7,6},{9,8},{10,9},{11,10},{12... | collective-permute-start | bytes 196616 | tf_op jit(solution)/shard_map/ppermute | solution.py:10
  41.9 4.5 %collective-permute-start.4 = (bf16[256,128]{1,0:T(8,128)(2,1)S(1)}, bf16[256,128]{1,0:T(8,128)(2,1)S(1)}, u32[]{:S(2)}, u32[]{:S(2)}) collective-permute-start(bf16[256,128]{1,0:T(8,128)(2,1)S(1)} %get-tuple-element.5), channel_id=1, source_target_pairs={{0,1},{1,2},{2,3},{3,4},{4,5},{5,6},{6,7},{8,9},{9,10},{10,11},{11... | collective-permute-start | bytes 196616 | tf_op jit(solution)/shard_map/ppermute | solution.py:10
  46.5 1.1 collective-permute-done.4
  47.6 2.0 %gather_fusion = bf16[54,128,128]{2,1,0:T(8,128)(2,1)} fusion(bf16[6,128,128]{2,1,0:T(8,128)(2,1)S(1)} %bitcast.95, s32[1024]{0:T(1024)S(1)} %pad_clamp_fusion), kind=kCustom, calls=%fused_computation.clone | custom fusion | bytes 3539160 | tf_op jit(solution)/shard_map/jit(_take)/gather | solution.py:59
  49.6 1.7 %broadcast_select_fusion = bf16[54,128,128]{2,1,0:T(8,128)(2,1)S(1)} fusion(bf16[54,128,128]{2,1,0:T(8,128)(2,1)} %gather_fusion, pred[54]{0:T(512)(128)(4,1)S(1)} %copy-done.15), kind=kLoop, calls=%fused_computation.21 | loop fusion | flops 884736 | bytes 3538998 | tf_op jit(solution)/shard_map/jit(_take)/select_n | solution.py:59
  51.3 0.6 fusion.50
  51.9 2.5 %fusion.6 = f32[2,128,128,1]{2,1,3,0:T(8,128)S(1)} fusion(f32[27,2,128,128]{3,2,1,0:T(8,128)S(1)} %bitcast.107, s32[27,2,128]{2,0,1:T(8,128)S(1)} %copy.22, pred[27,2,128]{2,0,1:T(8,128)(4,1)S(1)} %copy.23), kind=kOutput, calls=%fused_computation.8 | convolution fusion | flops 1360723968 | bytes 3704576 | tf_op jit(solution)/shard_map/kbrs,kbrc->bsc/dot_general | solution.py:63
  54.5 0.7 fusion.35
  55.2 1.9 %collective-permute-start.7 = (bf16[256,128]{1,0:T(8,128)(2,1)S(1)}, bf16[256,128]{1,0:T(8,128)(2,1)S(1)}, u32[]{:S(2)}, u32[]{:S(2)}) collective-permute-start(bf16[256,128]{1,0:T(8,128)(2,1)S(1)} %get-tuple-element.15), channel_id=1, source_target_pairs={{1,0},{2,1},{3,2},{4,3},{5,4},{6,5},{7,6},{9,8},{10,9},{11,10},{12... | collective-permute-start | bytes 196616 | tf_op jit(solution)/shard_map/ppermute | solution.py:10
  57.1 4.3 %collective-permute-start.6 = (bf16[256,128]{1,0:T(8,128)(2,1)S(1)}, bf16[256,128]{1,0:T(8,128)(2,1)S(1)}, u32[]{:S(2)}, u32[]{:S(2)}) collective-permute-start(bf16[256,128]{1,0:T(8,128)(2,1)S(1)} %get-tuple-element.15), channel_id=1, source_target_pairs={{0,1},{1,2},{2,3},{3,4},{4,5},{5,6},{6,7},{8,9},{9,10},{10,11},{11... | collective-permute-start | bytes 196616 | tf_op jit(solution)/shard_map/ppermute | solution.py:10
  61.4 1.6 convolution_convert_fusion
  63.1 2.0 %gather_fusion.1 = bf16[54,128,128]{2,1,0:T(8,128)(2,1)} fusion(bf16[6,128,128]{2,1,0:T(8,128)(2,1)S(1)} %bitcast.94, s32[1024]{0:T(1024)S(1)} %pad_clamp_fusion), kind=kCustom, calls=%fused_computation.1.clone | custom fusion | bytes 3539160 | tf_op jit(solution)/shard_map/jit(_take)/gather | solution.py:59
  65.1 1.7 %broadcast_select_fusion.1 = bf16[54,128,128]{2,1,0:T(8,128)(2,1)S(1)} fusion(bf16[54,128,128]{2,1,0:T(8,128)(2,1)} %gather_fusion.1, pred[54]{0:T(512)(128)(4,1)S(1)} %copy-done.15), kind=kLoop, calls=%fused_computation.22 | loop fusion | flops 884736 | bytes 3538998 | tf_op jit(solution)/shard_map/jit(_take)/select_n | solution.py:59
  66.8 0.7 convolution_convert_fusion.1
  67.5 0.5 copy-done.3
  68.0 0.6 copy-done.7
  68.6 1.3 pad_maximum_fusion
  70.1 1.4 copy-done.4
  71.5 0.6 fusion.51
  72.1 0.1 copy-done.11
  72.2 2.5 %fusion.4 = f32[2,128,128,1]{2,1,3,0:T(8,128)S(1)} fusion(f32[27,2,128,128]{3,2,1,0:T(8,128)S(1)} %bitcast.106, s32[27,2,128]{2,0,1:T(8,128)S(1)} %copy-done.11, pred[27,2,128]{2,0,1:T(8,128)(4,1)S(1)} %copy.23), kind=kOutput, calls=%fused_computation.6 | convolution fusion | flops 1360723968 | bytes 3704576 | tf_op jit(solution)/shard_map/kbrs,kbrc->bsc/dot_general | solution.py:63
  74.7 29.3 %reduce-scatter.2.cloned.1.call-done = bf16[2,864,128]{2,1,0:T(8,128)(2,1)} async-done(((bf16[2,3456,128]{2,1,0:T(8,128)(2,1)}), bf16[2,864,128]{2,1,0:T(8,128)(2,1)}) %reduce-scatter.2.cloned.1.call-update) | async-done | bytes 442384 | tf_op jit(solution)/shard_map/reduce_scatter | solution.py:103
  104.1 0.6 fusion.33
  104.8 55.8 %all-reduce.2.cloned.1.call-done = bf16[2,864,128]{2,1,0:T(8,128)(2,1)} async-done(((bf16[2,864,128]{2,1,0:T(8,128)(2,1)}), bf16[2,864,128]{2,1,0:T(8,128)(2,1)}) %all-reduce.2.cloned.1.call-update) | async-done | bytes 442384 | tf_op jit(solution)/shard_map/psum | solution.py:102
  160.5 1.1 convert_multiply_fusion
  161.6 1.0 slice_bitcast_fusion
  (52 shorter events, 0.8 us)
Async XLA Ops:
  7.2 19.6 %copy-start = (bf16[27,128,128]{2,1,0:T(8,128)(2,1)S(1)}, bf16[27,128,128]{2,1,0:T(8,128)(2,1)}, u32[]{:S(2)}) copy-start(bf16[27,128,128]{2,1,0:T(8,128)(2,1)} %param.14) | copy-start | bytes 2654212
  7.2 96.9 %reduce-scatter.2.cloned.1.call-start = ((), (), s32[]{:S(2)}) async-start(), calls=%async_computation.1 | async-start | bytes 2211840 | tf_op jit(solution)/shard_map/reduce_scatter | solution.py:103
  8.7 43.2 %copy-start.10 = (s32[27,2,128]{2,0,1:T(8,128)}, s32[27,2,128]{2,0,1:T(8,128)S(1)}, u32[]{:S(2)}) copy-start(s32[27,2,128]{2,0,1:T(8,128)S(1)} %copy.22) | copy-start | bytes 82948
  11.5 1.2 copy-start.5
  12.7 0.7 copy-start.14
  16.9 7.4 %collective-permute-start = (f32[256,128]{1,0:T(8,128)S(1)}, f32[256,128]{1,0:T(8,128)S(1)}, u32[]{:S(2)}, u32[]{:S(2)}) collective-permute-start(f32[256,128]{1,0:T(8,128)S(1)} %bitcast.110), channel_id=1, source_target_pairs={{1,0},{2,1},{3,2},{4,3},{5,4},{6,5},{7,6},{9,8},{10,9},{11,10},{12... | collective-permute-start | bytes 393224 | tf_op jit(solution)/shard_map/ppermute | solution.py:10
  18.9 6.5 %collective-permute-start.1 = (f32[256,128]{1,0:T(8,128)S(1)}, f32[256,128]{1,0:T(8,128)S(1)}, u32[]{:S(2)}, u32[]{:S(2)}) collective-permute-start(f32[256,128]{1,0:T(8,128)S(1)} %bitcast.111), channel_id=1, source_target_pairs={{0,1},{1,2},{2,3},{3,4},{4,5},{5,6},{6,7},{8,9},{9,10},{10,11},{11... | collective-permute-start | bytes 393224 | tf_op jit(solution)/shard_map/ppermute | solution.py:10
  26.8 1.2 copy-start.1
  28.0 11.8 %copy-start.12 = (bf16[256,128]{1,0:T(8,128)(2,1)S(1)}, bf16[256,128]{1,0:T(8,128)(2,1)}, u32[]{:S(2)}) copy-start(bf16[256,128]{1,0:T(8,128)(2,1)} %param.15) | copy-start | bytes 196612
  28.0 11.8 %copy-start.13 = (bf16[256,128]{1,0:T(8,128)(2,1)S(1)}, bf16[256,128]{1,0:T(8,128)(2,1)}, u32[]{:S(2)}) copy-start(bf16[256,128]{1,0:T(8,128)(2,1)} %param.9) | copy-start | bytes 196612
  31.6 7.0 %collective-permute-start.2 = (f32[256,128]{1,0:T(8,128)S(1)}, f32[256,128]{1,0:T(8,128)S(1)}, u32[]{:S(2)}, u32[]{:S(2)}) collective-permute-start(f32[256,128]{1,0:T(8,128)S(1)} %bitcast.113), channel_id=1, source_target_pairs={{1,0},{2,1},{3,2},{4,3},{5,4},{6,5},{7,6},{9,8},{10,9},{11,10},{12... | collective-permute-start | bytes 393224 | tf_op jit(solution)/shard_map/ppermute | solution.py:10
  33.5 6.3 %collective-permute-start.3 = (f32[256,128]{1,0:T(8,128)S(1)}, f32[256,128]{1,0:T(8,128)S(1)}, u32[]{:S(2)}, u32[]{:S(2)}) collective-permute-start(f32[256,128]{1,0:T(8,128)S(1)} %bitcast.112), channel_id=1, source_target_pairs={{0,1},{1,2},{2,3},{3,4},{4,5},{5,6},{6,7},{8,9},{9,10},{10,11},{11... | collective-permute-start | bytes 393224 | tf_op jit(solution)/shard_map/ppermute | solution.py:10
  39.9 7.6 %copy-start.8 = (bf16[256,128]{1,0:T(8,128)(2,1)}, bf16[256,128]{1,0:T(8,128)(2,1)S(1)}, u32[]{:S(2)}) copy-start(bf16[256,128]{1,0:T(8,128)(2,1)S(1)} %get-tuple-element.5) | copy-start | bytes 196612
  40.0 6.5 %collective-permute-start.5 = (bf16[256,128]{1,0:T(8,128)(2,1)S(1)}, bf16[256,128]{1,0:T(8,128)(2,1)S(1)}, u32[]{:S(2)}, u32[]{:S(2)}) collective-permute-start(bf16[256,128]{1,0:T(8,128)(2,1)S(1)} %get-tuple-element.5), channel_id=1, source_target_pairs={{1,0},{2,1},{3,2},{4,3},{5,4},{6,5},{7,6},{9,8},{10,9},{11,10},{12... | collective-permute-start | bytes 196616 | tf_op jit(solution)/shard_map/ppermute | solution.py:10
  41.9 5.7 %collective-permute-start.4 = (bf16[256,128]{1,0:T(8,128)(2,1)S(1)}, bf16[256,128]{1,0:T(8,128)(2,1)S(1)}, u32[]{:S(2)}, u32[]{:S(2)}) collective-permute-start(bf16[256,128]{1,0:T(8,128)(2,1)S(1)} %get-tuple-element.5), channel_id=1, source_target_pairs={{0,1},{1,2},{2,3},{3,4},{4,5},{5,6},{6,7},{8,9},{9,10},{10,11},{11... | collective-permute-start | bytes 196616 | tf_op jit(solution)/shard_map/ppermute | solution.py:10
  47.6 2.0 %copy-start.15 = (pred[54]{0:T(512)(128)(4,1)S(1)}, pred[54]{0:T(512)(128)(4,1)}, u32[]{:S(2)}) copy-start(pred[54]{0:T(512)(128)(4,1)} %compare_and_fusion.1) | copy-start | bytes 166
  51.9 9.5 %copy-start.2 = (bf16[27,2,128,128]{3,2,1,0:T(8,128)(2,1)S(1)}, bf16[27,2,128,128]{3,2,1,0:T(8,128)(2,1)}, u32[]{:S(2)}) copy-start(bf16[27,2,128,128]{3,2,1,0:T(8,128)(2,1)} %copy-done.1) | copy-start | bytes 5308420
  55.2 7.8 %collective-permute-start.7 = (bf16[256,128]{1,0:T(8,128)(2,1)S(1)}, bf16[256,128]{1,0:T(8,128)(2,1)S(1)}, u32[]{:S(2)}, u32[]{:S(2)}) collective-permute-start(bf16[256,128]{1,0:T(8,128)(2,1)S(1)} %get-tuple-element.15), channel_id=1, source_target_pairs={{1,0},{2,1},{3,2},{4,3},{5,4},{6,5},{7,6},{9,8},{10,9},{11,10},{12... | collective-permute-start | bytes 196616 | tf_op jit(solution)/shard_map/ppermute | solution.py:10
  57.1 5.9 %collective-permute-start.6 = (bf16[256,128]{1,0:T(8,128)(2,1)S(1)}, bf16[256,128]{1,0:T(8,128)(2,1)S(1)}, u32[]{:S(2)}, u32[]{:S(2)}) collective-permute-start(bf16[256,128]{1,0:T(8,128)(2,1)S(1)} %get-tuple-element.15), channel_id=1, source_target_pairs={{0,1},{1,2},{2,3},{3,4},{4,5},{5,6},{6,7},{8,9},{9,10},{10,11},{11... | collective-permute-start | bytes 196616 | tf_op jit(solution)/shard_map/ppermute | solution.py:10
  66.8 1.2 copy-start.3
  66.8 1.8 %copy-start.7 = (bf16[27,128,128]{2,1,0:T(8,128)(2,1)S(1)}, bf16[27,128,128]{2,1,0:T(8,128)(2,1)}, u32[]{:S(2)}) copy-start(bf16[27,128,128]{2,1,0:T(8,128)(2,1)} %convolution_convert_fusion) | copy-start | bytes 2654212
  68.6 1.4 copy-start.6
  70.0 1.5 copy-start.4
  70.0 90.5 %all-reduce.2.cloned.1.call-start = ((), (), s32[]{:S(2)}) async-start(), calls=%async_computation.2 | async-start | bytes 884736 | tf_op jit(solution)/shard_map/psum | solution.py:102
  71.5 0.8 copy-start.11
  72.2 31.9 %copy-start.9 = (bf16[256,128]{1,0:T(8,128)(2,1)S(1)}, bf16[256,128]{1,0:T(8,128)(2,1)}, u32[]{:S(2)}) copy-start(bf16[256,128]{1,0:T(8,128)(2,1)} %copy-done.8) | copy-start | bytes 196612
Sparse Core Ops, SparseCore 0:
  70.1 33.9 reduce-scatter.1
  106.4 54.0 all-reduce.1
where the time goes:
time: 172 us; the launch traced here: 169 us
  waiting for transfers between devices  89.3 us (52%)
  starting transfers between devices  25.5 us (15%)
  matrix products  19.6 us (11%)
  between operations  15.1 us (9%)
  local copies, waits for them, and re-layouts  11.1 us (6%)
  other arithmetic  8.81 us (5%)
    psum x1, waiting for transfers between devices, on_device(): whole_sum = lax.psum(stacked.astype(jnp.bfloat16), 'tile')  55.8 us
    reduce_scatter x1, waiting for transfers between devices, on_device(): lax.psum_scatter(whole_sum, 'grp', scatter_dimension=1, tiled=True)  29.3 us
    ppermute x8, starting transfers between devices, passed_along(): return lax.ppermute(value, axis, pairs)  25.4 us
    dot_general x2, matrix products, spread_terms(): jnp.einsum('kis,kirc->src', one_hot, partial_value.reshape(offsets, block...  6.78 us
    unnamed x34, local copies, waits for them, and re-layouts  5.25 us
    dot_general x2, matrix products, pull_back(): jnp.einsum('kbrs,kbrc->bsc', selector_wide, grad_pick, precision=lax.Prec...  5.06 us
    ppermute x8, waiting for transfers between devices, passed_along(): return lax.ppermute(value, axis, pairs)  4.12 us
    gather x2, local copies, waits for them, and re-layouts, pull_back(): jnp.take(grid_blocks, codes.reshape(-1), axis=0)  4.05 us
  transfers between devices with their start and end apart: 10, of which 6 were waited for; matrix products, arithmetic and copies ran while one was open for 4% of the time, Pallas kernels for 0%

commit v1 on v0

v1 whole, which is shorter than its diff:
```python
import jax
import jax.numpy as jnp
from jax import lax
from jax.experimental import pallas as pl
from jax.experimental.pallas import tpu as pltpu
from jax.sharding import PartitionSpec as P

F32 = jnp.float32
BF16 = jnp.bfloat16
KINDS = 3
LIMIT = 28 * 1024 * 1024
NT = (((1,), (1,)), ((), ()))


def swapped(value, axis, bits):
    count = lax.axis_size(axis)
    return lax.ppermute(value, axis, [(i, i ^ bits) for i in range(count) if i ^ bits < count])


def crossed(value):
    count = lax.axis_size("tile")
    pairs = [(i, ((i + 1) ^ 1) - 1) for i in range(count)]
    return lax.ppermute(value, "tile", [(i, j) for i, j in pairs if 0 <= j < count])


def sigmoid_terms(values):
    sigma = jax.nn.sigmoid(values)
    return values * sigma, sigma * (1.0 + values * (1.0 - sigma))


def halo_sides(odd, core, cross):
    return jnp.where(odd, cross, core), jnp.where(odd, core, cross)


def row_mask(rows, blk, count):
    block = lax.broadcasted_iota(jnp.int32, (rows, 1), 0) // blk
    return (block < count).astype(F32)


def pack_kernel(info, features, source_rows, codes, entries, core_out, cross_out):
    offsets, _, blk = source_rows.shape
    per = offsets // KINDS
    odd, count = info[0] == 1, info[1]
    coded = []
    for j in range(2):
        rows = source_rows[:, j, :]
        block = lax.rem(codes[:, j : j + 1], 2)
        live = (rows >= 0) & (count > j)
        coded.append(jnp.where(live, rows + blk * block, -1).astype(F32))
    first, second = coded
    both = count == 2
    entries[0] = first
    entries[1] = second
    to_prev = jnp.concatenate([first[i * KINDS : i * KINDS + 1] for i in range(per)], axis=0)
    last = jnp.where(both, second, first)
    to_next = jnp.concatenate([last[i * KINDS + 2 : i * KINDS + 3] for i in range(per)], axis=0)
    front, back = features[:blk, :], features[blk:, :]
    tail = jnp.where(both, back, front)
    pad = core_out.shape[0] - blk - per
    fill = jnp.full((pad, blk), -1.0, F32)
    to_prev = jnp.concatenate([to_prev, fill], axis=0).astype(BF16)
    to_next = jnp.concatenate([to_next, fill], axis=0).astype(BF16)
    core_out[:blk, :] = jnp.where(odd, front, tail)
    cross_out[:blk, :] = jnp.where(odd, tail, front)
    core_out[blk:, :] = jnp.where(odd, to_prev, to_next)
    cross_out[blk:, :] = jnp.where(odd, to_next, to_prev)


def targets_by_sources(columns, kind, per, index, blk):
    lane = lax.broadcasted_iota(jnp.int32, (blk, blk), 1).astype(F32)
    halves = []
    for side in range(2):
        at = (kind * 2 + side) * per + index
        entry = jnp.broadcast_to(columns[:, at : at + 1], (blk, blk))
        halves.append(jnp.concatenate([entry, entry - blk], axis=0))
    wide = jnp.concatenate([lane, lane], axis=0)
    parts = [jnp.where(half == wide, 1.0, 0.0).astype(BF16) for half in halves]
    return jnp.concatenate(parts, axis=1)


def sources_by_targets(entries, kind, per, index, blk):
    sub = lax.broadcasted_iota(jnp.int32, (blk, 2 * blk), 0).astype(F32)
    parts = []
    for side in range(2):
        at = (kind * 2 + side) * per + index
        row = entries[at : at + 1, :]
        wide = jnp.concatenate([row, row - blk], axis=1)
        parts.append(jnp.where(wide == sub, 1.0, 0.0).astype(BF16))
    return jnp.concatenate(parts, axis=0)


def convolve(columns, sources, weights, picked):
    blk, channels = columns.shape[0], weights.shape[1]
    per = picked.shape[1] // channels // KINDS
    for kind in range(KINDS):
        for i in range(per):
            select = targets_by_sources(columns, kind, per, i, blk)
            got = jnp.dot(select, sources[kind], preferred_element_type=F32)
            at = (i * KINDS + kind) * channels
            picked[:, at : at + channels] = got.astype(BF16)
    return jnp.dot(picked[...], weights[...], preferred_element_type=F32)


def pull_back(entries, grads, weights, sources, pulled, wgrad):
    blk, channels = entries.shape[1], grads.shape[1]
    per = pulled.shape[1] // channels // KINDS
    sums = []
    for kind in range(KINDS):
        base = kind * per * channels
        for i in range(per):
            select = sources_by_targets(entries, kind, per, i, blk)
            got = jnp.dot(select, grads, preferred_element_type=F32)
            at = base + i * channels
            pulled[:, at : at + channels] = got.astype(BF16)
        held = pulled[:, base : base + per * channels]
        wide = jnp.concatenate(
            [
                weights[(i * KINDS + kind) * channels : (i * KINDS + kind + 1) * channels, :]
                for i in range(per)
            ],
            axis=1,
        )
        sums.append(lax.dot_general(held, wide, NT, preferred_element_type=F32))
        turned = sources[kind].T
        terms = jnp.dot(turned, held, preferred_element_type=F32)
        for i in range(per):
            at = (i * KINDS + kind) * channels
            wgrad[at : at + channels, :] = terms[:, i * channels : (i + 1) * channels]
    return sums


def split_sums(sums, both, blk):
    low, mid, high = sums
    first = mid[:blk] + jnp.where(both, high[blk:], 0.0)
    second = mid[blk:] + low[blk:]
    return jnp.concatenate([first, second], axis=0), low[:blk], high[:blk]


def halves_out(odd_bit, wgrad, keep, send, at):
    shards, slot, _ = keep.shape
    rows = wgrad.shape[0] // shards // 2
    for s in range(shards):
        mine = pl.ds(s * 2 * rows + odd_bit * rows, rows)
        other = pl.ds(s * 2 * rows + (1 - odd_bit) * rows, rows)
        keep[s, :rows, :] = wgrad[mine, :]
        start = at + s * slot
        send[start : start + rows, :] = wgrad[other, :].astype(BF16)


def first_kernel(
    info, local, features, core_in, cross_in, weights,
    entries, halo, hidden, slope, core_out, cross_out, picked,
):
    blk = features.shape[0] // 2
    per = local.shape[1] // KINDS
    odd, count = info[0] == 1, info[1]
    both = count == 2
    from_next, from_prev = halo_sides(odd, core_in[...].astype(F32), cross_in[...].astype(F32))
    first, second = local[0], local[1]

    def of_kind(values, kind):
        return [values[i * KINDS + kind : i * KINDS + kind + 1] for i in range(per)]

    rows = [from_next[blk : blk + per]]
    rows += of_kind(second, 0) + of_kind(first, 1) + of_kind(second, 1)
    rows += [from_prev[blk : blk + per]]
    rows += of_kind(jnp.where(both, first, -1.0), 2)
    table = jnp.concatenate(rows, axis=0)
    entries[...] = table
    spare = -table.shape[0] % 8
    table = jnp.concatenate([table, jnp.zeros((spare, blk), F32)], axis=0)
    columns = table.T
    after, before = from_next[:blk].astype(BF16), from_prev[:blk].astype(BF16)
    halo[0] = after
    halo[1] = before
    front, back = features[:blk, :], features[blk:, :]
    sources = [
        jnp.concatenate([after, back], axis=0),
        features[...],
        jnp.concatenate([before, front], axis=0),
    ]
    pre = convolve(columns, sources, weights, picked)
    mask = row_mask(2 * blk, blk, count)
    value, grad = sigmoid_terms(pre)
    field = (value * mask).astype(BF16)
    hidden[...] = field
    slope[...] = grad * mask
    head = field[:blk]
    tail = jnp.where(both, field[blk:], head)
    core_out[...] = jnp.where(odd, head, tail)
    cross_out[...] = jnp.where(odd, tail, head)


def exchange_sides(odd, to_next, to_prev):
    return jnp.where(odd, to_prev, to_next), jnp.where(odd, to_next, to_prev)


def second_kernel(
    info, entries, features, hidden, core_in, cross_in, weights, cotangent,
    result, grads_out, own_out, keep, core_out, cross_out, picked, pulled, wgrad,
):
    blk = features.shape[0] // 2
    odd, count = info[0] == 1, info[1]
    both = count == 2
    after, before = halo_sides(odd, core_in[...], cross_in[...])
    front, back = hidden[:blk, :], hidden[blk:, :]
    sources = [
        jnp.concatenate([after, back], axis=0),
        hidden[...],
        jnp.concatenate([before, front], axis=0),
    ]
    table = entries[...]
    spare = -table.shape[0] % 8
    columns = jnp.concatenate([table, jnp.zeros((spare, blk), F32)], axis=0).T
    total = convolve(columns, sources, weights, picked) + features[...].astype(F32)
    mask = row_mask(2 * blk, blk, count)
    value, grad = sigmoid_terms(total)
    result[...] = (value * mask).astype(BF16)
    grads = (cotangent[...].astype(F32) * grad * mask).astype(BF16)
    grads_out[...] = grads
    sums = pull_back(entries, grads, weights, sources, pulled, wgrad)
    own, to_next, to_prev = split_sums(sums, both, blk)
    own_out[...] = own
    core, cross = exchange_sides(odd, to_next, to_prev)
    core_out[:blk, :] = core.astype(BF16)
    cross_out[...] = cross.astype(BF16)
    halves_out(info[0], wgrad, keep, core_out, blk)


def joined(own, odd, both, core_in, cross_in, blk):
    from_next, from_prev = halo_sides(odd, core_in, cross_in)
    first = own[:blk] + from_prev + jnp.where(both, 0.0, from_next)
    second = own[blk:] + jnp.where(both, from_next, 0.0)
    return jnp.concatenate([first, second], axis=0)


def third_kernel(
    info, entries, features, halo, own, core_in, cross_in, slope, grads_in, weights,
    own_out, keep, core_out, cross_out, pulled, wgrad,
):
    blk = features.shape[0] // 2
    odd, both = info[0] == 1, info[1] == 2
    core, cross = core_in[:blk, :].astype(F32), cross_in[...].astype(F32)
    summed = joined(own[...], odd, both, core, cross, blk)
    grads = (summed * slope[...]).astype(BF16)
    sources = [
        jnp.concatenate([halo[0], features[blk:, :]], axis=0),
        features[...],
        jnp.concatenate([halo[1], features[:blk, :]], axis=0),
    ]
    sums = pull_back(entries, grads, weights, sources, pulled, wgrad)
    own_sum, to_next, to_prev = split_sums(sums, both, blk)
    own_out[...] = own_sum + grads_in[...].astype(F32)
    core, cross = exchange_sides(odd, to_next, to_prev)
    core_out[:blk, :] = core.astype(BF16)
    cross_out[...] = cross.astype(BF16)
    halves_out(info[0], wgrad, keep, core_out, blk)


def last_kernel(info, own, core_in, cross_in, input_grad):
    blk = own.shape[0] // 2
    odd, both = info[0] == 1, info[1] == 2
    core, cross = core_in[:blk, :].astype(F32), cross_in[...].astype(F32)
    input_grad[...] = joined(own[...], odd, both, core, cross, blk).astype(BF16)


def shards_kernel(info, keep_one, keep_two, core_one, core_two, own, *sends):
    shards, slot, _ = keep_one.shape
    blk = core_one.shape[0] - shards * slot
    me = info[2]
    for d in range(shards):
        to = me ^ d
        at = pl.ds(pl.multiple_of(blk + to * slot, 16), slot)
        for half, keep, core in ((0, keep_one, core_one), (1, keep_two, core_two)):
            value = keep[to] + core[at, :].astype(F32)
            if d == 0:
                own[half] = value
            else:
                sends[d - 1][half] = value.astype(BF16)


def call(kernel, outs, *args, scratch=()):
    specs = [pl.BlockSpec(memory_space=pltpu.SMEM)]
    specs += [pl.BlockSpec(memory_space=pltpu.VMEM)] * (len(args) - 1)
    return pl.pallas_call(
        kernel,
        out_shape=[jax.ShapeDtypeStruct(shape, kind) for shape, kind in outs],
        in_specs=specs,
        out_specs=[pl.BlockSpec(memory_space=pltpu.VMEM)] * len(outs),
        scratch_shapes=[pltpu.VMEM(shape, kind) for shape, kind in scratch],
        compiler_params=pltpu.CompilerParams(vmem_limit_bytes=LIMIT),
    )(*args)


def on_device(
    features, source_rows, target_codes, block_count, weight_one, weight_two, out_cotangent
):
    offsets, blocks_dev, blk = source_rows.shape
    rows, channels = features.shape
    n_grp, n_tile = lax.axis_size("grp"), lax.axis_size("tile")
    per = offsets // KINDS
    info = jnp.stack(
        [lax.axis_index("tile") % 2, block_count[0], lax.axis_index("grp")]
    ).astype(jnp.int32)
    flat_one = weight_one.reshape(offsets * channels, channels)
    flat_two = weight_two.reshape(offsets * channels, channels)
    packed = blk + per + (-per % 16)
    half = offsets * channels // n_grp // 2
    wide = (rows, offsets * channels)
    field, block = ((rows, channels), BF16), ((blk, channels), BF16)
    summed = ((rows, channels), F32)
    slot = half + (-half % 16)
    keep_shape = ((n_grp, slot, channels), F32)
    core_shape = ((blk + n_grp * slot, channels), BF16)

    local, core, cross = call(
        pack_kernel,
        [((2, offsets, blk), F32), ((packed, channels), BF16), ((packed, channels), BF16)],
        info, features, source_rows, target_codes,
    )
    cross, core = crossed(cross), swapped(core, "tile", 1)
    entries, halo, hidden, slope, core, cross = call(
        first_kernel,
        [((2 * offsets, blk), F32), ((2, blk, channels), BF16), field, summed, block, block],
        info, local, features, core, cross, flat_one,
        scratch=[(wide, BF16)],
    )
    cross, core = crossed(cross), swapped(core, "tile", 1)
    result, grad_sum, own, keep_two, core_two, cross = call(
        second_kernel,
        [field, field, summed, keep_shape, core_shape, block],
        info, entries, features, hidden, core, cross, flat_two, out_cotangent,
        scratch=[(wide, BF16), (wide, BF16), ((offsets * channels, channels), F32)],
    )
    cross, core_two = crossed(cross), swapped(core_two, "tile", 1)
    own, keep_one, core_one, cross = call(
        third_kernel,
        [summed, keep_shape, core_shape, block],
        info, entries, features, halo, own, core_two, cross, slope, grad_sum, flat_one,
        scratch=[(wide, BF16), ((offsets * channels, channels), F32)],
    )
    core_one = swapped(core_one, "tile", 1)
    shard = (2, slot, channels)
    mine, *sends = call(
        shards_kernel,
        [(shard, F32)] + [(shard, BF16)] * (n_grp - 1),
        info, keep_one, keep_two, core_one, core_two,
    )
    for d, send in enumerate(sends):
        mine = mine + swapped(send, "grp", d + 1).astype(F32)
    cross = crossed(cross)
    (input_grad,) = call(last_kernel, [field], info, own, core_one, cross)
    bits = 2
    while bits < n_tile:
        mine = mine.astype(BF16)
        mine = mine.astype(F32) + swapped(mine, "tile", bits).astype(F32)
        bits *= 2
    voxel_total = n_grp * n_tile * rows
    mine = mine[:, :half] * float(voxel_total) ** (-0.5)
    other = swapped(mine, "tile", 1)
    odd = lax.axis_index("tile") % 2 == 1
    whole = jnp.concatenate(
        [jnp.where(odd, other, mine), jnp.where(odd, mine, other)], axis=1
    )
    return (result, input_grad, whole[0], whole[1])


def solution(mesh):
    in_specs = (
        P(("grp", "tile"), None),
        P(None, ("grp", "tile"), None),
        P(None, ("grp", "tile")),
        P(("grp", "tile")),
        P(),
        P(),
        P(("grp", "tile"), None),
    )
    out_specs = (P(("grp", "tile"), None), P(("grp", "tile"), None), P("grp", None), P("grp", None))
    return jax.shard_map(
        on_device, mesh=mesh, in_specs=in_specs, out_specs=out_specs, check_vma=False
    )
```

time: 172 us -> 78.3 us (0.46); the launches traced: 169 us -> 77.9 us
  waiting for transfers between devices: 89.3 us -> 35.4 us
  matrix products: 19.6 us -> 0 us
  between operations: 15.1 us -> 1.44 us
  Pallas kernels: 0 us -> 13.6 us
  local copies, waits for them, and re-layouts: 11.1 us -> 3.29 us
  other arithmetic: 8.81 us -> 1.37 us
  starting transfers between devices: 25.5 us -> 22.8 us
    psum x1 -> x0, waiting for transfers between devices: 55.8 us -> none  [on_device(): whole_sum = lax.psum(stacked.astype(jnp.bfloat16), 'tile')]
    ppermute x8 -> x14, waiting for transfers between devices: 4.12 us -> 35.4 us  [the longest x10 27.3 us: swapped(): lax.ppermute(value, axis, [(i, i ^ bits) for i in range(count) if i ^ bit...]
    reduce_scatter x1 -> x0, waiting for transfers between devices: 29.3 us -> none  [on_device(): lax.psum_scatter(whole_sum, 'grp', scatter_dimension=1, tiled=True)]
    dot_general x12 -> x0, matrix products: 19.6 us -> none  [the longest x2 6.78 us: spread_terms(): jnp.einsum('kis,kirc->src', one_hot, partial_value.reshape(offsets, block...]
    pallas_call x0 -> x6, Pallas kernels: none -> 13.6 us  [call(): pl.pallas_call(kernel, out_shape=[jax.ShapeDtypeStruct(shape, kind) for s...]
    gather x2 -> x0, local copies, waits for them, and re-layouts: 4.05 us -> none  [pull_back(): jnp.take(grid_blocks, codes.reshape(-1), axis=0)]
    select_n x3 -> x1, other arithmetic: 3.4 us -> 0.1 us  [on_device(): jnp.where(odd, mine, other)]
    ppermute x8 -> x14, starting transfers between devices: 25.4 us -> 22.8 us  [the longest x4 14.3 us: crossed(): lax.ppermute(value, 'tile', [(i, j) for i, j in pairs if 0 <= j < count])]
  transfers between devices with their start and end apart: 10 -> 14, of which waited for: 6 -> 9; matrix products, arithmetic and copies ran while one was open for 4% -> 0% of each run, Pallas kernels for 0% -> 2%
where the time goes in v1:
time: 78.3 us; the launch traced here: 77.9 us
  waiting for transfers between devices  35.4 us (45%)
  starting transfers between devices  22.8 us (29%)
  Pallas kernels  13.6 us (17%)
  local copies, waits for them, and re-layouts  3.29 us (4%)
  between operations  1.44 us (2%)
  other arithmetic  1.37 us (2%)
    ppermute x10, waiting for transfers between devices, swapped(): lax.ppermute(value, axis, [(i, i ^ bits) for i in range(count) if i ^ bit...  27.3 us
    ppermute x4, starting transfers between devices, crossed(): lax.ppermute(value, 'tile', [(i, j) for i, j in pairs if 0 <= j < count])  14.3 us
    pallas_call x6, Pallas kernels, call(): pl.pallas_call(kernel, out_shape=[jax.ShapeDtypeStruct(shape, kind) for s...  13.6 us
    ppermute x10, starting transfers between devices, swapped(): lax.ppermute(value, axis, [(i, i ^ bits) for i in range(count) if i ^ bit...  8.5 us
    ppermute x4, waiting for transfers between devices, crossed(): lax.ppermute(value, 'tile', [(i, j) for i, j in pairs if 0 <= j < count])  8.07 us
    unnamed x15, local copies, waits for them, and re-layouts  3.29 us
  transfers between devices with their start and end apart: 14, of which 9 were waited for; matrix products, arithmetic and copies ran while one was open for 0% of the time, Pallas kernels for 2%

profile of v1, /device:TPU:1, one launch (start us, length us, event | category | flops | bytes accessed | tf_op | source)
XLA Modules:
  0.0 77.9 jit_solution(15035148903548061389)
XLA Ops:
  0.6 0.0 copy-start.6
  0.6 0.0 copy-start.5
  1.3 0.0 copy-done.6
  1.3 0.1 copy.11.codes
  1.4 0.1 pad_add_fusion.info
  1.5 0.0 copy-done.5
  1.5 0.8 %copy-done.2 = bf16[256,128]{1,0:T(8,128)(2,1)S(1)} copy-done((bf16[256,128]{1,0:T(8,128)(2,1)S(1)}, bf16[256,128]{1,0:T(8,128)(2,1)}, u32[]{:S(2)}) %copy-start.2) | copy-done | bytes 65560
  2.3 0.6 shard_map.102
  3.0 0.1 collective-permute-start
  3.1 4.6 %collective-permute-start.1 = (bf16[144,128]{1,0:T(8,128)(2,1)S(1)}, bf16[144,128]{1,0:T(8,128)(2,1)S(1)}, u32[]{:S(2)}, u32[]{:S(2)}) collective-permute-start(bf16[144,128]{1,0:T(8,128)(2,1)S(1)} %get-tuple-element.29), channel_id=1, source_target_pairs={{1,2},{2,1},{3,4},{4,3},{5,6},{6,5},{9,10},{10,9},{11,12},{12,11},... | collective-permute-start | bytes 110600 | tf_op jit(solution)/shard_map/ppermute | solution.py:23
  7.7 0.0 collective-permute-done.core_in
  7.7 1.6 %collective-permute-done.1.cross_in = bf16[144,128]{1,0:T(8,128)(2,1)S(1)} collective-permute-done((bf16[144,128]{1,0:T(8,128)(2,1)S(1)}, bf16[144,128]{1,0:T(8,128)(2,1)S(1)}, u32[]{:S(2)}, u32[]{:S(2)}) %collective-permute-start.1) | collective-permute-done | bytes 36896 | tf_op jit(solution)/shard_map/ppermute | solution.py:23
  9.3 1.2 %copy-done = bf16[27,128,128]{2,1,0:T(8,128)(2,1)S(1)} copy-done((bf16[27,128,128]{2,1,0:T(8,128)(2,1)S(1)}, bf16[27,128,128]{2,1,0:T(8,128)(2,1)}, u32[]{:S(2)}) %copy-start) | copy-done | bytes 884760
  10.5 2.7 %shard_map.103 = (f32[54,128]{1,0:T(8,128)S(1)}, bf16[2,128,128]{2,1,0:T(8,128)(2,1)S(1)}, bf16[256,128]{1,0:T(8,128)(2,1)S(1)}, f32[256,128]{1,0:T(8,128)S(1)},...) custom-call(s32[3]{0:T(128)S(1)} %pad_add_fusion.info, f32[2,27,128]{2,1,0:T(8,128)S(1)} %get-tuple-element.27.local, ...), custom_call_target="tpu_custom_call" | custom-call | tf_op jit(solution)/shard_map/pallas_call | solution.py:285
  13.2 0.1 collective-permute-start.2
  13.3 4.1 %collective-permute-start.3 = (bf16[128,128]{1,0:T(8,128)(2,1)S(1)}, bf16[128,128]{1,0:T(8,128)(2,1)S(1)}, u32[]{:S(2)}, u32[]{:S(2)}) collective-permute-start(bf16[128,128]{1,0:T(8,128)(2,1)S(1)} %get-tuple-element.33), channel_id=1, source_target_pairs={{1,2},{2,1},{3,4},{4,3},{5,6},{6,5},{9,10},{10,9},{11,12},{12,11},... | collective-permute-start | bytes 98312 | tf_op jit(solution)/shard_map/ppermute | solution.py:23
  17.4 0.0 collective-permute-done.2.core_in
  17.4 1.6 %collective-permute-done.3.cross_in = bf16[128,128]{1,0:T(8,128)(2,1)S(1)} collective-permute-done((bf16[128,128]{1,0:T(8,128)(2,1)S(1)}, bf16[128,128]{1,0:T(8,128)(2,1)S(1)}, u32[]{:S(2)}, u32[]{:S(2)}) %collective-permute-start.3) | collective-permute-done | bytes 32800 | tf_op jit(solution)/shard_map/ppermute | solution.py:23
  19.0 1.2 %copy-done.3 = bf16[27,128,128]{2,1,0:T(8,128)(2,1)S(1)} copy-done((bf16[27,128,128]{2,1,0:T(8,128)(2,1)S(1)}, bf16[27,128,128]{2,1,0:T(8,128)(2,1)}, u32[]{:S(2)}) %copy-start.3) | copy-done | bytes 884760
  20.1 5.4 %shard_map.104 = (bf16[256,128]{1,0:T(8,128)(2,1)}, bf16[256,128]{1,0:T(8,128)(2,1)S(1)}, f32[256,128]{1,0:T(8,128)S(1)}, f32[4,432,128]{2,1,0:T(8,128)S(1)}, bf...) custom-call(s32[3]{0:T(128)S(1)} %pad_add_fusion.info, f32[54,128]{1,0:T(8,128)S(1)} %get-tuple-element.30.entries, ...), custom_call_target="tpu_custom_call" | custom-call | tf_op jit(solution)/shard_map/pallas_call | solution.py:285
  25.6 0.0 collective-permute-start.4
  25.6 3.7 %collective-permute-start.5 = (bf16[128,128]{1,0:T(8,128)(2,1)S(1)}, bf16[128,128]{1,0:T(8,128)(2,1)S(1)}, u32[]{:S(2)}, u32[]{:S(2)}) collective-permute-start(bf16[128,128]{1,0:T(8,128)(2,1)S(1)} %get-tuple-element.38), channel_id=1, source_target_pairs={{1,2},{2,1},{3,4},{4,3},{5,6},{6,5},{9,10},{10,9},{11,12},{12,11},... | collective-permute-start | bytes 98312 | tf_op jit(solution)/shard_map/ppermute | solution.py:23
  29.3 1.6 %collective-permute-done.5.cross_in = bf16[128,128]{1,0:T(8,128)(2,1)S(1)} collective-permute-done((bf16[128,128]{1,0:T(8,128)(2,1)S(1)}, bf16[128,128]{1,0:T(8,128)(2,1)S(1)}, u32[]{:S(2)}, u32[]{:S(2)}) %collective-permute-start.5) | collective-permute-done | bytes 32800 | tf_op jit(solution)/shard_map/ppermute | solution.py:23
  30.9 0.0 collective-permute-done.4.core_in.core_two
  30.9 2.9 %shard_map.105 = (f32[256,128]{1,0:T(8,128)S(1)}, f32[4,432,128]{2,1,0:T(8,128)S(1)}, bf16[1856,128]{1,0:T(8,128)(2,1)S(1)}, bf16[128,128]{1,0:T(8,128)(2,1)S(1)}) custom-call(s32[3]{0:T(128)S(1)} %pad_add_fusion.info, f32[54,128]{1,0:T(8,128)S(1)} %get-tuple-element.30.entries, bf16[256,128]{1,0:T(8,128)(2,1)S(1)} %copy-done.2, ...), custom_call_target="tpu_custom_call" | custom-call | tf_op jit(solution)/shard_map/pallas_call | solution.py:285
  33.8 0.1 collective-permute-start.6
  33.9 1.8 %collective-permute-done.6.core_in.core_one = bf16[1856,128]{1,0:T(8,128)(2,1)S(1)} collective-permute-done((bf16[1856,128]{1,0:T(8,128)(2,1)S(1)}, bf16[1856,128]{1,0:T(8,128)(2,1)S(1)}, u32[]{:S(2)}, u32[]{:S(2)}) %collective-permute-start.6) | collective-permute-done | bytes 475168 | tf_op jit(solution)/shard_map/ppermute | solution.py:17
  35.7 0.7 shard_map.107
  36.5 2.2 %collective-permute-start.10 = (bf16[2,432,128]{2,1,0:T(8,128)(2,1)S(1)}, bf16[2,432,128]{2,1,0:T(8,128)(2,1)S(1)}, u32[]{:S(2)}, u32[]{:S(2)}) collective-permute-start(bf16[2,432,128]{2,1,0:T(8,128)(2,1)S(1)} %get-tuple-element.49), channel_id=1, source_target_pairs={{0,24},{8,16},{16,8},{24,0},{1,25},{9,17},{17,9},{25,1},{2,26},{10... | collective-permute-start | bytes 663560 | tf_op jit(solution)/shard_map/ppermute | solution.py:17
  38.7 0.2 collective-permute-start.9
  38.9 0.3 collective-permute-start.8
  39.2 5.2 %collective-permute-done.10 = bf16[2,432,128]{2,1,0:T(8,128)(2,1)S(1)} collective-permute-done((bf16[2,432,128]{2,1,0:T(8,128)(2,1)S(1)}, bf16[2,432,128]{2,1,0:T(8,128)(2,1)S(1)}, u32[]{:S(2)}, u32[]{:S(2)}) %collective-permute-start.10) | collective-permute-done | bytes 221216 | tf_op jit(solution)/shard_map/ppermute | solution.py:17
  44.4 5.2 %collective-permute-done.9 = bf16[2,432,128]{2,1,0:T(8,128)(2,1)S(1)} collective-permute-done((bf16[2,432,128]{2,1,0:T(8,128)(2,1)S(1)}, bf16[2,432,128]{2,1,0:T(8,128)(2,1)S(1)}, u32[]{:S(2)}, u32[]{:S(2)}) %collective-permute-start.9) | collective-permute-done | bytes 221216 | tf_op jit(solution)/shard_map/ppermute | solution.py:17
  49.5 0.0 collective-permute-done.8
  49.5 0.1 add_convert_fusion.1
  49.6 1.8 %collective-permute-start.11 = (bf16[2,432,128]{2,1,0:T(8,128)(2,1)S(1)}, bf16[2,432,128]{2,1,0:T(8,128)(2,1)S(1)}, u32[]{:S(2)}, u32[]{:S(2)}) collective-permute-start(bf16[2,432,128]{2,1,0:T(8,128)(2,1)S(1)} %add_convert_fusion.1), channel_id=1, source_target_pairs={{0,2},{1,3},{2,0},{3,1},{4,6},{5,7},{6,4},{7,5},{8,10},{9,11},{10,... | collective-permute-start | bytes 663560 | tf_op jit(solution)/shard_map/ppermute | solution.py:17
  51.4 5.3 %collective-permute-done.11 = bf16[2,432,128]{2,1,0:T(8,128)(2,1)S(1)} collective-permute-done((bf16[2,432,128]{2,1,0:T(8,128)(2,1)S(1)}, bf16[2,432,128]{2,1,0:T(8,128)(2,1)S(1)}, u32[]{:S(2)}, u32[]{:S(2)}) %collective-permute-start.11) | collective-permute-done | bytes 221216 | tf_op jit(solution)/shard_map/ppermute | solution.py:17
  56.7 0.1 add_convert_fusion
  56.8 2.2 %collective-permute-start.12 = (bf16[2,432,128]{2,1,0:T(8,128)(2,1)S(1)}, bf16[2,432,128]{2,1,0:T(8,128)(2,1)S(1)}, u32[]{:S(2)}, u32[]{:S(2)}) collective-permute-start(bf16[2,432,128]{2,1,0:T(8,128)(2,1)S(1)} %add_convert_fusion), channel_id=1, source_target_pairs={{0,4},{1,5},{2,6},{3,7},{4,0},{5,1},{6,2},{7,3},{8,12},{9,13},{10,... | collective-permute-start | bytes 663560 | tf_op jit(solution)/shard_map/ppermute | solution.py:17
  59.0 9.9 %collective-permute-done.12 = bf16[2,432,128]{2,1,0:T(8,128)(2,1)S(1)} collective-permute-done((bf16[2,432,128]{2,1,0:T(8,128)(2,1)S(1)}, bf16[2,432,128]{2,1,0:T(8,128)(2,1)S(1)}, u32[]{:S(2)}, u32[]{:S(2)}) %collective-permute-start.12) | collective-permute-done | bytes 221216 | tf_op jit(solution)/shard_map/ppermute | solution.py:17
  68.9 0.1 add_multiply_fusion
  68.9 1.5 %collective-permute-start.13 = (f32[2,432,128]{2,1,0:T(8,128)S(1)}, f32[2,432,128]{2,1,0:T(8,128)S(1)}, u32[]{:S(2)}, u32[]{:S(2)}) collective-permute-start(f32[2,432,128]{2,1,0:T(8,128)S(1)} %add_multiply_fusion), channel_id=1, source_target_pairs={{0,1},{1,0},{2,3},{3,2},{4,5},{5,4},{6,7},{7,6},{8,9},{9,8},{10,11... | collective-permute-start | bytes 1327112 | tf_op jit(solution)/shard_map/ppermute | solution.py:17
  70.4 1.9 %collective-permute-start.7 = (bf16[128,128]{1,0:T(8,128)(2,1)S(1)}, bf16[128,128]{1,0:T(8,128)(2,1)S(1)}, u32[]{:S(2)}, u32[]{:S(2)}) collective-permute-start(bf16[128,128]{1,0:T(8,128)(2,1)S(1)} %get-tuple-element.43), channel_id=1, source_target_pairs={{1,2},{2,1},{3,4},{4,3},{5,6},{6,5},{9,10},{10,9},{11,12},{12,11},... | collective-permute-start | bytes 98312 | tf_op jit(solution)/shard_map/ppermute | solution.py:23
  72.4 3.3 %collective-permute-done.7.cross_in = bf16[128,128]{1,0:T(8,128)(2,1)S(1)} collective-permute-done((bf16[128,128]{1,0:T(8,128)(2,1)S(1)}, bf16[128,128]{1,0:T(8,128)(2,1)S(1)}, u32[]{:S(2)}, u32[]{:S(2)}) %collective-permute-start.7) | collective-permute-done | bytes 32800 | tf_op jit(solution)/shard_map/ppermute | solution.py:23
  75.7 1.2 %shard_map.106 = bf16[256,128]{1,0:T(8,128)(2,1)} custom-call(s32[3]{0:T(128)S(1)} %pad_add_fusion.info, f32[256,128]{1,0:T(8,128)S(1)} %get-tuple-element.41.own, bf16[1856,128]{1,0:T(8,128)(2,1)S(1)} %collective-permute-done.6.core_in.core_one, bf16[128,128]{1,0:T(8,128)(2,1)S(1)} %collective-permute-done.7.cross_in), custom_call_target="tpu_custom_call" | custom-call | tf_op jit(solution)/shard_map/pallas_call | solution.py:285
  76.9 0.0 collective-permute-done.13
  76.9 0.1 broadcast_select_fusion
  77.0 1.0 %fusion.2 = (f32[864,128]{1,0:T(8,128)}, f32[864,128]{1,0:T(8,128)}) fusion(f32[2,432,128]{2,1,0:T(8,128)S(1)} %get-tuple-element.52, f32[2,432,128]{2,1,0:T(8,128)S(1)} %get-tuple-element.53), kind=kLoop, calls=%fused_computation.5 | loop fusion | flops 221184 | bytes 1769472 | tf_op jit(solution)/shard_map/squeeze | solution.py:365
  (7 shorter events, 0.0 us)
Async XLA Ops:
  0.6 0.7 copy-start.6
  0.6 0.9 %copy-start.5 = (s32[27,2,128]{2,1,0:T(2,128)S(1)}, s32[27,2,128]{2,1,0:T(2,128)}, u32[]{:S(2)}) copy-start(s32[27,2,128]{2,1,0:T(2,128)} %source_rows.1) | copy-start | bytes 82948
  1.5 0.8 %copy-start.2 = (bf16[256,128]{1,0:T(8,128)(2,1)S(1)}, bf16[256,128]{1,0:T(8,128)(2,1)}, u32[]{:S(2)}) copy-start(bf16[256,128]{1,0:T(8,128)(2,1)} %features.7) | copy-start | bytes 196612
  3.0 4.7 %collective-permute-start = (bf16[144,128]{1,0:T(8,128)(2,1)S(1)}, bf16[144,128]{1,0:T(8,128)(2,1)S(1)}, u32[]{:S(2)}, u32[]{:S(2)}) collective-permute-start(bf16[144,128]{1,0:T(8,128)(2,1)S(1)} %get-tuple-element.28), channel_id=1, source_target_pairs={{0,1},{1,0},{2,3},{3,2},{4,5},{5,4},{6,7},{7,6},{8,9},{9,8},{10,11... | collective-permute-start | bytes 110600 | tf_op jit(solution)/shard_map/ppermute | solution.py:17
  3.1 6.2 %collective-permute-start.1 = (bf16[144,128]{1,0:T(8,128)(2,1)S(1)}, bf16[144,128]{1,0:T(8,128)(2,1)S(1)}, u32[]{:S(2)}, u32[]{:S(2)}) collective-permute-start(bf16[144,128]{1,0:T(8,128)(2,1)S(1)} %get-tuple-element.29), channel_id=1, source_target_pairs={{1,2},{2,1},{3,4},{4,3},{5,6},{6,5},{9,10},{10,9},{11,12},{12,11},... | collective-permute-start | bytes 110600 | tf_op jit(solution)/shard_map/ppermute | solution.py:23
  9.3 1.2 %copy-start = (bf16[27,128,128]{2,1,0:T(8,128)(2,1)S(1)}, bf16[27,128,128]{2,1,0:T(8,128)(2,1)}, u32[]{:S(2)}) copy-start(bf16[27,128,128]{2,1,0:T(8,128)(2,1)} %param.11) | copy-start | bytes 2654212
  10.5 8.5 %copy-start.4 = (bf16[256,128]{1,0:T(8,128)(2,1)S(1)}, bf16[256,128]{1,0:T(8,128)(2,1)}, u32[]{:S(2)}) copy-start(bf16[256,128]{1,0:T(8,128)(2,1)} %cotangent.1) | copy-start | bytes 196612
  10.5 20.5 %copy-start.1 = (bf16[27,128,128]{2,1,0:T(8,128)(2,1)S(1)}, bf16[27,128,128]{2,1,0:T(8,128)(2,1)}, u32[]{:S(2)}) copy-start(bf16[27,128,128]{2,1,0:T(8,128)(2,1)} %param.11) | copy-start | bytes 2654212
  13.2 4.2 %collective-permute-start.2 = (bf16[128,128]{1,0:T(8,128)(2,1)S(1)}, bf16[128,128]{1,0:T(8,128)(2,1)S(1)}, u32[]{:S(2)}, u32[]{:S(2)}) collective-permute-start(bf16[128,128]{1,0:T(8,128)(2,1)S(1)} %get-tuple-element.32), channel_id=1, source_target_pairs={{0,1},{1,0},{2,3},{3,2},{4,5},{5,4},{6,7},{7,6},{8,9},{9,8},{10,11... | collective-permute-start | bytes 98312 | tf_op jit(solution)/shard_map/ppermute | solution.py:17
  13.3 5.7 %collective-permute-start.3 = (bf16[128,128]{1,0:T(8,128)(2,1)S(1)}, bf16[128,128]{1,0:T(8,128)(2,1)S(1)}, u32[]{:S(2)}, u32[]{:S(2)}) collective-permute-start(bf16[128,128]{1,0:T(8,128)(2,1)S(1)} %get-tuple-element.33), channel_id=1, source_target_pairs={{1,2},{2,1},{3,4},{4,3},{5,6},{6,5},{9,10},{10,9},{11,12},{12,11},... | collective-permute-start | bytes 98312 | tf_op jit(solution)/shard_map/ppermute | solution.py:23
  19.0 1.2 %copy-start.3 = (bf16[27,128,128]{2,1,0:T(8,128)(2,1)S(1)}, bf16[27,128,128]{2,1,0:T(8,128)(2,1)}, u32[]{:S(2)}) copy-start(bf16[27,128,128]{2,1,0:T(8,128)(2,1)} %param.12) | copy-start | bytes 2654212
  25.6 5.3 %collective-permute-start.4 = (bf16[1856,128]{1,0:T(8,128)(2,1)S(1)}, bf16[1856,128]{1,0:T(8,128)(2,1)S(1)}, u32[]{:S(2)}, u32[]{:S(2)}) collective-permute-start(bf16[1856,128]{1,0:T(8,128)(2,1)S(1)} %get-tuple-element.37), channel_id=1, source_target_pairs={{0,1},{1,0},{2,3},{3,2},{4,5},{5,4},{6,7},{7,6},{8,9},{9,8},{10,11... | collective-permute-start | bytes 1425416 | tf_op jit(solution)/shard_map/ppermute | solution.py:17
  25.6 5.3 %collective-permute-start.5 = (bf16[128,128]{1,0:T(8,128)(2,1)S(1)}, bf16[128,128]{1,0:T(8,128)(2,1)S(1)}, u32[]{:S(2)}, u32[]{:S(2)}) collective-permute-start(bf16[128,128]{1,0:T(8,128)(2,1)S(1)} %get-tuple-element.38), channel_id=1, source_target_pairs={{1,2},{2,1},{3,4},{4,3},{5,6},{6,5},{9,10},{10,9},{11,12},{12,11},... | collective-permute-start | bytes 98312 | tf_op jit(solution)/shard_map/ppermute | solution.py:23
  33.8 1.9 %collective-permute-start.6 = (bf16[1856,128]{1,0:T(8,128)(2,1)S(1)}, bf16[1856,128]{1,0:T(8,128)(2,1)S(1)}, u32[]{:S(2)}, u32[]{:S(2)}) collective-permute-start(bf16[1856,128]{1,0:T(8,128)(2,1)S(1)} %get-tuple-element.42), channel_id=1, source_target_pairs={{0,1},{1,0},{2,3},{3,2},{4,5},{5,4},{6,7},{7,6},{8,9},{9,8},{10,11... | collective-permute-start | bytes 1425416 | tf_op jit(solution)/shard_map/ppermute | solution.py:17
  36.5 7.9 %collective-permute-start.10 = (bf16[2,432,128]{2,1,0:T(8,128)(2,1)S(1)}, bf16[2,432,128]{2,1,0:T(8,128)(2,1)S(1)}, u32[]{:S(2)}, u32[]{:S(2)}) collective-permute-start(bf16[2,432,128]{2,1,0:T(8,128)(2,1)S(1)} %get-tuple-element.49), channel_id=1, source_target_pairs={{0,24},{8,16},{16,8},{24,0},{1,25},{9,17},{17,9},{25,1},{2,26},{10... | collective-permute-start | bytes 663560 | tf_op jit(solution)/shard_map/ppermute | solution.py:17
  38.7 10.9 %collective-permute-start.9 = (bf16[2,432,128]{2,1,0:T(8,128)(2,1)S(1)}, bf16[2,432,128]{2,1,0:T(8,128)(2,1)S(1)}, u32[]{:S(2)}, u32[]{:S(2)}) collective-permute-start(bf16[2,432,128]{2,1,0:T(8,128)(2,1)S(1)} %get-tuple-element.48), channel_id=1, source_target_pairs={{0,16},{8,24},{16,0},{24,8},{1,17},{9,25},{17,1},{25,9},{2,18},{10... | collective-permute-start | bytes 663560 | tf_op jit(solution)/shard_map/ppermute | solution.py:17
  38.9 10.6 %collective-permute-start.8 = (bf16[2,432,128]{2,1,0:T(8,128)(2,1)S(1)}, bf16[2,432,128]{2,1,0:T(8,128)(2,1)S(1)}, u32[]{:S(2)}, u32[]{:S(2)}) collective-permute-start(bf16[2,432,128]{2,1,0:T(8,128)(2,1)S(1)} %get-tuple-element.47), channel_id=1, source_target_pairs={{0,8},{8,0},{16,24},{24,16},{1,9},{9,1},{17,25},{25,17},{2,10},{10... | collective-permute-start | bytes 663560 | tf_op jit(solution)/shard_map/ppermute | solution.py:17
  49.6 7.1 %collective-permute-start.11 = (bf16[2,432,128]{2,1,0:T(8,128)(2,1)S(1)}, bf16[2,432,128]{2,1,0:T(8,128)(2,1)S(1)}, u32[]{:S(2)}, u32[]{:S(2)}) collective-permute-start(bf16[2,432,128]{2,1,0:T(8,128)(2,1)S(1)} %add_convert_fusion.1), channel_id=1, source_target_pairs={{0,2},{1,3},{2,0},{3,1},{4,6},{5,7},{6,4},{7,5},{8,10},{9,11},{10,... | collective-permute-start | bytes 663560 | tf_op jit(solution)/shard_map/ppermute | solution.py:17
  56.8 12.1 %collective-permute-start.12 = (bf16[2,432,128]{2,1,0:T(8,128)(2,1)S(1)}, bf16[2,432,128]{2,1,0:T(8,128)(2,1)S(1)}, u32[]{:S(2)}, u32[]{:S(2)}) collective-permute-start(bf16[2,432,128]{2,1,0:T(8,128)(2,1)S(1)} %add_convert_fusion), channel_id=1, source_target_pairs={{0,4},{1,5},{2,6},{3,7},{4,0},{5,1},{6,2},{7,3},{8,12},{9,13},{10,... | collective-permute-start | bytes 663560 | tf_op jit(solution)/shard_map/ppermute | solution.py:17
  68.9 7.9 %collective-permute-start.13 = (f32[2,432,128]{2,1,0:T(8,128)S(1)}, f32[2,432,128]{2,1,0:T(8,128)S(1)}, u32[]{:S(2)}, u32[]{:S(2)}) collective-permute-start(f32[2,432,128]{2,1,0:T(8,128)S(1)} %add_multiply_fusion), channel_id=1, source_target_pairs={{0,1},{1,0},{2,3},{3,2},{4,5},{5,4},{6,7},{7,6},{8,9},{9,8},{10,11... | collective-permute-start | bytes 1327112 | tf_op jit(solution)/shard_map/ppermute | solution.py:17
  70.4 5.2 %collective-permute-start.7 = (bf16[128,128]{1,0:T(8,128)(2,1)S(1)}, bf16[128,128]{1,0:T(8,128)(2,1)S(1)}, u32[]{:S(2)}, u32[]{:S(2)}) collective-permute-start(bf16[128,128]{1,0:T(8,128)(2,1)S(1)} %get-tuple-element.43), channel_id=1, source_target_pairs={{1,2},{2,1},{3,4},{4,3},{5,6},{6,5},{9,10},{10,9},{11,12},{12,11},... | collective-permute-start | bytes 98312 | tf_op jit(solution)/shard_map/ppermute | solution.py:23

commit v2 on v1

--- a/solution.py
+++ b/solution.py
@@ -18,9 +18,16 @@
 
 
 def crossed(value):
-    count = lax.axis_size("tile")
-    pairs = [(i, ((i + 1) ^ 1) - 1) for i in range(count)]
-    return lax.ppermute(value, "tile", [(i, j) for i, j in pairs if 0 <= j < count])
+    groups, count = lax.axis_size("grp"), lax.axis_size("tile")
+    pairs = []
+    for i in range(groups * count):
+        group, tile = divmod(i, count)
+        other = ((tile + 1) ^ 1) - 1
+        if 0 <= other < count:
+            pairs.append((i, group * count + other))
+        elif (group ^ 1) < groups:
+            pairs.append((i, (group ^ 1) * count + tile))
+    return lax.ppermute(value, ("grp", "tile"), pairs)
 
 
 def sigmoid_terms(values):
@@ -51,8 +58,9 @@
     both = count == 2
     entries[0] = first
     entries[1] = second
-    to_prev = jnp.concatenate([first[i * KINDS : i * KINDS + 1] for i in range(per)], axis=0)
-    last = jnp.where(both, second, first)
+    head = jnp.where(info[3] == 0, -1.0, first)
+    to_prev = jnp.concatenate([head[i * KINDS : i * KINDS + 1] for i in range(per)], axis=0)
+    last = jnp.where(info[3] == 1, -1.0, jnp.where(both, second, first))
     to_next = jnp.concatenate([last[i * KINDS + 2 : i * KINDS + 3] for i in range(per)], axis=0)
     front, back = features[:blk, :], features[blk:, :]
     tail = jnp.where(both, back, front)
@@ -279,7 +287,7 @@
                 sends[d - 1][half] = value.astype(BF16)
 
 
-def call(kernel, outs, *args, scratch=()):
+def call(kernel, outs, *args, scratch=(), micros=1):
     specs = [pl.BlockSpec(memory_space=pltpu.SMEM)]
     specs += [pl.BlockSpec(memory_space=pltpu.VMEM)] * (len(args) - 1)
     return pl.pallas_call(
@@ -289,6 +297,9 @@
         out_specs=[pl.BlockSpec(memory_space=pltpu.VMEM)] * len(outs),
         scratch_shapes=[pltpu.VMEM(shape, kind) for shape, kind in scratch],
         compiler_params=pltpu.CompilerParams(vmem_limit_bytes=LIMIT),
+        cost_estimate=pl.CostEstimate(
+            flops=micros * 10**9, bytes_accessed=micros * 3 * 10**6, transcendentals=0
+        ),
     )(*args)
 
 
@@ -299,9 +310,9 @@
     rows, channels = features.shape
     n_grp, n_tile = lax.axis_size("grp"), lax.axis_size("tile")
     per = offsets // KINDS
-    info = jnp.stack(
-        [lax.axis_index("tile") % 2, block_count[0], lax.axis_index("grp")]
-    ).astype(jnp.int32)
+    tile = lax.axis_index("tile")
+    end = jnp.where(tile == 0, 0, jnp.where(tile == n_tile - 1, 1, 2))
+    info = jnp.stack([tile % 2, block_count[0], lax.axis_index("grp"), end]).astype(jnp.int32)
     flat_one = weight_one.reshape(offsets * channels, channels)
     flat_two = weight_two.reshape(offsets * channels, channels)
     packed = blk + per + (-per % 16)
@@ -317,6 +328,7 @@
         pack_kernel,
         [((2, offsets, blk), F32), ((packed, channels), BF16), ((packed, channels), BF16)],
         info, features, source_rows, target_codes,
+        micros=3,
     )
     cross, core = crossed(cross), swapped(core, "tile", 1)
     entries, halo, hidden, slope, core, cross = call(
@@ -324,6 +336,7 @@
         [((2 * offsets, blk), F32), ((2, blk, channels), BF16), field, summed, block, block],
         info, local, features, core, cross, flat_one,
         scratch=[(wide, BF16)],
+        micros=3,
     )
     cross, core = crossed(cross), swapped(core, "tile", 1)
     result, grad_sum, own, keep_two, core_two, cross = call(
@@ -331,6 +344,7 @@
         [field, field, summed, keep_shape, core_shape, block],
         info, entries, features, hidden, core, cross, flat_two, out_cotangent,
         scratch=[(wide, BF16), (wide, BF16), ((offsets * channels, channels), F32)],
+        micros=5,
     )
     cross, core_two = crossed(cross), swapped(core_two, "tile", 1)
     own, keep_one, core_one, cross = call(
@@ -346,9 +360,11 @@
         [(shard, F32)] + [(shard, BF16)] * (n_grp - 1),
         info, keep_one, keep_two, core_one, core_two,
     )
-    for d, send in enumerate(sends):
-        mine = mine + swapped(send, "grp", d + 1).astype(F32)
-    cross = crossed(cross)
+    cross, *sends = lax.optimization_barrier((cross, *sends))
+    got = [swapped(send, "grp", d + 1) for d, send in enumerate(sends)]
+    cross, *got = lax.optimization_barrier((crossed(cross), *got))
+    for part in got:
+        mine = mine + part.astype(F32)
     (input_grad,) = call(last_kernel, [field], info, own, core_one, cross)
     bits = 2
     while bits < n_tile:
@@ -358,7 +374,7 @@
     voxel_total = n_grp * n_tile * rows
     mine = mine[:, :half] * float(voxel_total) ** (-0.5)
     other = swapped(mine, "tile", 1)
-    odd = lax.axis_index("tile") % 2 == 1
+    odd = tile % 2 == 1
     whole = jnp.concatenate(
         [jnp.where(odd, other, mine), jnp.where(odd, mine, other)], axis=1
     )

time: 78.3 us -> 65.5 us (0.84)
  starting transfers between devices: 22.8 us -> 14.1 us
  waiting for transfers between devices: 35.4 us -> 33 us
  local copies, waits for them, and re-layouts: 3.29 us -> 1.53 us
    ppermute x4, starting transfers between devices: 14.3 us -> 6.48 us  [crossed(): return lax.ppermute(value, ('grp', 'tile'), pairs)]
    ppermute x10, waiting for transfers between devices: 27.3 us -> 24 us  [swapped(): lax.ppermute(value, axis, [(i, i ^ bits) for i in range(count) if i ^ bit...]
    unnamed x15 -> x11, local copies, waits for them, and re-layouts: 3.29 us -> 1.53 us
    ppermute x4, waiting for transfers between devices: 8.07 us -> 8.98 us  [crossed(): return lax.ppermute(value, ('grp', 'tile'), pairs)]
    ppermute x10, starting transfers between devices: 8.5 us -> 7.66 us  [swapped(): lax.ppermute(value, axis, [(i, i ^ bits) for i in range(count) if i ^ bit...]
  transfers between devices with their start and end apart: 14 -> 14, of which waited for: 9 -> 11; matrix products, arithmetic and copies ran while one was open for 0% -> 0% of each run, Pallas kernels for 2% -> 2%
where the time goes in v2:
time: 65.5 us; the launch traced here: 65 us
  waiting for transfers between devices  33 us (50%)
  starting transfers between devices  14.1 us (22%)
  Pallas kernels  13.6 us (21%)
  local copies, waits for them, and re-layouts  1.53 us (2%)
  between operations  1.39 us (2%)
  other arithmetic  1.37 us (2%)
    ppermute x10, waiting for transfers between devices, swapped(): lax.ppermute(value, axis, [(i, i ^ bits) for i in range(count) if i ^ bit...  24 us
    pallas_call x6, Pallas kernels, call(): pl.pallas_call(kernel, out_shape=[jax.ShapeDtypeStruct(shape, kind) for s...  13.6 us
    ppermute x4, waiting for transfers between devices, crossed(): return lax.ppermute(value, ('grp', 'tile'), pairs)  8.98 us
    ppermute x10, starting transfers between devices, swapped(): lax.ppermute(value, axis, [(i, i ^ bits) for i in range(count) if i ^ bit...  7.66 us
    ppermute x4, starting transfers between devices, crossed(): return lax.ppermute(value, ('grp', 'tile'), pairs)  6.48 us
    unnamed x11, local copies, waits for them, and re-layouts  1.53 us
  transfers between devices with their start and end apart: 14, of which 11 were waited for; matrix products, arithmetic and copies ran while one was open for 0% of the time, Pallas kernels for 2%

profile of v2, /device:TPU:1, one launch (start us, length us, event | category | flops | bytes accessed | tf_op | source)
XLA Modules:
  0.0 65.0 jit_solution(15519334527363801345)
XLA Ops:
  0.6 0.0 copy-start.3
  1.3 0.8 %copy.11.codes = s32[27,2]{1,0:T(8,128)S(1)} copy(s32[27,2]{0,1:T(2,128)} %param.9) | data formatting | bytes 432 | tf_op args[2]
  2.1 0.1 pad_add_fusion.info
  2.2 0.0 copy-done.3
  2.2 0.0 copy-start.4
  2.2 0.7 %copy-done.4 = s32[27,2,128]{2,1,0:T(2,128)S(1)} copy-done((s32[27,2,128]{2,1,0:T(2,128)S(1)}, s32[27,2,128]{2,1,0:T(2,128)}, u32[]{:S(2)}) %copy-start.4) | copy-done | bytes 27672
  2.9 0.6 shard_map.102
  3.6 0.1 collective-permute-start
  3.7 2.7 %collective-permute-start.1 = (bf16[144,128]{1,0:T(8,128)(2,1)S(1)}, bf16[144,128]{1,0:T(8,128)(2,1)S(1)}, u32[]{:S(2)}, u32[]{:S(2)}) collective-permute-start(bf16[144,128]{1,0:T(8,128)(2,1)S(1)} %get-tuple-element.37), channel_id=1, source_target_pairs={{0,8},{1,2},{2,1},{3,4},{4,3},{5,6},{6,5},{7,15},{8,0},{9,10},{10,... | collective-permute-start | bytes 110600 | tf_op jit(solution)/shard_map/ppermute | solution.py:30
  6.4 0.0 collective-permute-done.core_in
  6.4 1.8 %collective-permute-done.1.cross_in = bf16[144,128]{1,0:T(8,128)(2,1)S(1)} collective-permute-done((bf16[144,128]{1,0:T(8,128)(2,1)S(1)}, bf16[144,128]{1,0:T(8,128)(2,1)S(1)}, u32[]{:S(2)}, u32[]{:S(2)}) %collective-permute-start.1) | collective-permute-done | bytes 36896 | tf_op jit(solution)/shard_map/ppermute | solution.py:30
  8.3 0.0 copy-done.1
  8.3 2.7 %shard_map.103 = (f32[54,128]{1,0:T(8,128)S(1)}, bf16[2,128,128]{2,1,0:T(8,128)(2,1)S(1)}, bf16[256,128]{1,0:T(8,128)(2,1)S(1)}, f32[256,128]{1,0:T(8,128)S(1)},...) custom-call(s32[4]{0:T(128)S(1)} %pad_add_fusion.info, f32[2,27,128]{2,1,0:T(8,128)S(1)} %get-tuple-element.35.local, ...), custom_call_target="tpu_custom_call" | custom-call | flops 3000000000 | bytes 9000000 | tf_op jit(solution)/shard_map/pallas_call | solution.py:293
  11.0 0.5 collective-permute-start.2
  11.4 1.6 %collective-permute-start.3 = (bf16[128,128]{1,0:T(8,128)(2,1)S(1)}, bf16[128,128]{1,0:T(8,128)(2,1)S(1)}, u32[]{:S(2)}, u32[]{:S(2)}) collective-permute-start(bf16[128,128]{1,0:T(8,128)(2,1)S(1)} %get-tuple-element.41), channel_id=1, source_target_pairs={{0,8},{1,2},{2,1},{3,4},{4,3},{5,6},{6,5},{7,15},{8,0},{9,10},{10,... | collective-permute-start | bytes 98312 | tf_op jit(solution)/shard_map/ppermute | solution.py:30
  13.0 0.0 collective-permute-done.2.core_in
  13.0 2.1 %collective-permute-done.3.cross_in = bf16[128,128]{1,0:T(8,128)(2,1)S(1)} collective-permute-done((bf16[128,128]{1,0:T(8,128)(2,1)S(1)}, bf16[128,128]{1,0:T(8,128)(2,1)S(1)}, u32[]{:S(2)}, u32[]{:S(2)}) %collective-permute-start.3) | collective-permute-done | bytes 32800 | tf_op jit(solution)/shard_map/ppermute | solution.py:30
  15.1 0.0 copy-done
  15.1 0.0 copy-done.2
  15.1 5.4 %shard_map.104 = (bf16[256,128]{1,0:T(8,128)(2,1)}, bf16[256,128]{1,0:T(8,128)(2,1)S(1)}, f32[256,128]{1,0:T(8,128)S(1)}, f32[4,432,128]{2,1,0:T(8,128)S(1)}, bf...) custom-call(s32[4]{0:T(128)S(1)} %pad_add_fusion.info, f32[54,128]{1,0:T(8,128)S(1)} %get-tuple-element.38.entries, ...), custom_call_target="tpu_custom_call" | custom-call | flops 5000000000 | bytes 15000000 | tf_op jit(solution)/shard_map/pallas_call | solution.py:293
  20.5 0.4 collective-permute-start.4
  20.9 1.0 %collective-permute-start.5 = (bf16[128,128]{1,0:T(8,128)(2,1)S(1)}, bf16[128,128]{1,0:T(8,128)(2,1)S(1)}, u32[]{:S(2)}, u32[]{:S(2)}) collective-permute-start(bf16[128,128]{1,0:T(8,128)(2,1)S(1)} %get-tuple-element.46), channel_id=1, source_target_pairs={{0,8},{1,2},{2,1},{3,4},{4,3},{5,6},{6,5},{7,15},{8,0},{9,10},{10,... | collective-permute-start | bytes 98312 | tf_op jit(solution)/shard_map/ppermute | solution.py:30
  21.9 2.6 %collective-permute-done.5.cross_in = bf16[128,128]{1,0:T(8,128)(2,1)S(1)} collective-permute-done((bf16[128,128]{1,0:T(8,128)(2,1)S(1)}, bf16[128,128]{1,0:T(8,128)(2,1)S(1)}, u32[]{:S(2)}, u32[]{:S(2)}) %collective-permute-start.5) | collective-permute-done | bytes 32800 | tf_op jit(solution)/shard_map/ppermute | solution.py:30
  24.5 0.0 collective-permute-done.4.core_in.core_two
  24.5 2.9 %shard_map.105 = (f32[256,128]{1,0:T(8,128)S(1)}, f32[4,432,128]{2,1,0:T(8,128)S(1)}, bf16[1856,128]{1,0:T(8,128)(2,1)S(1)}, bf16[128,128]{1,0:T(8,128)(2,1)S(1)}) custom-call(s32[4]{0:T(128)S(1)} %pad_add_fusion.info, f32[54,128]{1,0:T(8,128)S(1)} %get-tuple-element.38.entries, bf16[256,128]{1,0:T(8,128)(2,1)S(1)} %copy-done.3, ...), custom_call_target="tpu_custom_call" | custom-call | flops 1000000000 | bytes 3000000 | tf_op jit(solution)/shard_map/pallas_call | solution.py:293
  27.4 0.5 collective-permute-start.6
  27.9 1.5 %collective-permute-done.6.core_one.core_in = bf16[1856,128]{1,0:T(8,128)(2,1)S(1)} collective-permute-done((bf16[1856,128]{1,0:T(8,128)(2,1)S(1)}, bf16[1856,128]{1,0:T(8,128)(2,1)S(1)}, u32[]{:S(2)}, u32[]{:S(2)}) %collective-permute-start.6) | collective-permute-done | bytes 475168 | tf_op jit(solution)/shard_map/ppermute | solution.py:17
  29.4 0.7 %shard_map.106 = (f32[2,432,128]{2,1,0:T(8,128)S(1)}, bf16[2,432,128]{2,1,0:T(8,128)(2,1)S(1)}, bf16[2,432,128]{2,1,0:T(8,128)(2,1)S(1)}, bf16[2,432,128]{2,1,0:T(8,128)(2,1)S(1)}) custom-call(s32[4]{0:T(128)S(1)} %pad_add_fusion.info, f32[4,432,128]{2,1,0:T(8,128)S(1)} %get-tuple-element.52.keep_one, f32[4,432,128]{2,1,0:T(8,128)S(1)} %get-tuple-element.53.keep_two, ...), custom_call_target="tpu_custom_call" | custom-call | flops 1000000000 | bytes 3000000 | tf_op jit(solution)/shard_map/pallas_call | solution.py:293
  30.1 1.8 %collective-permute-start.8 = (bf16[2,432,128]{2,1,0:T(8,128)(2,1)S(1)}, bf16[2,432,128]{2,1,0:T(8,128)(2,1)S(1)}, u32[]{:S(2)}, u32[]{:S(2)}) collective-permute-start(bf16[2,432,128]{2,1,0:T(8,128)(2,1)S(1)} %get-tuple-element.58), channel_id=1, source_target_pairs={{0,8},{8,0},{16,24},{24,16},{1,9},{9,1},{17,25},{25,17},{2,10},{10... | collective-permute-start | bytes 663560 | tf_op jit(solution)/shard_map/ppermute | solution.py:17
  31.9 1.2 %collective-permute-start.9 = (bf16[2,432,128]{2,1,0:T(8,128)(2,1)S(1)}, bf16[2,432,128]{2,1,0:T(8,128)(2,1)S(1)}, u32[]{:S(2)}, u32[]{:S(2)}) collective-permute-start(bf16[2,432,128]{2,1,0:T(8,128)(2,1)S(1)} %get-tuple-element.59), channel_id=1, source_target_pairs={{0,16},{8,24},{16,0},{24,8},{1,17},{9,25},{17,1},{25,9},{2,18},{10... | collective-permute-start | bytes 663560 | tf_op jit(solution)/shard_map/ppermute | solution.py:17
  33.1 0.0 collective-permute-start.10
  33.1 1.2 %collective-permute-start.7 = (bf16[128,128]{1,0:T(8,128)(2,1)S(1)}, bf16[128,128]{1,0:T(8,128)(2,1)S(1)}, u32[]{:S(2)}, u32[]{:S(2)}) collective-permute-start(bf16[128,128]{1,0:T(8,128)(2,1)S(1)} %get-tuple-element.57), channel_id=1, source_target_pairs={{0,8},{1,2},{2,1},{3,4},{4,3},{5,6},{6,5},{7,15},{8,0},{9,10},{10,... | collective-permute-start | bytes 98312 | tf_op jit(solution)/shard_map/ppermute | solution.py:30
  34.4 2.4 %collective-permute-done.7.cross_in = bf16[128,128]{1,0:T(8,128)(2,1)S(1)} collective-permute-done((bf16[128,128]{1,0:T(8,128)(2,1)S(1)}, bf16[128,128]{1,0:T(8,128)(2,1)S(1)}, u32[]{:S(2)}, u32[]{:S(2)}) %collective-permute-start.7) | collective-permute-done | bytes 32800 | tf_op jit(solution)/shard_map/ppermute | solution.py:30
  36.8 0.6 collective-permute-done.8
  37.4 0.8 %collective-permute-done.9 = bf16[2,432,128]{2,1,0:T(8,128)(2,1)S(1)} collective-permute-done((bf16[2,432,128]{2,1,0:T(8,128)(2,1)S(1)}, bf16[2,432,128]{2,1,0:T(8,128)(2,1)S(1)}, u32[]{:S(2)}, u32[]{:S(2)}) %collective-permute-start.9) | collective-permute-done | bytes 221216 | tf_op jit(solution)/shard_map/ppermute | solution.py:17
  38.2 4.9 %collective-permute-done.10 = bf16[2,432,128]{2,1,0:T(8,128)(2,1)S(1)} collective-permute-done((bf16[2,432,128]{2,1,0:T(8,128)(2,1)S(1)}, bf16[2,432,128]{2,1,0:T(8,128)(2,1)S(1)}, u32[]{:S(2)}, u32[]{:S(2)}) %collective-permute-start.10) | collective-permute-done | bytes 221216 | tf_op jit(solution)/shard_map/ppermute | solution.py:17
  43.1 0.1 add_convert_fusion.1
  43.2 0.5 collective-permute-start.11
  43.6 5.1 %collective-permute-done.11 = bf16[2,432,128]{2,1,0:T(8,128)(2,1)S(1)} collective-permute-done((bf16[2,432,128]{2,1,0:T(8,128)(2,1)S(1)}, bf16[2,432,128]{2,1,0:T(8,128)(2,1)S(1)}, u32[]{:S(2)}, u32[]{:S(2)}) %collective-permute-start.11) | collective-permute-done | bytes 221216 | tf_op jit(solution)/shard_map/ppermute | solution.py:17
  48.8 0.1 add_convert_fusion
  48.8 1.7 %collective-permute-start.12 = (bf16[2,432,128]{2,1,0:T(8,128)(2,1)S(1)}, bf16[2,432,128]{2,1,0:T(8,128)(2,1)S(1)}, u32[]{:S(2)}, u32[]{:S(2)}) collective-permute-start(bf16[2,432,128]{2,1,0:T(8,128)(2,1)S(1)} %add_convert_fusion), channel_id=1, source_target_pairs={{0,4},{1,5},{2,6},{3,7},{4,0},{5,1},{6,2},{7,3},{8,12},{9,13},{10,... | collective-permute-start | bytes 663560 | tf_op jit(solution)/shard_map/ppermute | solution.py:17
  50.5 10.9 %collective-permute-done.12 = bf16[2,432,128]{2,1,0:T(8,128)(2,1)S(1)} collective-permute-done((bf16[2,432,128]{2,1,0:T(8,128)(2,1)S(1)}, bf16[2,432,128]{2,1,0:T(8,128)(2,1)S(1)}, u32[]{:S(2)}, u32[]{:S(2)}) %collective-permute-start.12) | collective-permute-done | bytes 221216 | tf_op jit(solution)/shard_map/ppermute | solution.py:17
  61.5 0.1 add_multiply_fusion
  61.5 1.0 %collective-permute-start.13 = (f32[2,432,128]{2,1,0:T(8,128)S(1)}, f32[2,432,128]{2,1,0:T(8,128)S(1)}, u32[]{:S(2)}, u32[]{:S(2)}) collective-permute-start(f32[2,432,128]{2,1,0:T(8,128)S(1)} %add_multiply_fusion), channel_id=1, source_target_pairs={{0,1},{1,0},{2,3},{3,2},{4,5},{5,4},{6,7},{7,6},{8,9},{9,8},{10,11... | collective-permute-start | bytes 1327112 | tf_op jit(solution)/shard_map/ppermute | solution.py:17
  62.5 1.2 %shard_map.107 = bf16[256,128]{1,0:T(8,128)(2,1)} custom-call(s32[4]{0:T(128)S(1)} %pad_add_fusion.info, f32[256,128]{1,0:T(8,128)S(1)} %get-tuple-element.49.own, bf16[1856,128]{1,0:T(8,128)(2,1)S(1)} %collective-permute-done.6.core_one.core_in, bf16[128,128]{1,0:T(8,128)(2,1)S(1)} %collective-permute-done.7.cross_in), custom_call_target="tpu_custom_call" | custom-call | flops 1000000000 | bytes 3000000 | tf_op jit(solution)/shard_map/pallas_call | solution.py:293
  63.7 0.2 collective-permute-done.13
  63.9 0.1 broadcast_select_fusion
  64.0 1.0 %fusion.2 = (f32[864,128]{1,0:T(8,128)}, f32[864,128]{1,0:T(8,128)}) fusion(f32[2,432,128]{2,1,0:T(8,128)S(1)} %get-tuple-element.68, f32[2,432,128]{2,1,0:T(8,128)S(1)} %get-tuple-element.69), kind=kLoop, calls=%fused_computation.5 | loop fusion | flops 221184 | bytes 1769472 | tf_op jit(solution)/shard_map/squeeze | solution.py:381
  (3 shorter events, 0.0 us)
Async XLA Ops:
  0.6 1.6 %copy-start.3 = (bf16[256,128]{1,0:T(8,128)(2,1)S(1)}, bf16[256,128]{1,0:T(8,128)(2,1)}, u32[]{:S(2)}) copy-start(bf16[256,128]{1,0:T(8,128)(2,1)} %features.7) | copy-start | bytes 196612
  2.2 0.7 %copy-start.4 = (s32[27,2,128]{2,1,0:T(2,128)S(1)}, s32[27,2,128]{2,1,0:T(2,128)}, u32[]{:S(2)}) copy-start(s32[27,2,128]{2,1,0:T(2,128)} %source_rows.1) | copy-start | bytes 82948
  2.9 5.3 %copy-start.1 = (bf16[27,128,128]{2,1,0:T(8,128)(2,1)S(1)}, bf16[27,128,128]{2,1,0:T(8,128)(2,1)}, u32[]{:S(2)}) copy-start(bf16[27,128,128]{2,1,0:T(8,128)(2,1)} %param.11) | copy-start | bytes 2654212
  3.6 2.8 %collective-permute-start = (bf16[144,128]{1,0:T(8,128)(2,1)S(1)}, bf16[144,128]{1,0:T(8,128)(2,1)S(1)}, u32[]{:S(2)}, u32[]{:S(2)}) collective-permute-start(bf16[144,128]{1,0:T(8,128)(2,1)S(1)} %get-tuple-element.36), channel_id=1, source_target_pairs={{0,1},{1,0},{2,3},{3,2},{4,5},{5,4},{6,7},{7,6},{8,9},{9,8},{10,11... | collective-permute-start | bytes 110600 | tf_op jit(solution)/shard_map/ppermute | solution.py:17
  3.7 4.6 %collective-permute-start.1 = (bf16[144,128]{1,0:T(8,128)(2,1)S(1)}, bf16[144,128]{1,0:T(8,128)(2,1)S(1)}, u32[]{:S(2)}, u32[]{:S(2)}) collective-permute-start(bf16[144,128]{1,0:T(8,128)(2,1)S(1)} %get-tuple-element.37), channel_id=1, source_target_pairs={{0,8},{1,2},{2,1},{3,4},{4,3},{5,6},{6,5},{7,15},{8,0},{9,10},{10,... | collective-permute-start | bytes 110600 | tf_op jit(solution)/shard_map/ppermute | solution.py:30
  8.3 6.8 %copy-start = (bf16[27,128,128]{2,1,0:T(8,128)(2,1)S(1)}, bf16[27,128,128]{2,1,0:T(8,128)(2,1)}, u32[]{:S(2)}) copy-start(bf16[27,128,128]{2,1,0:T(8,128)(2,1)} %param.12) | copy-start | bytes 2654212
  8.3 6.8 %copy-start.2 = (bf16[256,128]{1,0:T(8,128)(2,1)S(1)}, bf16[256,128]{1,0:T(8,128)(2,1)}, u32[]{:S(2)}) copy-start(bf16[256,128]{1,0:T(8,128)(2,1)} %cotangent.1) | copy-start | bytes 196612
  11.0 2.0 %collective-permute-start.2 = (bf16[128,128]{1,0:T(8,128)(2,1)S(1)}, bf16[128,128]{1,0:T(8,128)(2,1)S(1)}, u32[]{:S(2)}, u32[]{:S(2)}) collective-permute-start(bf16[128,128]{1,0:T(8,128)(2,1)S(1)} %get-tuple-element.40), channel_id=1, source_target_pairs={{0,1},{1,0},{2,3},{3,2},{4,5},{5,4},{6,7},{7,6},{8,9},{9,8},{10,11... | collective-permute-start | bytes 98312 | tf_op jit(solution)/shard_map/ppermute | solution.py:17
  11.4 3.6 %collective-permute-start.3 = (bf16[128,128]{1,0:T(8,128)(2,1)S(1)}, bf16[128,128]{1,0:T(8,128)(2,1)S(1)}, u32[]{:S(2)}, u32[]{:S(2)}) collective-permute-start(bf16[128,128]{1,0:T(8,128)(2,1)S(1)} %get-tuple-element.41), channel_id=1, source_target_pairs={{0,8},{1,2},{2,1},{3,4},{4,3},{5,6},{6,5},{7,15},{8,0},{9,10},{10,... | collective-permute-start | bytes 98312 | tf_op jit(solution)/shard_map/ppermute | solution.py:30
  20.5 4.0 %collective-permute-start.4 = (bf16[1856,128]{1,0:T(8,128)(2,1)S(1)}, bf16[1856,128]{1,0:T(8,128)(2,1)S(1)}, u32[]{:S(2)}, u32[]{:S(2)}) collective-permute-start(bf16[1856,128]{1,0:T(8,128)(2,1)S(1)} %get-tuple-element.45), channel_id=1, source_target_pairs={{0,1},{1,0},{2,3},{3,2},{4,5},{5,4},{6,7},{7,6},{8,9},{9,8},{10,11... | collective-permute-start | bytes 1425416 | tf_op jit(solution)/shard_map/ppermute | solution.py:17
  20.9 3.6 %collective-permute-start.5 = (bf16[128,128]{1,0:T(8,128)(2,1)S(1)}, bf16[128,128]{1,0:T(8,128)(2,1)S(1)}, u32[]{:S(2)}, u32[]{:S(2)}) collective-permute-start(bf16[128,128]{1,0:T(8,128)(2,1)S(1)} %get-tuple-element.46), channel_id=1, source_target_pairs={{0,8},{1,2},{2,1},{3,4},{4,3},{5,6},{6,5},{7,15},{8,0},{9,10},{10,... | collective-permute-start | bytes 98312 | tf_op jit(solution)/shard_map/ppermute | solution.py:30
  27.4 1.9 %collective-permute-start.6 = (bf16[1856,128]{1,0:T(8,128)(2,1)S(1)}, bf16[1856,128]{1,0:T(8,128)(2,1)S(1)}, u32[]{:S(2)}, u32[]{:S(2)}) collective-permute-start(bf16[1856,128]{1,0:T(8,128)(2,1)S(1)} %get-tuple-element.50), channel_id=1, source_target_pairs={{0,1},{1,0},{2,3},{3,2},{4,5},{5,4},{6,7},{7,6},{8,9},{9,8},{10,11... | collective-permute-start | bytes 1425416 | tf_op jit(solution)/shard_map/ppermute | solution.py:17
  30.1 7.3 %collective-permute-start.8 = (bf16[2,432,128]{2,1,0:T(8,128)(2,1)S(1)}, bf16[2,432,128]{2,1,0:T(8,128)(2,1)S(1)}, u32[]{:S(2)}, u32[]{:S(2)}) collective-permute-start(bf16[2,432,128]{2,1,0:T(8,128)(2,1)S(1)} %get-tuple-element.58), channel_id=1, source_target_pairs={{0,8},{8,0},{16,24},{24,16},{1,9},{9,1},{17,25},{25,17},{2,10},{10... | collective-permute-start | bytes 663560 | tf_op jit(solution)/shard_map/ppermute | solution.py:17
  31.9 6.3 %collective-permute-start.9 = (bf16[2,432,128]{2,1,0:T(8,128)(2,1)S(1)}, bf16[2,432,128]{2,1,0:T(8,128)(2,1)S(1)}, u32[]{:S(2)}, u32[]{:S(2)}) collective-permute-start(bf16[2,432,128]{2,1,0:T(8,128)(2,1)S(1)} %get-tuple-element.59), channel_id=1, source_target_pairs={{0,16},{8,24},{16,0},{24,8},{1,17},{9,25},{17,1},{25,9},{2,18},{10... | collective-permute-start | bytes 663560 | tf_op jit(solution)/shard_map/ppermute | solution.py:17
  33.1 9.9 %collective-permute-start.10 = (bf16[2,432,128]{2,1,0:T(8,128)(2,1)S(1)}, bf16[2,432,128]{2,1,0:T(8,128)(2,1)S(1)}, u32[]{:S(2)}, u32[]{:S(2)}) collective-permute-start(bf16[2,432,128]{2,1,0:T(8,128)(2,1)S(1)} %get-tuple-element.60), channel_id=1, source_target_pairs={{0,24},{8,16},{16,8},{24,0},{1,25},{9,17},{17,9},{25,1},{2,26},{10... | collective-permute-start | bytes 663560 | tf_op jit(solution)/shard_map/ppermute | solution.py:17
  33.1 3.6 %collective-permute-start.7 = (bf16[128,128]{1,0:T(8,128)(2,1)S(1)}, bf16[128,128]{1,0:T(8,128)(2,1)S(1)}, u32[]{:S(2)}, u32[]{:S(2)}) collective-permute-start(bf16[128,128]{1,0:T(8,128)(2,1)S(1)} %get-tuple-element.57), channel_id=1, source_target_pairs={{0,8},{1,2},{2,1},{3,4},{4,3},{5,6},{6,5},{7,15},{8,0},{9,10},{10,... | collective-permute-start | bytes 98312 | tf_op jit(solution)/shard_map/ppermute | solution.py:30
  43.2 5.6 %collective-permute-start.11 = (bf16[2,432,128]{2,1,0:T(8,128)(2,1)S(1)}, bf16[2,432,128]{2,1,0:T(8,128)(2,1)S(1)}, u32[]{:S(2)}, u32[]{:S(2)}) collective-permute-start(bf16[2,432,128]{2,1,0:T(8,128)(2,1)S(1)} %add_convert_fusion.1), channel_id=1, source_target_pairs={{0,2},{1,3},{2,0},{3,1},{4,6},{5,7},{6,4},{7,5},{8,10},{9,11},{10,... | collective-permute-start | bytes 663560 | tf_op jit(solution)/shard_map/ppermute | solution.py:17
  48.8 12.6 %collective-permute-start.12 = (bf16[2,432,128]{2,1,0:T(8,128)(2,1)S(1)}, bf16[2,432,128]{2,1,0:T(8,128)(2,1)S(1)}, u32[]{:S(2)}, u32[]{:S(2)}) collective-permute-start(bf16[2,432,128]{2,1,0:T(8,128)(2,1)S(1)} %add_convert_fusion), channel_id=1, source_target_pairs={{0,4},{1,5},{2,6},{3,7},{4,0},{5,1},{6,2},{7,3},{8,12},{9,13},{10,... | collective-permute-start | bytes 663560 | tf_op jit(solution)/shard_map/ppermute | solution.py:17
  61.5 2.4 %collective-permute-start.13 = (f32[2,432,128]{2,1,0:T(8,128)S(1)}, f32[2,432,128]{2,1,0:T(8,128)S(1)}, u32[]{:S(2)}, u32[]{:S(2)}) collective-permute-start(f32[2,432,128]{2,1,0:T(8,128)S(1)} %add_multiply_fusion), channel_id=1, source_target_pairs={{0,1},{1,0},{2,3},{3,2},{4,5},{5,4},{6,7},{7,6},{8,9},{9,8},{10,11... | collective-permute-start | bytes 1327112 | tf_op jit(solution)/shard_map/ppermute | solution.py:17

commit v3 on v2

--- a/solution.py
+++ b/solution.py
@@ -272,19 +272,29 @@
     input_grad[...] = joined(own[...], odd, both, core, cross, blk).astype(BF16)
 
 
-def shards_kernel(info, keep_one, keep_two, core_one, core_two, own, *sends):
-    shards, slot, _ = keep_one.shape
-    blk = core_one.shape[0] - shards * slot
+def shards_kernel(info, keep, core, own, *sends):
+    shards, slot, _ = keep.shape
+    blk = core.shape[0] - shards * slot
     me = info[2]
     for d in range(shards):
         to = me ^ d
         at = pl.ds(pl.multiple_of(blk + to * slot, 16), slot)
-        for half, keep, core in ((0, keep_one, core_one), (1, keep_two, core_two)):
-            value = keep[to] + core[at, :].astype(F32)
-            if d == 0:
-                own[half] = value
-            else:
-                sends[d - 1][half] = value.astype(BF16)
+        value = keep[to] + core[at, :].astype(F32)
+        if d == 0:
+            own[...] = value
+        else:
+            sends[d - 1][...] = value.astype(BF16)
+
+
+def after(first, later):
+    return lax.optimization_barrier((first, later))[1]
+
+
+def added(value, others):
+    value = value.astype(F32)
+    for other in others:
+        value = value + other.astype(F32)
+    return value
 
 
 def call(kernel, outs, *args, scratch=(), micros=1):
@@ -347,38 +357,51 @@
         micros=5,
     )
     cross, core_two = crossed(cross), swapped(core_two, "tile", 1)
+    shard = (slot, channels)
+    shards = [(shard, F32)] + [(shard, BF16)] * (n_grp - 1)
+    mine_two, *sends_two = call(shards_kernel, shards, info, keep_two, core_two)
+    got_two = [swapped(send, "grp", d + 1) for d, send in enumerate(sends_two)]
+    own = after(sends_two[-1], own)
     own, keep_one, core_one, cross = call(
         third_kernel,
         [summed, keep_shape, core_shape, block],
         info, entries, features, halo, own, core_two, cross, slope, grad_sum, flat_one,
         scratch=[(wide, BF16), ((offsets * channels, channels), F32)],
+        micros=3,
     )
     core_one = swapped(core_one, "tile", 1)
-    shard = (2, slot, channels)
-    mine, *sends = call(
-        shards_kernel,
-        [(shard, F32)] + [(shard, BF16)] * (n_grp - 1),
-        info, keep_one, keep_two, core_one, core_two,
-    )
-    cross, *sends = lax.optimization_barrier((cross, *sends))
-    got = [swapped(send, "grp", d + 1) for d, send in enumerate(sends)]
-    cross, *got = lax.optimization_barrier((crossed(cross), *got))
-    for part in got:
-        mine = mine + part.astype(F32)
+    mine_one, *sends_one = call(shards_kernel, shards, info, keep_one, core_one)
+    got_one = [swapped(send, "grp", d + 1) for d, send in enumerate(sends_one)]
+    cross = crossed(after(sends_one[-1], cross))
+    got_two = [after(cross, got) for got in got_two]
+    two = added(mine_two, got_two).astype(BF16)
+    steps = [1 << b for b in range(1, (n_tile - 1).bit_length())]
+    other_two = swapped(two, "tile", steps[0])
+    one = added(mine_one, got_one).astype(BF16)
+    one = after(cross, one)
     (input_grad,) = call(last_kernel, [field], info, own, core_one, cross)
-    bits = 2
-    while bits < n_tile:
-        mine = mine.astype(BF16)
-        mine = mine.astype(F32) + swapped(mine, "tile", bits).astype(F32)
-        bits *= 2
+    for at, bits in enumerate(steps):
+        other_one = swapped(one, "tile", bits)
+        two = added(two, [other_two])
+        if at + 1 < len(steps):
+            two = after(one, two.astype(BF16))
+            other_two = swapped(two, "tile", steps[at + 1])
+            one = added(one, [other_one]).astype(BF16)
+        else:
+            one = added(one, [other_one])
     voxel_total = n_grp * n_tile * rows
-    mine = mine[:, :half] * float(voxel_total) ** (-0.5)
-    other = swapped(mine, "tile", 1)
+    scale = float(voxel_total) ** (-0.5)
     odd = tile % 2 == 1
-    whole = jnp.concatenate(
-        [jnp.where(odd, other, mine), jnp.where(odd, mine, other)], axis=1
-    )
-    return (result, input_grad, whole[0], whole[1])
+    outs = []
+    for half_sum in (one, two):
+        half_sum = half_sum[:half] * scale
+        other = swapped(half_sum, "tile", 1)
+        outs.append(
+            jnp.concatenate(
+                [jnp.where(odd, other, half_sum), jnp.where(odd, half_sum, other)], axis=0
+            )
+        )
+    return (result, input_grad, outs[0], outs[1])
 
 
 def solution(mesh):

time: 65.5 us -> 58.8 us (0.90)
  waiting for transfers between devices: 33 us -> 10.1 us
  starting transfers between devices: 14.1 us -> 29 us
    ppermute x10 -> x16, waiting for transfers between devices: 24 us -> 4.65 us  [swapped(): lax.ppermute(value, axis, [(i, i ^ bits) for i in range(count) if i ^ bit...]
    ppermute x10 -> x16, starting transfers between devices: 7.66 us -> 22.5 us  [swapped(): lax.ppermute(value, axis, [(i, i ^ bits) for i in range(count) if i ^ bit...]
    ppermute x4, waiting for transfers between devices: 8.98 us -> 5.44 us  [crossed(): return lax.ppermute(value, ('grp', 'tile'), pairs)]
    concatenate x0 -> x2, other arithmetic: none -> 1.58 us  [on_device(): jnp.concatenate([jnp.where(odd, other, half_sum), jnp.where(odd, half_sum...]
    squeeze x1 -> x0, other arithmetic: 0.97 us -> none  [on_device(): return (result, input_grad, whole[0], whole[1])]
    pallas_call x6 -> x7, Pallas kernels: 13.6 us -> 14.1 us  [call(): pl.pallas_call(kernel, out_shape=[jax.ShapeDtypeStruct(shape, kind) for s...]
  transfers between devices with their start and end apart: 14 -> 20, of which waited for: 11 -> 9; matrix products, arithmetic and copies ran while one was open for 0% -> 2% of each run, Pallas kernels for 2% -> 4%
where the time goes in v3:
time: 58.8 us; the launch traced here: 58.2 us
  starting transfers between devices  29 us (49%)
  Pallas kernels  14.1 us (24%)
  waiting for transfers between devices  10.1 us (17%)
  other arithmetic  2.02 us (3%)
  local copies, waits for them, and re-layouts  1.53 us (3%)
  between operations  1.41 us (2%)
    ppermute x16, starting transfers between devices, swapped(): lax.ppermute(value, axis, [(i, i ^ bits) for i in range(count) if i ^ bit...  22.5 us
    pallas_call x7, Pallas kernels, call(): pl.pallas_call(kernel, out_shape=[jax.ShapeDtypeStruct(shape, kind) for s...  14.1 us
    ppermute x4, starting transfers between devices, crossed(): return lax.ppermute(value, ('grp', 'tile'), pairs)  6.53 us
    ppermute x4, waiting for transfers between devices, crossed(): return lax.ppermute(value, ('grp', 'tile'), pairs)  5.44 us
    ppermute x16, waiting for transfers between devices, swapped(): lax.ppermute(value, axis, [(i, i ^ bits) for i in range(count) if i ^ bit...  4.65 us
    concatenate x2, other arithmetic, on_device(): jnp.concatenate([jnp.where(odd, other, half_sum), jnp.where(odd, half_sum...  1.58 us
    unnamed x11, local copies, waits for them, and re-layouts  1.53 us
  transfers between devices with their start and end apart: 20, of which 9 were waited for; matrix products, arithmetic and copies ran while one was open for 2% of the time, Pallas kernels for 4%

profile of v3, /device:TPU:1, one launch (start us, length us, event | category | flops | bytes accessed | tf_op | source)
XLA Modules:
  0.0 58.2 jit_solution(2407145951096290406)
XLA Ops:
  1.3 0.8 %copy.11.codes = s32[27,2]{1,0:T(8,128)S(1)} copy(s32[27,2]{0,1:T(2,128)} %param.9) | data formatting | bytes 432 | tf_op args[2]
  2.1 0.1 pad_add_fusion.info
  2.2 0.7 %copy-done.4 = s32[27,2,128]{2,1,0:T(2,128)S(1)} copy-done((s32[27,2,128]{2,1,0:T(2,128)S(1)}, s32[27,2,128]{2,1,0:T(2,128)}, u32[]{:S(2)}) %copy-start.4) | copy-done | bytes 27672
  2.9 0.6 %shard_map.102 = (f32[2,27,128]{2,1,0:T(8,128)S(1)}, bf16[144,128]{1,0:T(8,128)(2,1)S(1)}, bf16[144,128]{1,0:T(8,128)(2,1)S(1)}) custom-call(s32[4]{0:T(128)S(1)} %pad_add_fusion.info, bf16[256,128]{1,0:T(8,128)(2,1)S(1)} %copy-done.3, s32[27,2,128]{2,1,0:T(2,128)S(1)} %copy-done.4, s32[27,2]{1,0:T(8,128)S(1)} %copy.11.codes), custom_call_target="tpu_custom_call" | custom-call | flops 3000000000 | bytes 9000000 | tf_op jit(solution)/shard_map/pallas_call | solution.py:303
  3.6 0.1 collective-permute-start
  3.7 2.7 %collective-permute-start.1 = (bf16[144,128]{1,0:T(8,128)(2,1)S(1)}, bf16[144,128]{1,0:T(8,128)(2,1)S(1)}, u32[]{:S(2)}, u32[]{:S(2)}) collective-permute-start(bf16[144,128]{1,0:T(8,128)(2,1)S(1)} %get-tuple-element.40), channel_id=1, source_target_pairs={{0,8},{1,2},{2,1},{3,4},{4,3},{5,6},{6,5},{7,15},{8,0},{9,10},{10,... | collective-permute-start | bytes 110600 | tf_op jit(solution)/shard_map/ppermute | solution.py:30
  6.4 0.0 collective-permute-done.core_in
  6.4 1.8 %collective-permute-done.1.cross_in = bf16[144,128]{1,0:T(8,128)(2,1)S(1)} collective-permute-done((bf16[144,128]{1,0:T(8,128)(2,1)S(1)}, bf16[144,128]{1,0:T(8,128)(2,1)S(1)}, u32[]{:S(2)}, u32[]{:S(2)}) %collective-permute-start.1) | collective-permute-done | bytes 36896 | tf_op jit(solution)/shard_map/ppermute | solution.py:30
  8.3 2.7 %shard_map.103 = (f32[54,128]{1,0:T(8,128)S(1)}, bf16[2,128,128]{2,1,0:T(8,128)(2,1)S(1)}, bf16[256,128]{1,0:T(8,128)(2,1)S(1)}, f32[256,128]{1,0:T(8,128)S(1)},...) custom-call(s32[4]{0:T(128)S(1)} %pad_add_fusion.info, f32[2,27,128]{2,1,0:T(8,128)S(1)} %get-tuple-element.38.local, ...), custom_call_target="tpu_custom_call" | custom-call | flops 3000000000 | bytes 9000000 | tf_op jit(solution)/shard_map/pallas_call | solution.py:303
  11.0 0.5 collective-permute-start.2
  11.4 1.6 %collective-permute-start.3 = (bf16[128,128]{1,0:T(8,128)(2,1)S(1)}, bf16[128,128]{1,0:T(8,128)(2,1)S(1)}, u32[]{:S(2)}, u32[]{:S(2)}) collective-permute-start(bf16[128,128]{1,0:T(8,128)(2,1)S(1)} %get-tuple-element.44), channel_id=1, source_target_pairs={{0,8},{1,2},{2,1},{3,4},{4,3},{5,6},{6,5},{7,15},{8,0},{9,10},{10,... | collective-permute-start | bytes 98312 | tf_op jit(solution)/shard_map/ppermute | solution.py:30
  13.0 2.1 %collective-permute-done.3.cross_in = bf16[128,128]{1,0:T(8,128)(2,1)S(1)} collective-permute-done((bf16[128,128]{1,0:T(8,128)(2,1)S(1)}, bf16[128,128]{1,0:T(8,128)(2,1)S(1)}, u32[]{:S(2)}, u32[]{:S(2)}) %collective-permute-start.3) | collective-permute-done | bytes 32800 | tf_op jit(solution)/shard_map/ppermute | solution.py:30
  15.1 5.4 %shard_map.104 = (bf16[256,128]{1,0:T(8,128)(2,1)}, bf16[256,128]{1,0:T(8,128)(2,1)S(1)}, f32[256,128]{1,0:T(8,128)S(1)}, f32[4,432,128]{2,1,0:T(8,128)S(1)}, bf...) custom-call(s32[4]{0:T(128)S(1)} %pad_add_fusion.info, f32[54,128]{1,0:T(8,128)S(1)} %get-tuple-element.41.entries, ...), custom_call_target="tpu_custom_call" | custom-call | flops 5000000000 | bytes 15000000 | tf_op jit(solution)/shard_map/pallas_call | solution.py:303
  20.5 0.4 collective-permute-start.4
  20.9 1.0 %collective-permute-start.5 = (bf16[128,128]{1,0:T(8,128)(2,1)S(1)}, bf16[128,128]{1,0:T(8,128)(2,1)S(1)}, u32[]{:S(2)}, u32[]{:S(2)}) collective-permute-start(bf16[128,128]{1,0:T(8,128)(2,1)S(1)} %get-tuple-element.52), channel_id=1, source_target_pairs={{0,8},{1,2},{2,1},{3,4},{4,3},{5,6},{6,5},{7,15},{8,0},{9,10},{10,... | collective-permute-start | bytes 98312 | tf_op jit(solution)/shard_map/ppermute | solution.py:30
  21.9 0.5 collective-permute-done.4.core.core_in
  22.4 0.6 %shard_map.105 = (f32[432,128]{1,0:T(8,128)S(1)}, bf16[432,128]{1,0:T(8,128)(2,1)S(1)}, bf16[432,128]{1,0:T(8,128)(2,1)S(1)}, bf16[432,128]{1,0:T(8,128)(2,1)S(1)}) custom-call(s32[4]{0:T(128)S(1)} %pad_add_fusion.info, f32[4,432,128]{2,1,0:T(8,128)S(1)} %get-tuple-element.47.keep, bf16[1856,128]{1,0:T(8,128)(2,1)S(1)} %collective-permute-done.4.core.core_in), custom_call_target="tpu_custom_call" | custom-call | flops 1000000000 | bytes 3000000 | tf_op jit(solution)/shard_map/pallas_call | solution.py:303
  23.0 1.5 %collective-permute-done.5.cross_in = bf16[128,128]{1,0:T(8,128)(2,1)S(1)} collective-permute-done((bf16[128,128]{1,0:T(8,128)(2,1)S(1)}, bf16[128,128]{1,0:T(8,128)(2,1)S(1)}, u32[]{:S(2)}, u32[]{:S(2)}) %collective-permute-start.5) | collective-permute-done | bytes 32800 | tf_op jit(solution)/shard_map/ppermute | solution.py:30
  24.5 2.9 %shard_map.106 = (f32[256,128]{1,0:T(8,128)S(1)}, f32[4,432,128]{2,1,0:T(8,128)S(1)}, bf16[1856,128]{1,0:T(8,128)(2,1)S(1)}, bf16[128,128]{1,0:T(8,128)(2,1)S(1)}) custom-call(s32[4]{0:T(128)S(1)} %pad_add_fusion.info, f32[54,128]{1,0:T(8,128)S(1)} %get-tuple-element.41.entries, bf16[256,128]{1,0:T(8,128)(2,1)S(1)} %copy-done.3, ...), custom_call_target="tpu_custom_call" | custom-call | flops 3000000000 | bytes 9000000 | tf_op jit(solution)/shard_map/pallas_call | solution.py:303
  27.4 0.5 collective-permute-start.6
  27.9 2.7 %collective-permute-start.16 = (bf16[432,128]{1,0:T(8,128)(2,1)S(1)}, bf16[432,128]{1,0:T(8,128)(2,1)S(1)}, u32[]{:S(2)}, u32[]{:S(2)}) collective-permute-start(bf16[432,128]{1,0:T(8,128)(2,1)S(1)} %get-tuple-element.49), channel_id=1, source_target_pairs={{0,24},{8,16},{16,8},{24,0},{1,25},{9,17},{17,9},{25,1},{2,26},{10... | collective-permute-start | bytes 331784 | tf_op jit(solution)/shard_map/ppermute | solution.py:17
  30.6 0.3 collective-permute-start.14
  30.9 0.0 collective-permute-start.15
  30.9 0.6 %shard_map.107 = (f32[432,128]{1,0:T(8,128)S(1)}, bf16[432,128]{1,0:T(8,128)(2,1)S(1)}, bf16[432,128]{1,0:T(8,128)(2,1)S(1)}, bf16[432,128]{1,0:T(8,128)(2,1)S(1)}) custom-call(s32[4]{0:T(128)S(1)} %pad_add_fusion.info, f32[4,432,128]{2,1,0:T(8,128)S(1)} %get-tuple-element.57.keep, bf16[1856,128]{1,0:T(8,128)(2,1)S(1)} %collective-permute-done.6.core.core_in), custom_call_target="tpu_custom_call" | custom-call | flops 1000000000 | bytes 3000000 | tf_op jit(solution)/shard_map/pallas_call | solution.py:303
  31.5 1.3 %collective-permute-start.7 = (bf16[128,128]{1,0:T(8,128)(2,1)S(1)}, bf16[128,128]{1,0:T(8,128)(2,1)S(1)}, u32[]{:S(2)}, u32[]{:S(2)}) collective-permute-start(bf16[128,128]{1,0:T(8,128)(2,1)S(1)} %get-tuple-element.60), channel_id=1, source_target_pairs={{0,8},{1,2},{2,1},{3,4},{4,3},{5,6},{6,5},{7,15},{8,0},{9,10},{10,... | collective-permute-start | bytes 98312 | tf_op jit(solution)/shard_map/ppermute | solution.py:30
  32.8 2.2 %collective-permute-start.10 = (bf16[432,128]{1,0:T(8,128)(2,1)S(1)}, bf16[432,128]{1,0:T(8,128)(2,1)S(1)}, u32[]{:S(2)}, u32[]{:S(2)}) collective-permute-start(bf16[432,128]{1,0:T(8,128)(2,1)S(1)} %get-tuple-element.58), channel_id=1, source_target_pairs={{0,24},{8,16},{16,8},{24,0},{1,25},{9,17},{17,9},{25,1},{2,26},{10... | collective-permute-start | bytes 331784 | tf_op jit(solution)/shard_map/ppermute | solution.py:17
  35.0 0.0 collective-permute-done.16
  35.0 0.2 collective-permute-start.8
  35.2 0.0 collective-permute-done.7.cross_in
  35.2 1.4 %collective-permute-start.9 = (bf16[432,128]{1,0:T(8,128)(2,1)S(1)}, bf16[432,128]{1,0:T(8,128)(2,1)S(1)}, u32[]{:S(2)}, u32[]{:S(2)}) collective-permute-start(bf16[432,128]{1,0:T(8,128)(2,1)S(1)} %get-tuple-element.63), channel_id=1, source_target_pairs={{0,16},{8,24},{16,0},{24,8},{1,17},{9,25},{17,1},{25,9},{2,18},{10... | collective-permute-start | bytes 331784 | tf_op jit(solution)/shard_map/ppermute | solution.py:17
  36.7 0.0 collective-permute-done.15
  36.7 0.1 add_convert_fusion.1
  36.7 0.6 %collective-permute-start.17 = (bf16[432,128]{1,0:T(8,128)(2,1)S(1)}, bf16[432,128]{1,0:T(8,128)(2,1)S(1)}, u32[]{:S(2)}, u32[]{:S(2)}) collective-permute-start(bf16[432,128]{1,0:T(8,128)(2,1)S(1)} %add_convert_fusion.1), channel_id=1, source_target_pairs={{0,2},{1,3},{2,0},{3,1},{4,6},{5,7},{6,4},{7,5},{8,10},{9,11},{10,... | collective-permute-start | bytes 331784 | tf_op jit(solution)/shard_map/ppermute | solution.py:17
  37.4 1.2 %shard_map.108 = bf16[256,128]{1,0:T(8,128)(2,1)} custom-call(s32[4]{0:T(128)S(1)} %pad_add_fusion.info, f32[256,128]{1,0:T(8,128)S(1)} %get-tuple-element.55.own, bf16[1856,128]{1,0:T(8,128)(2,1)S(1)} %collective-permute-done.6.core.core_in, bf16[128,128]{1,0:T(8,128)(2,1)S(1)} %collective-permute-done.7.cross_in), custom_call_target="tpu_custom_call" | custom-call | flops 1000000000 | bytes 3000000 | tf_op jit(solution)/shard_map/pallas_call | solution.py:303
  38.6 1.9 %collective-permute-done.8 = bf16[432,128]{1,0:T(8,128)(2,1)S(1)} collective-permute-done((bf16[432,128]{1,0:T(8,128)(2,1)S(1)}, bf16[432,128]{1,0:T(8,128)(2,1)S(1)}, u32[]{:S(2)}, u32[]{:S(2)}) %collective-permute-start.8) | collective-permute-done | bytes 110624 | tf_op jit(solution)/shard_map/ppermute | solution.py:17
  40.5 0.1 add_convert_fusion.3
  40.6 2.0 %collective-permute-start.11 = (bf16[432,128]{1,0:T(8,128)(2,1)S(1)}, bf16[432,128]{1,0:T(8,128)(2,1)S(1)}, u32[]{:S(2)}, u32[]{:S(2)}) collective-permute-start(bf16[432,128]{1,0:T(8,128)(2,1)S(1)} %add_convert_fusion.3), channel_id=1, source_target_pairs={{0,2},{1,3},{2,0},{3,1},{4,6},{5,7},{6,4},{7,5},{8,10},{9,11},{10,... | collective-permute-start | bytes 331784 | tf_op jit(solution)/shard_map/ppermute | solution.py:17
  42.6 1.3 %collective-permute-start.18 = (bf16[432,128]{1,0:T(8,128)(2,1)S(1)}, bf16[432,128]{1,0:T(8,128)(2,1)S(1)}, u32[]{:S(2)}, u32[]{:S(2)}) collective-permute-start(bf16[432,128]{1,0:T(8,128)(2,1)S(1)} %add_convert_fusion), channel_id=1, source_target_pairs={{0,4},{1,5},{2,6},{3,7},{4,0},{5,1},{6,2},{7,3},{8,12},{9,13},{10,... | collective-permute-start | bytes 331784 | tf_op jit(solution)/shard_map/ppermute | solution.py:17
  43.9 0.8 %collective-permute-done.11 = bf16[432,128]{1,0:T(8,128)(2,1)S(1)} collective-permute-done((bf16[432,128]{1,0:T(8,128)(2,1)S(1)}, bf16[432,128]{1,0:T(8,128)(2,1)S(1)}, u32[]{:S(2)}, u32[]{:S(2)}) %collective-permute-start.11) | collective-permute-done | bytes 110624 | tf_op jit(solution)/shard_map/ppermute | solution.py:17
  44.8 2.6 %collective-permute-start.12 = (bf16[432,128]{1,0:T(8,128)(2,1)S(1)}, bf16[432,128]{1,0:T(8,128)(2,1)S(1)}, u32[]{:S(2)}, u32[]{:S(2)}) collective-permute-start(bf16[432,128]{1,0:T(8,128)(2,1)S(1)} %add_convert_fusion.2), channel_id=1, source_target_pairs={{0,4},{1,5},{2,6},{3,7},{4,0},{5,1},{6,2},{7,3},{8,12},{9,13},{10,... | collective-permute-start | bytes 331784 | tf_op jit(solution)/shard_map/ppermute | solution.py:17
  47.4 0.8 %collective-permute-done.18 = bf16[432,128]{1,0:T(8,128)(2,1)S(1)} collective-permute-done((bf16[432,128]{1,0:T(8,128)(2,1)S(1)}, bf16[432,128]{1,0:T(8,128)(2,1)S(1)}, u32[]{:S(2)}, u32[]{:S(2)}) %collective-permute-start.18) | collective-permute-done | bytes 110624 | tf_op jit(solution)/shard_map/ppermute | solution.py:17
  48.3 6.4 %collective-permute-start.19 = (f32[432,128]{1,0:T(8,128)S(1)}, f32[432,128]{1,0:T(8,128)S(1)}, u32[]{:S(2)}, u32[]{:S(2)}) collective-permute-start(f32[432,128]{1,0:T(8,128)S(1)} %add_multiply_fusion), channel_id=1, source_target_pairs={{0,1},{1,0},{2,3},{3,2},{4,5},{5,4},{6,7},{7,6},{8,9},{9,8},{10,11... | collective-permute-start | bytes 663560 | tf_op jit(solution)/shard_map/ppermute | solution.py:17
  54.7 0.3 collective-permute-done.12
  55.0 1.3 %collective-permute-start.13 = (f32[432,128]{1,0:T(8,128)S(1)}, f32[432,128]{1,0:T(8,128)S(1)}, u32[]{:S(2)}, u32[]{:S(2)}) collective-permute-start(f32[432,128]{1,0:T(8,128)S(1)} %add_multiply_fusion.1), channel_id=1, source_target_pairs={{0,1},{1,0},{2,3},{3,2},{4,5},{5,4},{6,7},{7,6},{8,9},{9,8},{10,11... | collective-permute-start | bytes 663560 | tf_op jit(solution)/shard_map/ppermute | solution.py:17
  56.3 0.1 broadcast_select_fusion.1
  56.4 0.8 %pad_maximum_fusion.1 = f32[864,128]{1,0:T(8,128)} fusion(f32[432,128]{1,0:T(8,128)S(1)} %get-tuple-element.73, f32[432,128]{1,0:T(8,128)S(1)} %get-tuple-element.72), kind=kLoop, calls=%fused_computation.1 | loop fusion | flops 110592 | bytes 884736 | tf_op jit(solution)/shard_map/concatenate | solution.py:400
  57.1 0.3 collective-permute-done.13
  57.4 0.8 %pad_maximum_fusion = f32[864,128]{1,0:T(8,128)} fusion(f32[432,128]{1,0:T(8,128)S(1)} %get-tuple-element.75, f32[432,128]{1,0:T(8,128)S(1)} %get-tuple-element.74), kind=kLoop, calls=%fused_computation | loop fusion | flops 110592 | bytes 884736 | tf_op jit(solution)/shard_map/concatenate | solution.py:400
  (21 shorter events, 0.2 us)
Async XLA Ops:
  0.6 1.6 %copy-start.3 = (bf16[256,128]{1,0:T(8,128)(2,1)S(1)}, bf16[256,128]{1,0:T(8,128)(2,1)}, u32[]{:S(2)}) copy-start(bf16[256,128]{1,0:T(8,128)(2,1)} %features.7) | copy-start | bytes 196612
  2.2 0.7 %copy-start.4 = (s32[27,2,128]{2,1,0:T(2,128)S(1)}, s32[27,2,128]{2,1,0:T(2,128)}, u32[]{:S(2)}) copy-start(s32[27,2,128]{2,1,0:T(2,128)} %source_rows.1) | copy-start | bytes 82948
  2.9 5.3 %copy-start.1 = (bf16[27,128,128]{2,1,0:T(8,128)(2,1)S(1)}, bf16[27,128,128]{2,1,0:T(8,128)(2,1)}, u32[]{:S(2)}) copy-start(bf16[27,128,128]{2,1,0:T(8,128)(2,1)} %param.11) | copy-start | bytes 2654212
  3.6 2.8 %collective-permute-start = (bf16[144,128]{1,0:T(8,128)(2,1)S(1)}, bf16[144,128]{1,0:T(8,128)(2,1)S(1)}, u32[]{:S(2)}, u32[]{:S(2)}) collective-permute-start(bf16[144,128]{1,0:T(8,128)(2,1)S(1)} %get-tuple-element.39), channel_id=1, source_target_pairs={{0,1},{1,0},{2,3},{3,2},{4,5},{5,4},{6,7},{7,6},{8,9},{9,8},{10,11... | collective-permute-start | bytes 110600 | tf_op jit(solution)/shard_map/ppermute | solution.py:17
  3.7 4.6 %collective-permute-start.1 = (bf16[144,128]{1,0:T(8,128)(2,1)S(1)}, bf16[144,128]{1,0:T(8,128)(2,1)S(1)}, u32[]{:S(2)}, u32[]{:S(2)}) collective-permute-start(bf16[144,128]{1,0:T(8,128)(2,1)S(1)} %get-tuple-element.40), channel_id=1, source_target_pairs={{0,8},{1,2},{2,1},{3,4},{4,3},{5,6},{6,5},{7,15},{8,0},{9,10},{10,... | collective-permute-start | bytes 110600 | tf_op jit(solution)/shard_map/ppermute | solution.py:30
  8.3 6.8 %copy-start = (bf16[27,128,128]{2,1,0:T(8,128)(2,1)S(1)}, bf16[27,128,128]{2,1,0:T(8,128)(2,1)}, u32[]{:S(2)}) copy-start(bf16[27,128,128]{2,1,0:T(8,128)(2,1)} %param.12) | copy-start | bytes 2654212
  8.3 6.8 %copy-start.2 = (bf16[256,128]{1,0:T(8,128)(2,1)S(1)}, bf16[256,128]{1,0:T(8,128)(2,1)}, u32[]{:S(2)}) copy-start(bf16[256,128]{1,0:T(8,128)(2,1)} %cotangent.1) | copy-start | bytes 196612
  11.0 2.0 %collective-permute-start.2 = (bf16[128,128]{1,0:T(8,128)(2,1)S(1)}, bf16[128,128]{1,0:T(8,128)(2,1)S(1)}, u32[]{:S(2)}, u32[]{:S(2)}) collective-permute-start(bf16[128,128]{1,0:T(8,128)(2,1)S(1)} %get-tuple-element.43), channel_id=1, source_target_pairs={{0,1},{1,0},{2,3},{3,2},{4,5},{5,4},{6,7},{7,6},{8,9},{9,8},{10,11... | collective-permute-start | bytes 98312 | tf_op jit(solution)/shard_map/ppermute | solution.py:17
  11.4 3.6 %collective-permute-start.3 = (bf16[128,128]{1,0:T(8,128)(2,1)S(1)}, bf16[128,128]{1,0:T(8,128)(2,1)S(1)}, u32[]{:S(2)}, u32[]{:S(2)}) collective-permute-start(bf16[128,128]{1,0:T(8,128)(2,1)S(1)} %get-tuple-element.44), channel_id=1, source_target_pairs={{0,8},{1,2},{2,1},{3,4},{4,3},{5,6},{6,5},{7,15},{8,0},{9,10},{10,... | collective-permute-start | bytes 98312 | tf_op jit(solution)/shard_map/ppermute | solution.py:30
  20.5 1.9 %collective-permute-start.4 = (bf16[1856,128]{1,0:T(8,128)(2,1)S(1)}, bf16[1856,128]{1,0:T(8,128)(2,1)S(1)}, u32[]{:S(2)}, u32[]{:S(2)}) collective-permute-start(bf16[1856,128]{1,0:T(8,128)(2,1)S(1)} %get-tuple-element.48), channel_id=1, source_target_pairs={{0,1},{1,0},{2,3},{3,2},{4,5},{5,4},{6,7},{7,6},{8,9},{9,8},{10,11... | collective-permute-start | bytes 1425416 | tf_op jit(solution)/shard_map/ppermute | solution.py:17
  20.9 3.6 %collective-permute-start.5 = (bf16[128,128]{1,0:T(8,128)(2,1)S(1)}, bf16[128,128]{1,0:T(8,128)(2,1)S(1)}, u32[]{:S(2)}, u32[]{:S(2)}) collective-permute-start(bf16[128,128]{1,0:T(8,128)(2,1)S(1)} %get-tuple-element.52), channel_id=1, source_target_pairs={{0,8},{1,2},{2,1},{3,4},{4,3},{5,6},{6,5},{7,15},{8,0},{9,10},{10,... | collective-permute-start | bytes 98312 | tf_op jit(solution)/shard_map/ppermute | solution.py:30
  27.4 3.4 %collective-permute-start.6 = (bf16[1856,128]{1,0:T(8,128)(2,1)S(1)}, bf16[1856,128]{1,0:T(8,128)(2,1)S(1)}, u32[]{:S(2)}, u32[]{:S(2)}) collective-permute-start(bf16[1856,128]{1,0:T(8,128)(2,1)S(1)} %get-tuple-element.56), channel_id=1, source_target_pairs={{0,1},{1,0},{2,3},{3,2},{4,5},{5,4},{6,7},{7,6},{8,9},{9,8},{10,11... | collective-permute-start | bytes 1425416 | tf_op jit(solution)/shard_map/ppermute | solution.py:17
  27.9 7.1 %collective-permute-start.16 = (bf16[432,128]{1,0:T(8,128)(2,1)S(1)}, bf16[432,128]{1,0:T(8,128)(2,1)S(1)}, u32[]{:S(2)}, u32[]{:S(2)}) collective-permute-start(bf16[432,128]{1,0:T(8,128)(2,1)S(1)} %get-tuple-element.49), channel_id=1, source_target_pairs={{0,24},{8,16},{16,8},{24,0},{1,25},{9,17},{17,9},{25,1},{2,26},{10... | collective-permute-start | bytes 331784 | tf_op jit(solution)/shard_map/ppermute | solution.py:17
  30.6 6.1 %collective-permute-start.14 = (bf16[432,128]{1,0:T(8,128)(2,1)S(1)}, bf16[432,128]{1,0:T(8,128)(2,1)S(1)}, u32[]{:S(2)}, u32[]{:S(2)}) collective-permute-start(bf16[432,128]{1,0:T(8,128)(2,1)S(1)} %get-tuple-element.66), channel_id=1, source_target_pairs={{0,8},{8,0},{16,24},{24,16},{1,9},{9,1},{17,25},{25,17},{2,10},{10... | collective-permute-start | bytes 331784 | tf_op jit(solution)/shard_map/ppermute | solution.py:17
  30.9 5.8 %collective-permute-start.15 = (bf16[432,128]{1,0:T(8,128)(2,1)S(1)}, bf16[432,128]{1,0:T(8,128)(2,1)S(1)}, u32[]{:S(2)}, u32[]{:S(2)}) collective-permute-start(bf16[432,128]{1,0:T(8,128)(2,1)S(1)} %get-tuple-element.68), channel_id=1, source_target_pairs={{0,16},{8,24},{16,0},{24,8},{1,17},{9,25},{17,1},{25,9},{2,18},{10... | collective-permute-start | bytes 331784 | tf_op jit(solution)/shard_map/ppermute | solution.py:17
  31.5 3.7 %collective-permute-start.7 = (bf16[128,128]{1,0:T(8,128)(2,1)S(1)}, bf16[128,128]{1,0:T(8,128)(2,1)S(1)}, u32[]{:S(2)}, u32[]{:S(2)}) collective-permute-start(bf16[128,128]{1,0:T(8,128)(2,1)S(1)} %get-tuple-element.60), channel_id=1, source_target_pairs={{0,8},{1,2},{2,1},{3,4},{4,3},{5,6},{6,5},{7,15},{8,0},{9,10},{10,... | collective-permute-start | bytes 98312 | tf_op jit(solution)/shard_map/ppermute | solution.py:30
  32.8 7.7 %collective-permute-start.10 = (bf16[432,128]{1,0:T(8,128)(2,1)S(1)}, bf16[432,128]{1,0:T(8,128)(2,1)S(1)}, u32[]{:S(2)}, u32[]{:S(2)}) collective-permute-start(bf16[432,128]{1,0:T(8,128)(2,1)S(1)} %get-tuple-element.58), channel_id=1, source_target_pairs={{0,24},{8,16},{16,8},{24,0},{1,25},{9,17},{17,9},{25,1},{2,26},{10... | collective-permute-start | bytes 331784 | tf_op jit(solution)/shard_map/ppermute | solution.py:17
  35.0 5.5 %collective-permute-start.8 = (bf16[432,128]{1,0:T(8,128)(2,1)S(1)}, bf16[432,128]{1,0:T(8,128)(2,1)S(1)}, u32[]{:S(2)}, u32[]{:S(2)}) collective-permute-start(bf16[432,128]{1,0:T(8,128)(2,1)S(1)} %get-tuple-element.62), channel_id=1, source_target_pairs={{0,8},{8,0},{16,24},{24,16},{1,9},{9,1},{17,25},{25,17},{2,10},{10... | collective-permute-start | bytes 331784 | tf_op jit(solution)/shard_map/ppermute | solution.py:17
  35.2 5.3 %collective-permute-start.9 = (bf16[432,128]{1,0:T(8,128)(2,1)S(1)}, bf16[432,128]{1,0:T(8,128)(2,1)S(1)}, u32[]{:S(2)}, u32[]{:S(2)}) collective-permute-start(bf16[432,128]{1,0:T(8,128)(2,1)S(1)} %get-tuple-element.63), channel_id=1, source_target_pairs={{0,16},{8,24},{16,0},{24,8},{1,17},{9,25},{17,1},{25,9},{2,18},{10... | collective-permute-start | bytes 331784 | tf_op jit(solution)/shard_map/ppermute | solution.py:17
  36.7 5.9 %collective-permute-start.17 = (bf16[432,128]{1,0:T(8,128)(2,1)S(1)}, bf16[432,128]{1,0:T(8,128)(2,1)S(1)}, u32[]{:S(2)}, u32[]{:S(2)}) collective-permute-start(bf16[432,128]{1,0:T(8,128)(2,1)S(1)} %add_convert_fusion.1), channel_id=1, source_target_pairs={{0,2},{1,3},{2,0},{3,1},{4,6},{5,7},{6,4},{7,5},{8,10},{9,11},{10,... | collective-permute-start | bytes 331784 | tf_op jit(solution)/shard_map/ppermute | solution.py:17
  40.6 4.2 %collective-permute-start.11 = (bf16[432,128]{1,0:T(8,128)(2,1)S(1)}, bf16[432,128]{1,0:T(8,128)(2,1)S(1)}, u32[]{:S(2)}, u32[]{:S(2)}) collective-permute-start(bf16[432,128]{1,0:T(8,128)(2,1)S(1)} %add_convert_fusion.3), channel_id=1, source_target_pairs={{0,2},{1,3},{2,0},{3,1},{4,6},{5,7},{6,4},{7,5},{8,10},{9,11},{10,... | collective-permute-start | bytes 331784 | tf_op jit(solution)/shard_map/ppermute | solution.py:17
  42.6 5.6 %collective-permute-start.18 = (bf16[432,128]{1,0:T(8,128)(2,1)S(1)}, bf16[432,128]{1,0:T(8,128)(2,1)S(1)}, u32[]{:S(2)}, u32[]{:S(2)}) collective-permute-start(bf16[432,128]{1,0:T(8,128)(2,1)S(1)} %add_convert_fusion), channel_id=1, source_target_pairs={{0,4},{1,5},{2,6},{3,7},{4,0},{5,1},{6,2},{7,3},{8,12},{9,13},{10,... | collective-permute-start | bytes 331784 | tf_op jit(solution)/shard_map/ppermute | solution.py:17
  44.8 10.2 %collective-permute-start.12 = (bf16[432,128]{1,0:T(8,128)(2,1)S(1)}, bf16[432,128]{1,0:T(8,128)(2,1)S(1)}, u32[]{:S(2)}, u32[]{:S(2)}) collective-permute-start(bf16[432,128]{1,0:T(8,128)(2,1)S(1)} %add_convert_fusion.2), channel_id=1, source_target_pairs={{0,4},{1,5},{2,6},{3,7},{4,0},{5,1},{6,2},{7,3},{8,12},{9,13},{10,... | collective-permute-start | bytes 331784 | tf_op jit(solution)/shard_map/ppermute | solution.py:17
  48.3 8.0 %collective-permute-start.19 = (f32[432,128]{1,0:T(8,128)S(1)}, f32[432,128]{1,0:T(8,128)S(1)}, u32[]{:S(2)}, u32[]{:S(2)}) collective-permute-start(f32[432,128]{1,0:T(8,128)S(1)} %add_multiply_fusion), channel_id=1, source_target_pairs={{0,1},{1,0},{2,3},{3,2},{4,5},{5,4},{6,7},{7,6},{8,9},{9,8},{10,11... | collective-permute-start | bytes 663560 | tf_op jit(solution)/shard_map/ppermute | solution.py:17
  55.0 2.4 %collective-permute-start.13 = (f32[432,128]{1,0:T(8,128)S(1)}, f32[432,128]{1,0:T(8,128)S(1)}, u32[]{:S(2)}, u32[]{:S(2)}) collective-permute-start(f32[432,128]{1,0:T(8,128)S(1)} %add_multiply_fusion.1), channel_id=1, source_target_pairs={{0,1},{1,0},{2,3},{3,2},{4,5},{5,4},{6,7},{7,6},{8,9},{9,8},{10,11... | collective-permute-start | bytes 663560 | tf_op jit(solution)/shard_map/ppermute | solution.py:17

commit v4 on v3

v4 whole, which is shorter than its diff:
```python
import jax
import jax.numpy as jnp
from jax import lax
from jax.experimental import pallas as pl
from jax.experimental.pallas import tpu as pltpu
from jax.sharding import PartitionSpec as P

F32 = jnp.float32
BF16 = jnp.bfloat16
KINDS = 3
LIMIT = 28 * 1024 * 1024
NT = (((1,), (1,)), ((), ()))


def swapped(value, axis, bits):
    count = lax.axis_size(axis)
    return lax.ppermute(value, axis, [(i, i ^ bits) for i in range(count) if i ^ bits < count])


def crossed(value):
    groups, count = lax.axis_size("grp"), lax.axis_size("tile")
    pairs = []
    for i in range(groups * count):
        group, tile = divmod(i, count)
        other = ((tile + 1) ^ 1) - 1
        if 0 <= other < count:
            pairs.append((i, group * count + other))
        elif (group ^ 1) < groups:
            pairs.append((i, (group ^ 1) * count + tile))
    return lax.ppermute(value, ("grp", "tile"), pairs)


def sigmoid_terms(values):
    sigma = jax.nn.sigmoid(values)
    return values * sigma, sigma * (1.0 + values * (1.0 - sigma))


def place():
    tile = lax.axis_index("tile")
    return tile % 2 == 1, tile > 0, tile < lax.axis_size("tile") - 1


def halo_sides(odd, core, cross):
    return jnp.where(odd, cross, core), jnp.where(odd, core, cross)


def exchange_sides(odd, to_next, to_prev):
    return jnp.where(odd, to_prev, to_next), jnp.where(odd, to_next, to_prev)


def row_mask(rows, blk, count):
    block = lax.broadcasted_iota(jnp.int32, (rows, 1), 0) // blk
    return (block < count).astype(F32)


def of_kind(values, kind):
    return [values[i : i + 1] for i in range(kind, values.shape[0], KINDS)]


def stacked(rows, blk, fill):
    spare = -len(rows) % 8
    if spare:
        rows = rows + [jnp.full((spare, blk), fill, F32)]
    return jnp.concatenate(rows, axis=0)


def pack_kernel(count_ref, features, source_rows, codes, near, core_out, cross_out):
    offsets, _, blk = source_rows.shape
    per = offsets // KINDS
    count = count_ref[0]
    both = count == 2
    odd, has_prev, has_next = place()
    diagonal = lax.broadcasted_iota(jnp.int32, (offsets, offsets), 0) == lax.broadcasted_iota(
        jnp.int32, (offsets, offsets), 1
    )
    coded = []
    for j in range(2):
        rows = source_rows[:, j, :]
        block = lax.rem(codes[j : j + 1, :], 2).astype(F32)
        block = jnp.sum(jnp.where(diagonal, block, 0.0), axis=1, keepdims=True)
        live = (rows >= 0) & (count > j)
        coded.append(jnp.where(live, rows.astype(F32) + blk * block, -1.0))
    first, second = coded
    inner = jnp.where(both, first, -1.0)
    rows = of_kind(second, 0) + of_kind(first, 1) + of_kind(second, 1) + of_kind(inner, 2)
    near[...] = stacked(rows, blk, -1.0)
    to_prev = of_kind(jnp.where(has_prev, first, -1.0), 0)
    last = jnp.where(both, second, first)
    to_next = of_kind(jnp.where(has_next, last, -1.0), 2)
    pad = core_out.shape[0] - blk - per
    fill = [jnp.full((pad, blk), -1.0, F32)]
    to_prev = jnp.concatenate(to_prev + fill, axis=0).astype(BF16)
    to_next = jnp.concatenate(to_next + fill, axis=0).astype(BF16)
    front, back = features[:blk, :], features[blk:, :]
    tail = jnp.where(both, back, front)
    core_out[:blk, :], cross_out[:blk, :] = exchange_sides(odd, tail, front)
    core_out[blk:, :], cross_out[blk:, :] = exchange_sides(odd, to_next, to_prev)


def by_targets(columns, at, blk):
    lane = lax.broadcasted_iota(jnp.int32, (blk, blk), 1).astype(F32).astype(BF16)
    one, zero = jnp.ones((blk, blk), BF16), jnp.zeros((blk, blk), BF16)
    entry = jnp.broadcast_to(columns[:, at : at + 1], (blk, blk)).astype(BF16)
    halves = [jnp.where(entry == lane + b * blk, one, zero) for b in range(2)]
    return jnp.concatenate(halves, axis=0)


def by_sources(entries, at, blk):
    sub = lax.broadcasted_iota(jnp.int32, (blk, blk), 0).astype(F32).astype(BF16)
    one, zero = jnp.ones((blk, blk), BF16), jnp.zeros((blk, blk), BF16)
    entry = jnp.broadcast_to(entries[at : at + 1, :], (blk, blk)).astype(BF16)
    halves = [jnp.where(entry == sub + b * blk, one, zero) for b in range(2)]
    return jnp.concatenate(halves, axis=1)


def weights_of(weights, kind, per, axis):
    channels = weights.shape[1]
    parts = []
    for i in range(per):
        at = (i * KINDS + kind) * channels
        parts.append(weights[at : at + channels, :])
    return jnp.concatenate(parts, axis=axis)


def middle_part(pairs, source, weights, picked):
    per, channels = pairs.shape[0], weights.shape[1]
    for i in range(per):
        got = jnp.dot(pairs[i], source, preferred_element_type=F32)
        picked[:, i * channels : (i + 1) * channels] = got.astype(BF16)
    wide = weights_of(weights, 1, per, 0)
    return jnp.dot(picked[...], wide, preferred_element_type=F32)


def outer_part(far, singles, sources, weights, picked):
    per, channels = singles.shape[0] // 2, weights.shape[1]
    for side, source in enumerate(sources):
        for i in range(per):
            at = side * per + i
            select = jnp.concatenate([far[at], singles[at]], axis=1)
            got = jnp.dot(select, source, preferred_element_type=F32)
            picked[:, at * channels : (at + 1) * channels] = got.astype(BF16)
    wide = jnp.concatenate([weights_of(weights, kind, per, 0) for kind in (0, 2)], axis=0)
    return jnp.dot(picked[...], wide, preferred_element_type=F32)


def local_kernel(
    near, features, weights, pairs, singles, pairs_turned, singles_turned, part, picked
):
    blk = near.shape[1]
    per = pairs.shape[0]
    columns = near[...].T
    for i in range(per):
        at, to = per + i, 2 * per + i
        pairs[i, :, :blk] = by_targets(columns, at, blk)
        pairs[i, :, blk:] = by_targets(columns, to, blk)
        pairs_turned[i, :blk, :] = by_sources(near, at, blk)
        pairs_turned[i, blk:, :] = by_sources(near, to, blk)
    part[...] = middle_part(pairs, features[...], weights, picked)
    for i in range(per):
        for side, at in ((0, i), (1, 3 * per + i)):
            singles[side * per + i] = by_targets(columns, at, blk)
            singles_turned[side * per + i] = by_sources(near, at, blk)


def pull_back(far_turned, pairs_turned, singles_turned, grads, weights, sources, pulled, wgrad):
    per, channels = pairs_turned.shape[0], grads.shape[1]
    sums = []
    for kind in range(KINDS):
        base = kind * per * channels
        for i in range(per):
            if kind == 1:
                select = pairs_turned[i]
            else:
                side = (kind // 2) * per + i
                select = jnp.concatenate([far_turned[side], singles_turned[side]], axis=0)
            got = jnp.dot(select, grads, preferred_element_type=F32)
            at = base + i * channels
            pulled[:, at : at + channels] = got.astype(BF16)
        held = pulled[:, base : base + per * channels]
        wide = weights_of(weights, kind, per, 1)
        sums.append(lax.dot_general(held, wide, NT, preferred_element_type=F32))
        terms = jnp.dot(sources[kind].T, held, preferred_element_type=F32)
        for i in range(per):
            at = (i * KINDS + kind) * channels
            wgrad[at : at + channels, :] = terms[:, i * channels : (i + 1) * channels]
    return sums


def split_sums(sums, both, blk):
    low, mid, high = sums
    first = mid[:blk] + jnp.where(both, high[blk:], 0.0)
    second = mid[blk:] + low[blk:]
    return jnp.concatenate([first, second], axis=0), low[:blk], high[:blk]


def halves_out(odd, wgrad, keep, send, at):
    shards, slot, _ = keep.shape
    rows = wgrad.shape[0] // shards // 2
    bit = odd.astype(jnp.int32)
    for s in range(shards):
        mine = pl.ds((s * 2 + bit) * rows, rows)
        other = pl.ds((s * 2 + 1 - bit) * rows, rows)
        keep[s, :rows, :] = wgrad[mine, :]
        start = at + s * slot
        send[start : start + rows, :] = wgrad[other, :].astype(BF16)


def first_kernel(
    count_ref, features, core_in, cross_in, singles, part, weights,
    entries, far, halo, hidden, slope, core_out, cross_out, picked,
):
    blk = features.shape[0] // 2
    per = singles.shape[0] // 2
    count = count_ref[0]
    odd, _, _ = place()
    from_next, from_prev = halo_sides(odd, core_in[...].astype(F32), cross_in[...].astype(F32))
    table = stacked([from_next[blk : blk + per], from_prev[blk : blk + per]], blk, -1.0)
    entries[...] = table
    columns = table.T
    for at in range(2 * per):
        far[at] = by_targets(columns, at, blk)
    after, before = from_next[:blk].astype(BF16), from_prev[:blk].astype(BF16)
    halo[0] = after
    halo[1] = before
    front, back = features[:blk, :], features[blk:, :]
    sources = [
        jnp.concatenate([after, back], axis=0),
        jnp.concatenate([before, front], axis=0),
    ]
    pre = part[...] + outer_part(far, singles, sources, weights, picked)
    mask = row_mask(2 * blk, blk, count)
    value, grad = sigmoid_terms(pre)
    field = (value * mask).astype(BF16)
    hidden[...] = field
    slope[...] = grad * mask
    head = field[:blk]
    tail = jnp.where(count == 2, field[blk:], head)
    core_out[...], cross_out[...] = exchange_sides(odd, tail, head)


def middle_kernel(hidden, pairs, entries, weights, part, far_turned, picked):
    part[...] = middle_part(pairs, hidden[...], weights, picked)
    for at in range(far_turned.shape[0]):
        far_turned[at] = by_sources(entries, at, entries.shape[1])


def second_kernel(
    count_ref, features, hidden, core_in, cross_in, far, singles, part, weights, cotangent,
    far_turned, pairs_turned, singles_turned,
    result, grads_out, own_out, keep, core_out, cross_out, picked, pulled, wgrad,
):
    blk = features.shape[0] // 2
    count = count_ref[0]
    both = count == 2
    odd, _, _ = place()
    after, before = halo_sides(odd, core_in[...], cross_in[...])
    front, back = hidden[:blk, :], hidden[blk:, :]
    low = jnp.concatenate([after, back], axis=0)
    high = jnp.concatenate([before, front], axis=0)
    total = part[...] + outer_part(far, singles, [low, high], weights, picked)
    total = total + features[...].astype(F32)
    mask = row_mask(2 * blk, blk, count)
    value, grad = sigmoid_terms(total)
    result[...] = (value * mask).astype(BF16)
    grads = (cotangent[...].astype(F32) * grad * mask).astype(BF16)
    grads_out[...] = grads
    sources = [low, hidden[...], high]
    sums = pull_back(
        far_turned, pairs_turned, singles_turned, grads, weights, sources, pulled, wgrad
    )
    own, to_next, to_prev = split_sums(sums, both, blk)
    own_out[...] = own
    core, cross = exchange_sides(odd, to_next, to_prev)
    core_out[:blk, :] = core.astype(BF16)
    cross_out[...] = cross.astype(BF16)
    halves_out(odd, wgrad, keep, core_out, blk)


def joined(own, odd, both, core_in, cross_in, blk):
    from_next, from_prev = halo_sides(odd, core_in, cross_in)
    first = own[:blk] + from_prev + jnp.where(both, 0.0, from_next)
    second = own[blk:] + jnp.where(both, from_next, 0.0)
    return jnp.concatenate([first, second], axis=0)


def third_kernel(
    count_ref, features, halo, own, core_in, cross_in, slope, grads_in, weights,
    far_turned, pairs_turned, singles_turned,
    own_out, keep, core_out, cross_out, pulled, wgrad,
):
    blk = features.shape[0] // 2
    both = count_ref[0] == 2
    odd, _, _ = place()
    core, cross = core_in[:blk, :].astype(F32), cross_in[...].astype(F32)
    summed = joined(own[...], odd, both, core, cross, blk)
    grads = (summed * slope[...]).astype(BF16)
    sources = [
        jnp.concatenate([halo[0], features[blk:, :]], axis=0),
        features[...],
        jnp.concatenate([halo[1], features[:blk, :]], axis=0),
    ]
    sums = pull_back(
        far_turned, pairs_turned, singles_turned, grads, weights, sources, pulled, wgrad
    )
    own_sum, to_next, to_prev = split_sums(sums, both, blk)
    own_out[...] = own_sum + grads_in[...].astype(F32)
    core, cross = exchange_sides(odd, to_next, to_prev)
    core_out[:blk, :] = core.astype(BF16)
    cross_out[...] = cross.astype(BF16)
    halves_out(odd, wgrad, keep, core_out, blk)


def last_kernel(count_ref, own, core_in, cross_in, input_grad):
    blk = own.shape[0] // 2
    both = count_ref[0] == 2
    odd, _, _ = place()
    core, cross = core_in[:blk, :].astype(F32), cross_in[...].astype(F32)
    input_grad[...] = joined(own[...], odd, both, core, cross, blk).astype(BF16)


def shards_kernel(keep, core, own, *sends):
    shards, slot, _ = keep.shape
    blk = core.shape[0] - shards * slot
    me = lax.axis_index("grp")
    for d in range(shards):
        to = me ^ d
        at = pl.ds(pl.multiple_of(blk + to * slot, 16), slot)
        value = keep[to] + core[at, :].astype(F32)
        if d == 0:
            own[...] = value
        else:
            sends[d - 1][...] = value.astype(BF16)


def after(first, later):
    return lax.optimization_barrier((first, later))[1]


def added(value, others):
    value = value.astype(F32)
    for other in others:
        value = value + other.astype(F32)
    return value


def call(kernel, outs, *args, scratch=(), micros=1):
    vmem, smem = pl.BlockSpec(memory_space=pltpu.VMEM), pl.BlockSpec(memory_space=pltpu.SMEM)
    return pl.pallas_call(
        kernel,
        out_shape=[jax.ShapeDtypeStruct(shape, kind) for shape, kind in outs],
        in_specs=[smem if arg.shape == (1,) else vmem for arg in args],
        out_specs=[vmem] * len(outs),
        scratch_shapes=[pltpu.VMEM(shape, kind) for shape, kind in scratch],
        compiler_params=pltpu.CompilerParams(vmem_limit_bytes=LIMIT),
        cost_estimate=pl.CostEstimate(
            flops=micros * 10**9, bytes_accessed=micros * 3 * 10**6, transcendentals=0
        ),
    )(*args)


def on_device(
    features, source_rows, target_codes, block_count, weight_one, weight_two, out_cotangent
):
    offsets, _, blk = source_rows.shape
    rows, channels = features.shape
    n_grp, n_tile = lax.axis_size("grp"), lax.axis_size("tile")
    per = offsets // KINDS
    flat_one = weight_one.reshape(offsets * channels, channels)
    flat_two = weight_two.reshape(offsets * channels, channels)
    packed = blk + per + (-per % 16)
    half = offsets * channels // n_grp // 2
    slot = half + (-half % 16)
    field, block = ((rows, channels), BF16), ((blk, channels), BF16)
    summed = ((rows, channels), F32)
    keep_shape = ((n_grp, slot, channels), F32)
    core_shape = ((blk + n_grp * slot, channels), BF16)
    pairs_shape = ((per, 2 * blk, 2 * blk), BF16)
    single_shape, turned_shape = ((2 * per, 2 * blk, blk), BF16), ((2 * per, blk, 2 * blk), BF16)
    inner, outer = ((rows, per * channels), BF16), ((rows, 2 * per * channels), BF16)
    pulled = ((rows, offsets * channels), BF16)
    wgrad = ((offsets * channels, channels), F32)
    count = block_count

    near, core, cross = call(
        pack_kernel,
        [((4 * per + (-4 * per % 8), blk), F32), ((packed, channels), BF16), ((packed, channels), BF16)],
        count, features, source_rows, target_codes.T,
        micros=3,
    )
    cross, core = crossed(cross), swapped(core, "tile", 1)
    pairs, singles, pairs_turned, singles_turned, part = call(
        local_kernel,
        [pairs_shape, single_shape, pairs_shape, turned_shape, summed],
        near, features, flat_one,
        scratch=[inner],
        micros=2,
    )
    entries, far, halo, hidden, slope, core, cross = call(
        first_kernel,
        [
            ((2 * per + (-2 * per % 8), blk), F32), single_shape, ((2, blk, channels), BF16),
            field, summed, block, block,
        ],
        count, features, core, cross, singles, part, flat_one,
        scratch=[outer],
        micros=2,
    )
    cross, core = crossed(cross), swapped(core, "tile", 1)
    part, far_turned = call(
        middle_kernel,
        [summed, turned_shape],
        hidden, pairs, entries, flat_two,
        scratch=[inner],
        micros=1,
    )
    result, grad_sum, own, keep_two, core_two, cross = call(
        second_kernel,
        [field, field, summed, keep_shape, core_shape, block],
        count, features, hidden, core, cross, far, singles, part, flat_two, out_cotangent,
        far_turned, pairs_turned, singles_turned,
        scratch=[outer, pulled, wgrad],
        micros=4,
    )
    cross, core_two = crossed(cross), swapped(core_two, "tile", 1)
    shard = (slot, channels)
    shards = [(shard, F32)] + [(shard, BF16)] * (n_grp - 1)
    mine_two, *sends_two = call(shards_kernel, shards, keep_two, core_two)
    got_two = [swapped(send, "grp", d + 1) for d, send in enumerate(sends_two)]
    own = after(sends_two[-1], own)
    own, keep_one, core_one, cross = call(
        third_kernel,
        [summed, keep_shape, core_shape, block],
        count, features, halo, own, core_two, cross, slope, grad_sum, flat_one,
        far_turned, pairs_turned, singles_turned,
        scratch=[pulled, wgrad],
        micros=3,
    )
    core_one = swapped(core_one, "tile", 1)
    mine_one, *sends_one = call(shards_kernel, shards, keep_one, core_one)
    got_one = [swapped(send, "grp", d + 1) for d, send in enumerate(sends_one)]
    cross = crossed(after(sends_one[-1], cross))
    got_two = [after(cross, got) for got in got_two]
    two = added(mine_two, got_two).astype(BF16)
    steps = [1 << b for b in range(1, (n_tile - 1).bit_length())]
    other_two = swapped(two, "tile", steps[0])
    one = added(mine_one, got_one).astype(BF16)
    one = after(cross, one)
    (input_grad,) = call(last_kernel, [field], count, own, core_one, cross)
    for at, bits in enumerate(steps):
        other_one = swapped(one, "tile", bits)
        two = added(two, [other_two])
        if at + 1 < len(steps):
            two = after(one, two.astype(BF16))
            other_two = swapped(two, "tile", steps[at + 1])
            one = added(one, [other_one]).astype(BF16)
        else:
            one = added(one, [other_one])
    voxel_total = n_grp * n_tile * rows
    scale = float(voxel_total) ** (-0.5)
    odd = lax.axis_index("tile") % 2 == 1
    outs = []
    for half_sum in (one, two):
        half_sum = half_sum[:half] * scale
        other = swapped(half_sum, "tile", 1)
        outs.append(
            jnp.concatenate(
                [jnp.where(odd, other, half_sum), jnp.where(odd, half_sum, other)], axis=0
            )
        )
    return (result, input_grad, outs[0], outs[1])


def solution(mesh):
    in_specs = (
        P(("grp", "tile"), None),
        P(None, ("grp", "tile"), None),
        P(None, ("grp", "tile")),
        P(("grp", "tile")),
        P(),
        P(),
        P(("grp", "tile"), None),
    )
    out_specs = (P(("grp", "tile"), None), P(("grp", "tile"), None), P("grp", None), P("grp", None))
    return jax.shard_map(
        on_device, mesh=mesh, in_specs=in_specs, out_specs=out_specs, check_vma=False
    )
```

time: 58.8 us -> 55.6 us (0.946)
  Pallas kernels: 14.1 us -> 10.6 us
  starting transfers between devices: 29 us -> 25.8 us
  waiting for transfers between devices: 10.1 us -> 13.1 us
  local copies, waits for them, and re-layouts: 1.53 us -> 2.27 us
    ppermute x16, waiting for transfers between devices: 4.65 us -> 8.99 us  [swapped(): lax.ppermute(value, axis, [(i, i ^ bits) for i in range(count) if i ^ bit...]
    pallas_call x7 -> x9, Pallas kernels: 14.1 us -> 10.6 us  [call(): pl.pallas_call(kernel, out_shape=[jax.ShapeDtypeStruct(shape, kind) for s...]
    ppermute x16, starting transfers between devices: 22.5 us -> 19.2 us  [swapped(): lax.ppermute(value, axis, [(i, i ^ bits) for i in range(count) if i ^ bit...]
    ppermute x4, waiting for transfers between devices: 5.44 us -> 4.13 us  [crossed(): return lax.ppermute(value, ('grp', 'tile'), pairs)]
    unnamed x11 -> x14, local copies, waits for them, and re-layouts: 1.53 us -> 2.27 us
  transfers between devices with their start and end apart: 20 -> 20, of which waited for: 9 -> 11; matrix products, arithmetic and copies ran while one was open for 2% -> 2% of each run, Pallas kernels for 4% -> 5%
where the time goes in v4:
time: 55.6 us; the launch traced here: 55.1 us
  starting transfers between devices  25.8 us (46%)
  waiting for transfers between devices  13.1 us (24%)
  Pallas kernels  10.6 us (19%)
  local copies, waits for them, and re-layouts  2.27 us (4%)
  other arithmetic  1.93 us (3%)
  between operations  1.41 us (3%)
    ppermute x16, starting transfers between devices, swapped(): lax.ppermute(value, axis, [(i, i ^ bits) for i in range(count) if i ^ bit...  19.2 us
    pallas_call x9, Pallas kernels, call(): pl.pallas_call(kernel, out_shape=[jax.ShapeDtypeStruct(shape, kind) for s...  10.6 us
    ppermute x16, waiting for transfers between devices, swapped(): lax.ppermute(value, axis, [(i, i ^ bits) for i in range(count) if i ^ bit...  8.99 us
    ppermute x4, starting transfers between devices, crossed(): return lax.ppermute(value, ('grp', 'tile'), pairs)  6.54 us
    ppermute x4, waiting for transfers between devices, crossed(): return lax.ppermute(value, ('grp', 'tile'), pairs)  4.13 us
    unnamed x14, local copies, waits for them, and re-layouts  2.27 us
    concatenate x2, other arithmetic, on_device(): jnp.concatenate([jnp.where(odd, other, half_sum), jnp.where(odd, half_sum...  1.58 us
  transfers between devices with their start and end apart: 20, of which 11 were waited for; matrix products, arithmetic and copies ran while one was open for 2% of the time, Pallas kernels for 5%

profile of v4, /device:TPU:1, one launch (start us, length us, event | category | flops | bytes accessed | tf_op | source)
XLA Modules:
  0.0 55.1 jit_solution(8168220223734994755)
XLA Ops:
  1.3 0.8 %copy-done.3 = bf16[256,128]{1,0:T(8,128)(2,1)S(1)} copy-done((bf16[256,128]{1,0:T(8,128)(2,1)S(1)}, bf16[256,128]{1,0:T(8,128)(2,1)}, u32[]{:S(2)}) %copy-start.3) | copy-done | bytes 65560
  2.1 0.7 %copy-done.5 = s32[27,2,128]{2,1,0:T(2,128)S(1)} copy-done((s32[27,2,128]{2,1,0:T(2,128)S(1)}, s32[27,2,128]{2,1,0:T(2,128)}, u32[]{:S(2)}) %copy-start.5) | copy-done | bytes 27672
  2.9 0.7 %copy-done.6 = s32[27,2]{0,1:T(2,128)S(1)} copy-done((s32[27,2]{0,1:T(2,128)S(1)}, s32[27,2]{0,1:T(2,128)}, u32[]{:S(2)}) %copy-start.6) | copy-done | bytes 240
  3.5 0.1 shard_map.102
  3.7 0.1 collective-permute-start
  3.8 2.7 %collective-permute-start.1 = (bf16[144,128]{1,0:T(8,128)(2,1)S(1)}, bf16[144,128]{1,0:T(8,128)(2,1)S(1)}, u32[]{:S(2)}, u32[]{:S(2)}) collective-permute-start(bf16[144,128]{1,0:T(8,128)(2,1)S(1)} %get-tuple-element.47), channel_id=1, source_target_pairs={{0,8},{1,2},{2,1},{3,4},{4,3},{5,6},{6,5},{7,15},{8,0},{9,10},{10,... | collective-permute-start | bytes 110600 | tf_op jit(solution)/shard_map/ppermute | solution.py:30
  6.5 1.1 %shard_map.103 = (bf16[9,256,256]{2,1,0:T(8,128)(2,1)S(1)}, bf16[18,256,128]{2,1,0:T(8,128)(2,1)S(1)}, bf16[9,256,256]{2,1,0:T(8,128)(2,1)S(1)}, bf16[18,128,256]{2,1,0:T(8,128)(2,1)S(1)}, f32[256,128]{1,0:T(8,128)S(1)}) custom-call(f32[40,128]{1,0:T(8,128)S(1)} %get-tuple-element.48.near, bf16[256,128]{1,0:T(8,128)(2,1)S(1)} %copy-done.3, ...), custom_call_target="tpu_custom_call" | custom-call | flops 2000000000 | bytes 6000000 | tf_op jit(solution)/shard_map/pallas_call | solution.py:348
  7.6 0.7 %collective-permute-done.1.cross_in = bf16[144,128]{1,0:T(8,128)(2,1)S(1)} collective-permute-done((bf16[144,128]{1,0:T(8,128)(2,1)S(1)}, bf16[144,128]{1,0:T(8,128)(2,1)S(1)}, u32[]{:S(2)}, u32[]{:S(2)}) %collective-permute-start.1) | collective-permute-done | bytes 36896 | tf_op jit(solution)/shard_map/ppermute | solution.py:30
  8.3 1.3 %shard_map.104 = (f32[24,128]{1,0:T(8,128)S(1)}, bf16[18,256,128]{2,1,0:T(8,128)(2,1)S(1)}, bf16[2,128,128]{2,1,0:T(8,128)(2,1)S(1)}, bf16[256,128]{1,0:T(8,128)...) custom-call(s32[1]{0:T(128)S(6)} %copy.11.count_ref, ...), custom_call_target="tpu_custom_call" | custom-call | flops 2000000000 | bytes 6000000 | tf_op jit(solution)/shard_map/pallas_call | solution.py:348
  9.6 0.5 collective-permute-start.2
  10.1 1.6 %collective-permute-start.3 = (bf16[128,128]{1,0:T(8,128)(2,1)S(1)}, bf16[128,128]{1,0:T(8,128)(2,1)S(1)}, u32[]{:S(2)}, u32[]{:S(2)}) collective-permute-start(bf16[128,128]{1,0:T(8,128)(2,1)S(1)} %get-tuple-element.53), channel_id=1, source_target_pairs={{0,8},{1,2},{2,1},{3,4},{4,3},{5,6},{6,5},{7,15},{8,0},{9,10},{10,... | collective-permute-start | bytes 98312 | tf_op jit(solution)/shard_map/ppermute | solution.py:30
  11.7 0.7 %shard_map.105 = (f32[256,128]{1,0:T(8,128)S(1)}, bf16[18,128,256]{2,1,0:T(8,128)(2,1)S(1)}) custom-call(bf16[256,128]{1,0:T(8,128)(2,1)S(1)} %get-tuple-element.51.hidden, bf16[9,256,256]{2,1,0:T(8,128)(2,1)S(1)} %get-tuple-element.55.pairs, f32[24,128]{1,0:T(8,128)S(1)} %get-tuple-element.56.entries, bf16[3456,128]{1,0:T(8,128)(2,1)S(1)} %bitcast.3), custom_call_target="tpu_custom_call" | custom-call | flops 1000000000 | bytes 3000000 | tf_op jit(solution)/shard_map/pallas_call | solution.py:348
  12.4 1.3 %collective-permute-done.3.cross_in = bf16[128,128]{1,0:T(8,128)(2,1)S(1)} collective-permute-done((bf16[128,128]{1,0:T(8,128)(2,1)S(1)}, bf16[128,128]{1,0:T(8,128)(2,1)S(1)}, u32[]{:S(2)}, u32[]{:S(2)}) %collective-permute-start.3) | collective-permute-done | bytes 32800 | tf_op jit(solution)/shard_map/ppermute | solution.py:30
  13.7 3.9 %shard_map.106 = (bf16[256,128]{1,0:T(8,128)(2,1)}, bf16[256,128]{1,0:T(8,128)(2,1)S(1)}, f32[256,128]{1,0:T(8,128)S(1)}, f32[4,432,128]{2,1,0:T(8,128)S(1)}, bf...) custom-call(s32[1]{0:T(128)S(6)} %copy.11.count_ref, bf16[256,128]{1,0:T(8,128)(2,1)S(1)} %copy-done.4, ...), custom_call_target="tpu_custom_call" | custom-call | flops 4000000000 | bytes 12000000 | tf_op jit(solution)/shard_map/pallas_call | solution.py:348
  17.7 0.4 collective-permute-start.4
  18.1 1.0 %collective-permute-start.5 = (bf16[128,128]{1,0:T(8,128)(2,1)S(1)}, bf16[128,128]{1,0:T(8,128)(2,1)S(1)}, u32[]{:S(2)}, u32[]{:S(2)}) collective-permute-start(bf16[128,128]{1,0:T(8,128)(2,1)S(1)} %get-tuple-element.68), channel_id=1, source_target_pairs={{0,8},{1,2},{2,1},{3,4},{4,3},{5,6},{6,5},{7,15},{8,0},{9,10},{10,... | collective-permute-start | bytes 98312 | tf_op jit(solution)/shard_map/ppermute | solution.py:30
  19.1 0.5 collective-permute-done.4.core.core_in
  19.5 0.1 shard_map.107
  19.6 2.1 %collective-permute-done.5.cross_in = bf16[128,128]{1,0:T(8,128)(2,1)S(1)} collective-permute-done((bf16[128,128]{1,0:T(8,128)(2,1)S(1)}, bf16[128,128]{1,0:T(8,128)(2,1)S(1)}, u32[]{:S(2)}, u32[]{:S(2)}) %collective-permute-start.5) | collective-permute-done | bytes 32800 | tf_op jit(solution)/shard_map/ppermute | solution.py:30
  21.7 2.6 %shard_map.108 = (f32[256,128]{1,0:T(8,128)S(1)}, f32[4,432,128]{2,1,0:T(8,128)S(1)}, bf16[1856,128]{1,0:T(8,128)(2,1)S(1)}, bf16[128,128]{1,0:T(8,128)(2,1)S(1)}) custom-call(s32[1]{0:T(128)S(6)} %copy.11.count_ref, bf16[256,128]{1,0:T(8,128)(2,1)S(1)} %copy-done.4, bf16[2,128,128]{2,1,0:T(8,128)(2,1)S(1)} %get-tuple-element.62.halo, ...), custom_call_target="tpu_custom_call" | custom-call | flops 3000000000 | bytes 9000000 | tf_op jit(solution)/shard_map/pallas_call | solution.py:348
  24.2 0.4 collective-permute-start.6
  24.7 2.7 %collective-permute-start.16 = (bf16[432,128]{1,0:T(8,128)(2,1)S(1)}, bf16[432,128]{1,0:T(8,128)(2,1)S(1)}, u32[]{:S(2)}, u32[]{:S(2)}) collective-permute-start(bf16[432,128]{1,0:T(8,128)(2,1)S(1)} %get-tuple-element.65), channel_id=1, source_target_pairs={{0,24},{8,16},{16,8},{24,0},{1,25},{9,17},{17,9},{25,1},{2,26},{10... | collective-permute-start | bytes 331784 | tf_op jit(solution)/shard_map/ppermute | solution.py:17
  27.4 0.3 collective-permute-start.14
  27.6 0.0 collective-permute-start.15
  27.7 0.1 shard_map.109
  27.8 1.3 %collective-permute-start.7 = (bf16[128,128]{1,0:T(8,128)(2,1)S(1)}, bf16[128,128]{1,0:T(8,128)(2,1)S(1)}, u32[]{:S(2)}, u32[]{:S(2)}) collective-permute-start(bf16[128,128]{1,0:T(8,128)(2,1)S(1)} %get-tuple-element.76), channel_id=1, source_target_pairs={{0,8},{1,2},{2,1},{3,4},{4,3},{5,6},{6,5},{7,15},{8,0},{9,10},{10,... | collective-permute-start | bytes 98312 | tf_op jit(solution)/shard_map/ppermute | solution.py:30
  29.1 2.2 %collective-permute-start.10 = (bf16[432,128]{1,0:T(8,128)(2,1)S(1)}, bf16[432,128]{1,0:T(8,128)(2,1)S(1)}, u32[]{:S(2)}, u32[]{:S(2)}) collective-permute-start(bf16[432,128]{1,0:T(8,128)(2,1)S(1)} %get-tuple-element.74), channel_id=1, source_target_pairs={{0,24},{8,16},{16,8},{24,0},{1,25},{9,17},{17,9},{25,1},{2,26},{10... | collective-permute-start | bytes 331784 | tf_op jit(solution)/shard_map/ppermute | solution.py:17
  31.2 1.9 %collective-permute-done.14 = bf16[432,128]{1,0:T(8,128)(2,1)S(1)} collective-permute-done((bf16[432,128]{1,0:T(8,128)(2,1)S(1)}, bf16[432,128]{1,0:T(8,128)(2,1)S(1)}, u32[]{:S(2)}, u32[]{:S(2)}) %collective-permute-start.14) | collective-permute-done | bytes 110624 | tf_op jit(solution)/shard_map/ppermute | solution.py:17
  33.1 1.2 %collective-permute-start.8 = (bf16[432,128]{1,0:T(8,128)(2,1)S(1)}, bf16[432,128]{1,0:T(8,128)(2,1)S(1)}, u32[]{:S(2)}, u32[]{:S(2)}) collective-permute-start(bf16[432,128]{1,0:T(8,128)(2,1)S(1)} %get-tuple-element.78), channel_id=1, source_target_pairs={{0,8},{8,0},{16,24},{24,16},{1,9},{9,1},{17,25},{25,17},{2,10},{10... | collective-permute-start | bytes 331784 | tf_op jit(solution)/shard_map/ppermute | solution.py:17
  34.3 0.2 collective-permute-start.9
  34.5 0.1 add_convert_fusion.1
  34.6 0.1 collective-permute-start.17
  34.7 0.7 %shard_map.110 = bf16[256,128]{1,0:T(8,128)(2,1)} custom-call(s32[1]{0:T(128)S(6)} %copy.11.count_ref, f32[256,128]{1,0:T(8,128)S(1)} %get-tuple-element.71.own, bf16[1856,128]{1,0:T(8,128)(2,1)S(1)} %collective-permute-done.6.core.core_in, bf16[128,128]{1,0:T(8,128)(2,1)S(1)} %collective-permute-done.7.cross_in), custom_call_target="tpu_custom_call" | custom-call | flops 1000000000 | bytes 3000000 | tf_op jit(solution)/shard_map/pallas_call | solution.py:348
  35.3 1.9 %collective-permute-done.8 = bf16[432,128]{1,0:T(8,128)(2,1)S(1)} collective-permute-done((bf16[432,128]{1,0:T(8,128)(2,1)S(1)}, bf16[432,128]{1,0:T(8,128)(2,1)S(1)}, u32[]{:S(2)}, u32[]{:S(2)}) %collective-permute-start.8) | collective-permute-done | bytes 110624 | tf_op jit(solution)/shard_map/ppermute | solution.py:17
  37.2 0.9 %collective-permute-done.9 = bf16[432,128]{1,0:T(8,128)(2,1)S(1)} collective-permute-done((bf16[432,128]{1,0:T(8,128)(2,1)S(1)}, bf16[432,128]{1,0:T(8,128)(2,1)S(1)}, u32[]{:S(2)}, u32[]{:S(2)}) %collective-permute-start.9) | collective-permute-done | bytes 110624 | tf_op jit(solution)/shard_map/ppermute | solution.py:17
  38.2 0.1 add_convert_fusion.3
  38.2 0.1 collective-permute-start.11
  38.3 0.2 collective-permute-done.17
  38.6 1.7 %collective-permute-start.18 = (bf16[432,128]{1,0:T(8,128)(2,1)S(1)}, bf16[432,128]{1,0:T(8,128)(2,1)S(1)}, u32[]{:S(2)}, u32[]{:S(2)}) collective-permute-start(bf16[432,128]{1,0:T(8,128)(2,1)S(1)} %add_convert_fusion), channel_id=1, source_target_pairs={{0,4},{1,5},{2,6},{3,7},{4,0},{5,1},{6,2},{7,3},{8,12},{9,13},{10,... | collective-permute-start | bytes 331784 | tf_op jit(solution)/shard_map/ppermute | solution.py:17
  40.3 1.7 %collective-permute-done.11 = bf16[432,128]{1,0:T(8,128)(2,1)S(1)} collective-permute-done((bf16[432,128]{1,0:T(8,128)(2,1)S(1)}, bf16[432,128]{1,0:T(8,128)(2,1)S(1)}, u32[]{:S(2)}, u32[]{:S(2)}) %collective-permute-start.11) | collective-permute-done | bytes 110624 | tf_op jit(solution)/shard_map/ppermute | solution.py:17
  42.0 0.6 %collective-permute-start.12 = (bf16[432,128]{1,0:T(8,128)(2,1)S(1)}, bf16[432,128]{1,0:T(8,128)(2,1)S(1)}, u32[]{:S(2)}, u32[]{:S(2)}) collective-permute-start(bf16[432,128]{1,0:T(8,128)(2,1)S(1)} %add_convert_fusion.2), channel_id=1, source_target_pairs={{0,4},{1,5},{2,6},{3,7},{4,0},{5,1},{6,2},{7,3},{8,12},{9,13},{10,... | collective-permute-start | bytes 331784 | tf_op jit(solution)/shard_map/ppermute | solution.py:17
  42.6 1.7 %collective-permute-done.18 = bf16[432,128]{1,0:T(8,128)(2,1)S(1)} collective-permute-done((bf16[432,128]{1,0:T(8,128)(2,1)S(1)}, bf16[432,128]{1,0:T(8,128)(2,1)S(1)}, u32[]{:S(2)}, u32[]{:S(2)}) %collective-permute-start.18) | collective-permute-done | bytes 110624 | tf_op jit(solution)/shard_map/ppermute | solution.py:17
  44.3 7.6 %collective-permute-start.19 = (f32[432,128]{1,0:T(8,128)S(1)}, f32[432,128]{1,0:T(8,128)S(1)}, u32[]{:S(2)}, u32[]{:S(2)}) collective-permute-start(f32[432,128]{1,0:T(8,128)S(1)} %add_multiply_fusion), channel_id=1, source_target_pairs={{0,1},{1,0},{2,3},{3,2},{4,5},{5,4},{6,7},{7,6},{8,9},{9,8},{10,11... | collective-permute-start | bytes 663560 | tf_op jit(solution)/shard_map/ppermute | solution.py:17
  52.0 1.2 %collective-permute-start.13 = (f32[432,128]{1,0:T(8,128)S(1)}, f32[432,128]{1,0:T(8,128)S(1)}, u32[]{:S(2)}, u32[]{:S(2)}) collective-permute-start(f32[432,128]{1,0:T(8,128)S(1)} %add_multiply_fusion.1), channel_id=1, source_target_pairs={{0,1},{1,0},{2,3},{3,2},{4,5},{5,4},{6,7},{7,6},{8,9},{9,8},{10,11... | collective-permute-start | bytes 663560 | tf_op jit(solution)/shard_map/ppermute | solution.py:17
  53.1 0.1 broadcast_select_fusion.1
  53.2 0.8 %pad_maximum_fusion.1 = f32[864,128]{1,0:T(8,128)} fusion(f32[432,128]{1,0:T(8,128)S(1)} %get-tuple-element.89, f32[432,128]{1,0:T(8,128)S(1)} %get-tuple-element.88), kind=kLoop, calls=%fused_computation.1 | loop fusion | flops 110592 | bytes 884736 | tf_op jit(solution)/shard_map/concatenate | solution.py:466
  54.0 0.3 collective-permute-done.13
  54.3 0.8 %pad_maximum_fusion = f32[864,128]{1,0:T(8,128)} fusion(f32[432,128]{1,0:T(8,128)S(1)} %get-tuple-element.91, f32[432,128]{1,0:T(8,128)S(1)} %get-tuple-element.90), kind=kLoop, calls=%fused_computation | loop fusion | flops 110592 | bytes 884736 | tf_op jit(solution)/shard_map/concatenate | solution.py:466
  (25 shorter events, 0.2 us)
Async XLA Ops:
  1.3 0.8 %copy-start.3 = (bf16[256,128]{1,0:T(8,128)(2,1)S(1)}, bf16[256,128]{1,0:T(8,128)(2,1)}, u32[]{:S(2)}) copy-start(bf16[256,128]{1,0:T(8,128)(2,1)} %features.9) | copy-start | bytes 196612
  2.1 0.7 %copy-start.5 = (s32[27,2,128]{2,1,0:T(2,128)S(1)}, s32[27,2,128]{2,1,0:T(2,128)}, u32[]{:S(2)}) copy-start(s32[27,2,128]{2,1,0:T(2,128)} %source_rows.1) | copy-start | bytes 82948
  2.9 0.7 %copy-start.6 = (s32[27,2]{0,1:T(2,128)S(1)}, s32[27,2]{0,1:T(2,128)}, u32[]{:S(2)}) copy-start(s32[27,2]{0,1:T(2,128)} %param.9) | copy-start | bytes 652
  3.5 2.9 %copy-start.1 = (bf16[27,128,128]{2,1,0:T(8,128)(2,1)S(1)}, bf16[27,128,128]{2,1,0:T(8,128)(2,1)}, u32[]{:S(2)}) copy-start(bf16[27,128,128]{2,1,0:T(8,128)(2,1)} %param.11) | copy-start | bytes 2654212
  3.7 4.0 %collective-permute-start = (bf16[144,128]{1,0:T(8,128)(2,1)S(1)}, bf16[144,128]{1,0:T(8,128)(2,1)S(1)}, u32[]{:S(2)}, u32[]{:S(2)}) collective-permute-start(bf16[144,128]{1,0:T(8,128)(2,1)S(1)} %get-tuple-element.46), channel_id=1, source_target_pairs={{0,1},{1,0},{2,3},{3,2},{4,5},{5,4},{6,7},{7,6},{8,9},{9,8},{10,11... | collective-permute-start | bytes 110600 | tf_op jit(solution)/shard_map/ppermute | solution.py:17
  3.8 4.6 %collective-permute-start.1 = (bf16[144,128]{1,0:T(8,128)(2,1)S(1)}, bf16[144,128]{1,0:T(8,128)(2,1)S(1)}, u32[]{:S(2)}, u32[]{:S(2)}) collective-permute-start(bf16[144,128]{1,0:T(8,128)(2,1)S(1)} %get-tuple-element.47), channel_id=1, source_target_pairs={{0,8},{1,2},{2,1},{3,4},{4,3},{5,6},{6,5},{7,15},{8,0},{9,10},{10,... | collective-permute-start | bytes 110600 | tf_op jit(solution)/shard_map/ppermute | solution.py:30
  8.3 3.3 %copy-start = (bf16[27,128,128]{2,1,0:T(8,128)(2,1)S(1)}, bf16[27,128,128]{2,1,0:T(8,128)(2,1)}, u32[]{:S(2)}) copy-start(bf16[27,128,128]{2,1,0:T(8,128)(2,1)} %param.12) | copy-start | bytes 2654212
  9.6 2.7 %collective-permute-start.2 = (bf16[128,128]{1,0:T(8,128)(2,1)S(1)}, bf16[128,128]{1,0:T(8,128)(2,1)S(1)}, u32[]{:S(2)}, u32[]{:S(2)}) collective-permute-start(bf16[128,128]{1,0:T(8,128)(2,1)S(1)} %get-tuple-element.52), channel_id=1, source_target_pairs={{0,1},{1,0},{2,3},{3,2},{4,5},{5,4},{6,7},{7,6},{8,9},{9,8},{10,11... | collective-permute-start | bytes 98312 | tf_op jit(solution)/shard_map/ppermute | solution.py:17
  10.1 3.6 %collective-permute-start.3 = (bf16[128,128]{1,0:T(8,128)(2,1)S(1)}, bf16[128,128]{1,0:T(8,128)(2,1)S(1)}, u32[]{:S(2)}, u32[]{:S(2)}) collective-permute-start(bf16[128,128]{1,0:T(8,128)(2,1)S(1)} %get-tuple-element.53), channel_id=1, source_target_pairs={{0,8},{1,2},{2,1},{3,4},{4,3},{5,6},{6,5},{7,15},{8,0},{9,10},{10,... | collective-permute-start | bytes 98312 | tf_op jit(solution)/shard_map/ppermute | solution.py:30
  11.7 2.1 %copy-start.2 = (bf16[256,128]{1,0:T(8,128)(2,1)S(1)}, bf16[256,128]{1,0:T(8,128)(2,1)}, u32[]{:S(2)}) copy-start(bf16[256,128]{1,0:T(8,128)(2,1)} %cotangent.1) | copy-start | bytes 196612
  11.7 2.1 %copy-start.4 = (bf16[256,128]{1,0:T(8,128)(2,1)S(1)}, bf16[256,128]{1,0:T(8,128)(2,1)}, u32[]{:S(2)}) copy-start(bf16[256,128]{1,0:T(8,128)(2,1)} %features.9) | copy-start | bytes 196612
  17.7 1.9 %collective-permute-start.4 = (bf16[1856,128]{1,0:T(8,128)(2,1)S(1)}, bf16[1856,128]{1,0:T(8,128)(2,1)S(1)}, u32[]{:S(2)}, u32[]{:S(2)}) collective-permute-start(bf16[1856,128]{1,0:T(8,128)(2,1)S(1)} %get-tuple-element.64), channel_id=1, source_target_pairs={{0,1},{1,0},{2,3},{3,2},{4,5},{5,4},{6,7},{7,6},{8,9},{9,8},{10,11... | collective-permute-start | bytes 1425416 | tf_op jit(solution)/shard_map/ppermute | solution.py:17
  18.1 3.6 %collective-permute-start.5 = (bf16[128,128]{1,0:T(8,128)(2,1)S(1)}, bf16[128,128]{1,0:T(8,128)(2,1)S(1)}, u32[]{:S(2)}, u32[]{:S(2)}) collective-permute-start(bf16[128,128]{1,0:T(8,128)(2,1)S(1)} %get-tuple-element.68), channel_id=1, source_target_pairs={{0,8},{1,2},{2,1},{3,4},{4,3},{5,6},{6,5},{7,15},{8,0},{9,10},{10,... | collective-permute-start | bytes 98312 | tf_op jit(solution)/shard_map/ppermute | solution.py:30
  24.2 3.4 %collective-permute-start.6 = (bf16[1856,128]{1,0:T(8,128)(2,1)S(1)}, bf16[1856,128]{1,0:T(8,128)(2,1)S(1)}, u32[]{:S(2)}, u32[]{:S(2)}) collective-permute-start(bf16[1856,128]{1,0:T(8,128)(2,1)S(1)} %get-tuple-element.72), channel_id=1, source_target_pairs={{0,1},{1,0},{2,3},{3,2},{4,5},{5,4},{6,7},{7,6},{8,9},{9,8},{10,11... | collective-permute-start | bytes 1425416 | tf_op jit(solution)/shard_map/ppermute | solution.py:17
  24.7 9.8 %collective-permute-start.16 = (bf16[432,128]{1,0:T(8,128)(2,1)S(1)}, bf16[432,128]{1,0:T(8,128)(2,1)S(1)}, u32[]{:S(2)}, u32[]{:S(2)}) collective-permute-start(bf16[432,128]{1,0:T(8,128)(2,1)S(1)} %get-tuple-element.65), channel_id=1, source_target_pairs={{0,24},{8,16},{16,8},{24,0},{1,25},{9,17},{17,9},{25,1},{2,26},{10... | collective-permute-start | bytes 331784 | tf_op jit(solution)/shard_map/ppermute | solution.py:17
  27.4 5.7 %collective-permute-start.14 = (bf16[432,128]{1,0:T(8,128)(2,1)S(1)}, bf16[432,128]{1,0:T(8,128)(2,1)S(1)}, u32[]{:S(2)}, u32[]{:S(2)}) collective-permute-start(bf16[432,128]{1,0:T(8,128)(2,1)S(1)} %get-tuple-element.82), channel_id=1, source_target_pairs={{0,8},{8,0},{16,24},{24,16},{1,9},{9,1},{17,25},{25,17},{2,10},{10... | collective-permute-start | bytes 331784 | tf_op jit(solution)/shard_map/ppermute | solution.py:17
  27.6 6.9 %collective-permute-start.15 = (bf16[432,128]{1,0:T(8,128)(2,1)S(1)}, bf16[432,128]{1,0:T(8,128)(2,1)S(1)}, u32[]{:S(2)}, u32[]{:S(2)}) collective-permute-start(bf16[432,128]{1,0:T(8,128)(2,1)S(1)} %get-tuple-element.84), channel_id=1, source_target_pairs={{0,16},{8,24},{16,0},{24,8},{1,17},{9,25},{17,1},{25,9},{2,18},{10... | collective-permute-start | bytes 331784 | tf_op jit(solution)/shard_map/ppermute | solution.py:17
  27.8 6.5 %collective-permute-start.7 = (bf16[128,128]{1,0:T(8,128)(2,1)S(1)}, bf16[128,128]{1,0:T(8,128)(2,1)S(1)}, u32[]{:S(2)}, u32[]{:S(2)}) collective-permute-start(bf16[128,128]{1,0:T(8,128)(2,1)S(1)} %get-tuple-element.76), channel_id=1, source_target_pairs={{0,8},{1,2},{2,1},{3,4},{4,3},{5,6},{6,5},{7,15},{8,0},{9,10},{10,... | collective-permute-start | bytes 98312 | tf_op jit(solution)/shard_map/ppermute | solution.py:30
  29.1 6.3 %collective-permute-start.10 = (bf16[432,128]{1,0:T(8,128)(2,1)S(1)}, bf16[432,128]{1,0:T(8,128)(2,1)S(1)}, u32[]{:S(2)}, u32[]{:S(2)}) collective-permute-start(bf16[432,128]{1,0:T(8,128)(2,1)S(1)} %get-tuple-element.74), channel_id=1, source_target_pairs={{0,24},{8,16},{16,8},{24,0},{1,25},{9,17},{17,9},{25,1},{2,26},{10... | collective-permute-start | bytes 331784 | tf_op jit(solution)/shard_map/ppermute | solution.py:17
  33.1 4.2 %collective-permute-start.8 = (bf16[432,128]{1,0:T(8,128)(2,1)S(1)}, bf16[432,128]{1,0:T(8,128)(2,1)S(1)}, u32[]{:S(2)}, u32[]{:S(2)}) collective-permute-start(bf16[432,128]{1,0:T(8,128)(2,1)S(1)} %get-tuple-element.78), channel_id=1, source_target_pairs={{0,8},{8,0},{16,24},{24,16},{1,9},{9,1},{17,25},{25,17},{2,10},{10... | collective-permute-start | bytes 331784 | tf_op jit(solution)/shard_map/ppermute | solution.py:17
  34.3 3.9 %collective-permute-start.9 = (bf16[432,128]{1,0:T(8,128)(2,1)S(1)}, bf16[432,128]{1,0:T(8,128)(2,1)S(1)}, u32[]{:S(2)}, u32[]{:S(2)}) collective-permute-start(bf16[432,128]{1,0:T(8,128)(2,1)S(1)} %get-tuple-element.79), channel_id=1, source_target_pairs={{0,16},{8,24},{16,0},{24,8},{1,17},{9,25},{17,1},{25,9},{2,18},{10... | collective-permute-start | bytes 331784 | tf_op jit(solution)/shard_map/ppermute | solution.py:17
  34.6 4.0 %collective-permute-start.17 = (bf16[432,128]{1,0:T(8,128)(2,1)S(1)}, bf16[432,128]{1,0:T(8,128)(2,1)S(1)}, u32[]{:S(2)}, u32[]{:S(2)}) collective-permute-start(bf16[432,128]{1,0:T(8,128)(2,1)S(1)} %add_convert_fusion.1), channel_id=1, source_target_pairs={{0,2},{1,3},{2,0},{3,1},{4,6},{5,7},{6,4},{7,5},{8,10},{9,11},{10,... | collective-permute-start | bytes 331784 | tf_op jit(solution)/shard_map/ppermute | solution.py:17
  38.2 3.7 %collective-permute-start.11 = (bf16[432,128]{1,0:T(8,128)(2,1)S(1)}, bf16[432,128]{1,0:T(8,128)(2,1)S(1)}, u32[]{:S(2)}, u32[]{:S(2)}) collective-permute-start(bf16[432,128]{1,0:T(8,128)(2,1)S(1)} %add_convert_fusion.3), channel_id=1, source_target_pairs={{0,2},{1,3},{2,0},{3,1},{4,6},{5,7},{6,4},{7,5},{8,10},{9,11},{10,... | collective-permute-start | bytes 331784 | tf_op jit(solution)/shard_map/ppermute | solution.py:17
  38.6 5.7 %collective-permute-start.18 = (bf16[432,128]{1,0:T(8,128)(2,1)S(1)}, bf16[432,128]{1,0:T(8,128)(2,1)S(1)}, u32[]{:S(2)}, u32[]{:S(2)}) collective-permute-start(bf16[432,128]{1,0:T(8,128)(2,1)S(1)} %add_convert_fusion), channel_id=1, source_target_pairs={{0,4},{1,5},{2,6},{3,7},{4,0},{5,1},{6,2},{7,3},{8,12},{9,13},{10,... | collective-permute-start | bytes 331784 | tf_op jit(solution)/shard_map/ppermute | solution.py:17
  42.0 9.9 %collective-permute-start.12 = (bf16[432,128]{1,0:T(8,128)(2,1)S(1)}, bf16[432,128]{1,0:T(8,128)(2,1)S(1)}, u32[]{:S(2)}, u32[]{:S(2)}) collective-permute-start(bf16[432,128]{1,0:T(8,128)(2,1)S(1)} %add_convert_fusion.2), channel_id=1, source_target_pairs={{0,4},{1,5},{2,6},{3,7},{4,0},{5,1},{6,2},{7,3},{8,12},{9,13},{10,... | collective-permute-start | bytes 331784 | tf_op jit(solution)/shard_map/ppermute | solution.py:17
  44.3 8.8 %collective-permute-start.19 = (f32[432,128]{1,0:T(8,128)S(1)}, f32[432,128]{1,0:T(8,128)S(1)}, u32[]{:S(2)}, u32[]{:S(2)}) collective-permute-start(f32[432,128]{1,0:T(8,128)S(1)} %add_multiply_fusion), channel_id=1, source_target_pairs={{0,1},{1,0},{2,3},{3,2},{4,5},{5,4},{6,7},{7,6},{8,9},{9,8},{10,11... | collective-permute-start | bytes 663560 | tf_op jit(solution)/shard_map/ppermute | solution.py:17
  52.0 2.3 %collective-permute-start.13 = (f32[432,128]{1,0:T(8,128)S(1)}, f32[432,128]{1,0:T(8,128)S(1)}, u32[]{:S(2)}, u32[]{:S(2)}) collective-permute-start(f32[432,128]{1,0:T(8,128)S(1)} %add_multiply_fusion.1), channel_id=1, source_target_pairs={{0,1},{1,0},{2,3},{3,2},{4,5},{5,4},{6,7},{7,6},{8,9},{9,8},{10,11... | collective-permute-start | bytes 663560 | tf_op jit(solution)/shard_map/ppermute | solution.py:17

commit v5 on v4

--- a/solution.py
+++ b/solution.py
@@ -49,7 +49,7 @@
 
 
 def row_mask(rows, blk, count):
-    block = lax.broadcasted_iota(jnp.int32, (rows, 1), 0) // blk
+    block = lax.broadcasted_iota(jnp.int32, (rows, count.shape[1]), 0) // blk
     return (block < count).astype(F32)
 
 
@@ -64,10 +64,23 @@
     return jnp.concatenate(rows, axis=0)
 
 
-def pack_kernel(count_ref, features, source_rows, codes, near, core_out, cross_out):
+def pack_kernel(
+    features_in, rows_in, codes_in, near, core_out, cross_out, count_out,
+    features, source_rows, codes, done,
+):
+    copies = []
+    for at, (source, target) in enumerate(
+        [(rows_in, source_rows), (codes_in, codes), (features_in, features)]
+    ):
+        copies.append(pltpu.make_async_copy(source, target, done.at[at]))
+        copies[-1].start()
+    for copy in copies:
+        copy.wait()
     offsets, _, blk = source_rows.shape
     per = offsets // KINDS
-    count = count_ref[0]
+    count = jnp.where(codes[:1, KINDS - 1 : KINDS] // 2 == 2, 1, 2)
+    count = jnp.broadcast_to(count, (1, blk))
+    count_out[...] = jnp.broadcast_to(count, count_out.shape)
     both = count == 2
     odd, has_prev, has_next = place()
     diagonal = lax.broadcasted_iota(jnp.int32, (offsets, offsets), 0) == lax.broadcasted_iota(
@@ -211,7 +224,7 @@
 ):
     blk = features.shape[0] // 2
     per = singles.shape[0] // 2
-    count = count_ref[0]
+    count = count_ref[:1, :]
     odd, _, _ = place()
     from_next, from_prev = halo_sides(odd, core_in[...].astype(F32), cross_in[...].astype(F32))
     table = stacked([from_next[blk : blk + per], from_prev[blk : blk + per]], blk, -1.0)
@@ -250,7 +263,7 @@
     result, grads_out, own_out, keep, core_out, cross_out, picked, pulled, wgrad,
 ):
     blk = features.shape[0] // 2
-    count = count_ref[0]
+    count = count_ref[:1, :]
     both = count == 2
     odd, _, _ = place()
     after, before = halo_sides(odd, core_in[...], cross_in[...])
@@ -289,7 +302,7 @@
     own_out, keep, core_out, cross_out, pulled, wgrad,
 ):
     blk = features.shape[0] // 2
-    both = count_ref[0] == 2
+    both = count_ref[:1, :] == 2
     odd, _, _ = place()
     core, cross = core_in[:blk, :].astype(F32), cross_in[...].astype(F32)
     summed = joined(own[...], odd, both, core, cross, blk)
@@ -312,7 +325,7 @@
 
 def last_kernel(count_ref, own, core_in, cross_in, input_grad):
     blk = own.shape[0] // 2
-    both = count_ref[0] == 2
+    both = count_ref[:1, :] == 2
     odd, _, _ = place()
     core, cross = core_in[:blk, :].astype(F32), cross_in[...].astype(F32)
     input_grad[...] = joined(own[...], odd, both, core, cross, blk).astype(BF16)
@@ -343,14 +356,14 @@
     return value
 
 
-def call(kernel, outs, *args, scratch=(), micros=1):
-    vmem, smem = pl.BlockSpec(memory_space=pltpu.VMEM), pl.BlockSpec(memory_space=pltpu.SMEM)
+def call(kernel, outs, *args, scratch=(), micros=1, far=False):
+    vmem = pl.BlockSpec(memory_space=pltpu.VMEM)
     return pl.pallas_call(
         kernel,
         out_shape=[jax.ShapeDtypeStruct(shape, kind) for shape, kind in outs],
-        in_specs=[smem if arg.shape == (1,) else vmem for arg in args],
+        in_specs=[pl.BlockSpec(memory_space=pltpu.HBM if far else pltpu.VMEM)] * len(args),
         out_specs=[vmem] * len(outs),
-        scratch_shapes=[pltpu.VMEM(shape, kind) for shape, kind in scratch],
+        scratch_shapes=[pltpu.VMEM(*one) if isinstance(one, tuple) else one for one in scratch],
         compiler_params=pltpu.CompilerParams(vmem_limit_bytes=LIMIT),
         cost_estimate=pl.CostEstimate(
             flops=micros * 10**9, bytes_accessed=micros * 3 * 10**6, transcendentals=0
@@ -379,13 +392,24 @@
     inner, outer = ((rows, per * channels), BF16), ((rows, 2 * per * channels), BF16)
     pulled = ((rows, offsets * channels), BF16)
     wgrad = ((offsets * channels, channels), F32)
-    count = block_count
-
-    near, core, cross = call(
+
+    near, core, cross, count = call(
         pack_kernel,
-        [((4 * per + (-4 * per % 8), blk), F32), ((packed, channels), BF16), ((packed, channels), BF16)],
-        count, features, source_rows, target_codes.T,
+        [
+            ((4 * per + (-4 * per % 8), blk), F32), ((packed, channels), BF16),
+            ((packed, channels), BF16), ((8, channels), jnp.int32),
+        ],
+        *[
+            pltpu.with_memory_space_constraint(value, pltpu.HBM)
+            for value in (features, source_rows, target_codes.T)
+        ],
+        scratch=[
+            pltpu.VMEM(features.shape, BF16), pltpu.VMEM(source_rows.shape, jnp.int32),
+            pltpu.VMEM(target_codes.shape[::-1], jnp.int32),
+            pltpu.SemaphoreType.DMA((3,)),
+        ],
         micros=3,
+        far=True,
     )
     cross, core = crossed(cross), swapped(core, "tile", 1)
     pairs, singles, pairs_turned, singles_turned, part = call(

time: 55.6 us -> 53.4 us (0.960)
  local copies, waits for them, and re-layouts: 2.27 us -> 0.02 us
  Pallas kernels: 10.6 us -> 11.3 us
  between operations: 1.41 us -> 0.77 us
    unnamed x14 -> x8, local copies, waits for them, and re-layouts: 2.27 us -> 0.02 us
    pallas_call x9, Pallas kernels: 10.6 us -> 11.3 us  [call(): pl.pallas_call(kernel, out_shape=[jax.ShapeDtypeStruct(shape, kind) for s...]
where the time goes in v5:
time: 53.4 us; the launch traced here: 53 us
  starting transfers between devices  25.9 us (49%)
  waiting for transfers between devices  13.1 us (25%)
  Pallas kernels  11.3 us (21%)
  other arithmetic  1.94 us (4%)
  between operations  0.77 us (1%)
    ppermute x16, starting transfers between devices, swapped(): lax.ppermute(value, axis, [(i, i ^ bits) for i in range(count) if i ^ bit...  19.3 us
    pallas_call x9, Pallas kernels, call(): pl.pallas_call(kernel, out_shape=[jax.ShapeDtypeStruct(shape, kind) for s...  11.3 us
    ppermute x16, waiting for transfers between devices, swapped(): lax.ppermute(value, axis, [(i, i ^ bits) for i in range(count) if i ^ bit...  8.95 us
    ppermute x4, starting transfers between devices, crossed(): return lax.ppermute(value, ('grp', 'tile'), pairs)  6.56 us
    ppermute x4, waiting for transfers between devices, crossed(): return lax.ppermute(value, ('grp', 'tile'), pairs)  4.13 us
    concatenate x2, other arithmetic, on_device(): jnp.concatenate([jnp.where(odd, other, half_sum), jnp.where(odd, half_sum...  1.58 us
  transfers between devices with their start and end apart: 20, of which 11 were waited for; matrix products, arithmetic and copies ran while one was open for 2% of the time, Pallas kernels for 5%

profile of v5, /device:TPU:1, one launch (start us, length us, event | category | flops | bytes accessed | tf_op | source)
XLA Modules:
  0.0 53.0 jit_solution(6739303031837176414)
XLA Ops:
  0.7 1.1 %shard_map.93 = (f32[40,128]{1,0:T(8,128)S(1)}, bf16[144,128]{1,0:T(8,128)(2,1)S(1)}, bf16[144,128]{1,0:T(8,128)(2,1)S(1)}, s32[8,128]{1,0:T(8,128)S(1)}) custom-call(bf16[256,128]{1,0:T(8,128)(2,1)} %features.7, s32[27,2,128]{2,1,0:T(2,128)} %rows_in.1, s32[2,27]{1,0:T(2,128)} %bitcast.8), custom_call_target="tpu_custom_call" | custom-call | flops 3000000000 | bytes 9000000 | tf_op jit(solution)/shard_map/pallas_call | solution.py:361
  1.8 0.1 collective-permute-start
  1.9 2.7 %collective-permute-start.1 = (bf16[144,128]{1,0:T(8,128)(2,1)S(1)}, bf16[144,128]{1,0:T(8,128)(2,1)S(1)}, u32[]{:S(2)}, u32[]{:S(2)}) collective-permute-start(bf16[144,128]{1,0:T(8,128)(2,1)S(1)} %get-tuple-element.49), channel_id=1, source_target_pairs={{0,8},{1,2},{2,1},{3,4},{4,3},{5,6},{6,5},{7,15},{8,0},{9,10},{10,... | collective-permute-start | bytes 110600 | tf_op jit(solution)/shard_map/ppermute | solution.py:30
  4.6 1.1 %shard_map.94 = (bf16[9,256,256]{2,1,0:T(8,128)(2,1)S(1)}, bf16[18,256,128]{2,1,0:T(8,128)(2,1)S(1)}, bf16[9,256,256]{2,1,0:T(8,128)(2,1)S(1)}, bf16[18,128,256]{2,1,0:T(8,128)(2,1)S(1)}, f32[256,128]{1,0:T(8,128)S(1)}) custom-call(f32[40,128]{1,0:T(8,128)S(1)} %get-tuple-element.50.near, bf16[256,128]{1,0:T(8,128)(2,1)S(1)} %copy-done.3, ...), custom_call_target="tpu_custom_call" | custom-call | flops 2000000000 | bytes 6000000 | tf_op jit(solution)/shard_map/pallas_call | solution.py:361
  5.8 0.7 %collective-permute-done.1.cross_in = bf16[144,128]{1,0:T(8,128)(2,1)S(1)} collective-permute-done((bf16[144,128]{1,0:T(8,128)(2,1)S(1)}, bf16[144,128]{1,0:T(8,128)(2,1)S(1)}, u32[]{:S(2)}, u32[]{:S(2)}) %collective-permute-start.1) | collective-permute-done | bytes 36896 | tf_op jit(solution)/shard_map/ppermute | solution.py:30
  6.5 1.3 %shard_map.95 = (f32[24,128]{1,0:T(8,128)S(1)}, bf16[18,256,128]{2,1,0:T(8,128)(2,1)S(1)}, bf16[2,128,128]{2,1,0:T(8,128)(2,1)S(1)}, bf16[256,128]{1,0:T(8,128)(...) custom-call(s32[8,128]{1,0:T(8,128)S(1)} %get-tuple-element.47.count_ref, ...), custom_call_target="tpu_custom_call" | custom-call | flops 2000000000 | bytes 6000000 | tf_op jit(solution)/shard_map/pallas_call | solution.py:361
  7.8 0.5 collective-permute-start.2
  8.2 1.6 %collective-permute-start.3 = (bf16[128,128]{1,0:T(8,128)(2,1)S(1)}, bf16[128,128]{1,0:T(8,128)(2,1)S(1)}, u32[]{:S(2)}, u32[]{:S(2)}) collective-permute-start(bf16[128,128]{1,0:T(8,128)(2,1)S(1)} %get-tuple-element.55), channel_id=1, source_target_pairs={{0,8},{1,2},{2,1},{3,4},{4,3},{5,6},{6,5},{7,15},{8,0},{9,10},{10,... | collective-permute-start | bytes 98312 | tf_op jit(solution)/shard_map/ppermute | solution.py:30
  9.8 0.7 %shard_map.96 = (f32[256,128]{1,0:T(8,128)S(1)}, bf16[18,128,256]{2,1,0:T(8,128)(2,1)S(1)}) custom-call(bf16[256,128]{1,0:T(8,128)(2,1)S(1)} %get-tuple-element.53.hidden, bf16[9,256,256]{2,1,0:T(8,128)(2,1)S(1)} %get-tuple-element.57.pairs, f32[24,128]{1,0:T(8,128)S(1)} %get-tuple-element.58.entries, bf16[3456,128]{1,0:T(8,128)(2,1)S(1)} %bitcast.3), custom_call_target="tpu_custom_call" | custom-call | flops 1000000000 | bytes 3000000 | tf_op jit(solution)/shard_map/pallas_call | solution.py:361
  10.5 1.3 %collective-permute-done.3.cross_in = bf16[128,128]{1,0:T(8,128)(2,1)S(1)} collective-permute-done((bf16[128,128]{1,0:T(8,128)(2,1)S(1)}, bf16[128,128]{1,0:T(8,128)(2,1)S(1)}, u32[]{:S(2)}, u32[]{:S(2)}) %collective-permute-start.3) | collective-permute-done | bytes 32800 | tf_op jit(solution)/shard_map/ppermute | solution.py:30
  11.9 3.7 %shard_map.97 = (bf16[256,128]{1,0:T(8,128)(2,1)}, bf16[256,128]{1,0:T(8,128)(2,1)S(1)}, f32[256,128]{1,0:T(8,128)S(1)}, f32[4,432,128]{2,1,0:T(8,128)S(1)}, bf1...) custom-call(s32[8,128]{1,0:T(8,128)S(1)} %get-tuple-element.47.count_ref, bf16[256,128]{1,0:T(8,128)(2,1)S(1)} %copy-done.3, ...), custom_call_target="tpu_custom_call" | custom-call | flops 4000000000 | bytes 12000000 | tf_op jit(solution)/shard_map/pallas_call | solution.py:361
  15.5 0.4 collective-permute-start.4
  16.0 1.0 %collective-permute-start.5 = (bf16[128,128]{1,0:T(8,128)(2,1)S(1)}, bf16[128,128]{1,0:T(8,128)(2,1)S(1)}, u32[]{:S(2)}, u32[]{:S(2)}) collective-permute-start(bf16[128,128]{1,0:T(8,128)(2,1)S(1)} %get-tuple-element.70), channel_id=1, source_target_pairs={{0,8},{1,2},{2,1},{3,4},{4,3},{5,6},{6,5},{7,15},{8,0},{9,10},{10,... | collective-permute-start | bytes 98312 | tf_op jit(solution)/shard_map/ppermute | solution.py:30
  17.0 0.5 collective-permute-done.4.core.core_in
  17.4 0.1 shard_map.98
  17.5 2.1 %collective-permute-done.5.cross_in = bf16[128,128]{1,0:T(8,128)(2,1)S(1)} collective-permute-done((bf16[128,128]{1,0:T(8,128)(2,1)S(1)}, bf16[128,128]{1,0:T(8,128)(2,1)S(1)}, u32[]{:S(2)}, u32[]{:S(2)}) %collective-permute-start.5) | collective-permute-done | bytes 32800 | tf_op jit(solution)/shard_map/ppermute | solution.py:30
  19.6 2.6 %shard_map.99 = (f32[256,128]{1,0:T(8,128)S(1)}, f32[4,432,128]{2,1,0:T(8,128)S(1)}, bf16[1856,128]{1,0:T(8,128)(2,1)S(1)}, bf16[128,128]{1,0:T(8,128)(2,1)S(1)}) custom-call(s32[8,128]{1,0:T(8,128)S(1)} %get-tuple-element.47.count_ref, bf16[256,128]{1,0:T(8,128)(2,1)S(1)} %copy-done.3, bf16[2,128,128]{2,1,0:T(8,128)(2,1)S(1)} %get-tuple-element.64.halo, ...), custom_call_target="tpu_custom_call" | custom-call | flops 3000000000 | bytes 9000000 | tf_op jit(solution)/shard_map/pallas_call | solution.py:361
  22.2 0.5 collective-permute-start.6
  22.6 2.7 %collective-permute-start.16 = (bf16[432,128]{1,0:T(8,128)(2,1)S(1)}, bf16[432,128]{1,0:T(8,128)(2,1)S(1)}, u32[]{:S(2)}, u32[]{:S(2)}) collective-permute-start(bf16[432,128]{1,0:T(8,128)(2,1)S(1)} %get-tuple-element.67), channel_id=1, source_target_pairs={{0,24},{8,16},{16,8},{24,0},{1,25},{9,17},{17,9},{25,1},{2,26},{10... | collective-permute-start | bytes 331784 | tf_op jit(solution)/shard_map/ppermute | solution.py:17
  25.3 0.3 collective-permute-start.14
  25.6 0.0 collective-permute-start.15
  25.6 0.0 collective-permute-done.6.core.core_in
  25.6 0.1 shard_map.100
  25.7 1.3 %collective-permute-start.7 = (bf16[128,128]{1,0:T(8,128)(2,1)S(1)}, bf16[128,128]{1,0:T(8,128)(2,1)S(1)}, u32[]{:S(2)}, u32[]{:S(2)}) collective-permute-start(bf16[128,128]{1,0:T(8,128)(2,1)S(1)} %get-tuple-element.78), channel_id=1, source_target_pairs={{0,8},{1,2},{2,1},{3,4},{4,3},{5,6},{6,5},{7,15},{8,0},{9,10},{10,... | collective-permute-start | bytes 98312 | tf_op jit(solution)/shard_map/ppermute | solution.py:30
  27.0 2.2 %collective-permute-start.10 = (bf16[432,128]{1,0:T(8,128)(2,1)S(1)}, bf16[432,128]{1,0:T(8,128)(2,1)S(1)}, u32[]{:S(2)}, u32[]{:S(2)}) collective-permute-start(bf16[432,128]{1,0:T(8,128)(2,1)S(1)} %get-tuple-element.76), channel_id=1, source_target_pairs={{0,24},{8,16},{16,8},{24,0},{1,25},{9,17},{17,9},{25,1},{2,26},{10... | collective-permute-start | bytes 331784 | tf_op jit(solution)/shard_map/ppermute | solution.py:17
  29.1 1.8 %collective-permute-done.14 = bf16[432,128]{1,0:T(8,128)(2,1)S(1)} collective-permute-done((bf16[432,128]{1,0:T(8,128)(2,1)S(1)}, bf16[432,128]{1,0:T(8,128)(2,1)S(1)}, u32[]{:S(2)}, u32[]{:S(2)}) %collective-permute-start.14) | collective-permute-done | bytes 110624 | tf_op jit(solution)/shard_map/ppermute | solution.py:17
  31.0 1.2 %collective-permute-start.8 = (bf16[432,128]{1,0:T(8,128)(2,1)S(1)}, bf16[432,128]{1,0:T(8,128)(2,1)S(1)}, u32[]{:S(2)}, u32[]{:S(2)}) collective-permute-start(bf16[432,128]{1,0:T(8,128)(2,1)S(1)} %get-tuple-element.80), channel_id=1, source_target_pairs={{0,8},{8,0},{16,24},{24,16},{1,9},{9,1},{17,25},{25,17},{2,10},{10... | collective-permute-start | bytes 331784 | tf_op jit(solution)/shard_map/ppermute | solution.py:17
  32.2 0.2 collective-permute-start.9
  32.4 0.1 add_convert_fusion.1
  32.5 0.1 collective-permute-start.17
  32.6 0.7 %shard_map.101 = bf16[256,128]{1,0:T(8,128)(2,1)} custom-call(s32[8,128]{1,0:T(8,128)S(1)} %get-tuple-element.47.count_ref, f32[256,128]{1,0:T(8,128)S(1)} %get-tuple-element.73.own, bf16[1856,128]{1,0:T(8,128)(2,1)S(1)} %collective-permute-done.6.core.core_in, bf16[128,128]{1,0:T(8,128)(2,1)S(1)} %collective-permute-done.7.cross_in), custom_call_target="tpu_custom_call" | custom-call | flops 1000000000 | bytes 3000000 | tf_op jit(solution)/shard_map/pallas_call | solution.py:361
  33.3 1.9 %collective-permute-done.8 = bf16[432,128]{1,0:T(8,128)(2,1)S(1)} collective-permute-done((bf16[432,128]{1,0:T(8,128)(2,1)S(1)}, bf16[432,128]{1,0:T(8,128)(2,1)S(1)}, u32[]{:S(2)}, u32[]{:S(2)}) %collective-permute-start.8) | collective-permute-done | bytes 110624 | tf_op jit(solution)/shard_map/ppermute | solution.py:17
  35.2 0.9 %collective-permute-done.9 = bf16[432,128]{1,0:T(8,128)(2,1)S(1)} collective-permute-done((bf16[432,128]{1,0:T(8,128)(2,1)S(1)}, bf16[432,128]{1,0:T(8,128)(2,1)S(1)}, u32[]{:S(2)}, u32[]{:S(2)}) %collective-permute-start.9) | collective-permute-done | bytes 110624 | tf_op jit(solution)/shard_map/ppermute | solution.py:17
  36.1 0.1 add_convert_fusion.3
  36.2 0.1 collective-permute-start.11
  36.2 0.2 collective-permute-done.17
  36.5 1.7 %collective-permute-start.18 = (bf16[432,128]{1,0:T(8,128)(2,1)S(1)}, bf16[432,128]{1,0:T(8,128)(2,1)S(1)}, u32[]{:S(2)}, u32[]{:S(2)}) collective-permute-start(bf16[432,128]{1,0:T(8,128)(2,1)S(1)} %add_convert_fusion), channel_id=1, source_target_pairs={{0,4},{1,5},{2,6},{3,7},{4,0},{5,1},{6,2},{7,3},{8,12},{9,13},{10,... | collective-permute-start | bytes 331784 | tf_op jit(solution)/shard_map/ppermute | solution.py:17
  38.2 1.6 %collective-permute-done.11 = bf16[432,128]{1,0:T(8,128)(2,1)S(1)} collective-permute-done((bf16[432,128]{1,0:T(8,128)(2,1)S(1)}, bf16[432,128]{1,0:T(8,128)(2,1)S(1)}, u32[]{:S(2)}, u32[]{:S(2)}) %collective-permute-start.11) | collective-permute-done | bytes 110624 | tf_op jit(solution)/shard_map/ppermute | solution.py:17
  39.9 0.7 %collective-permute-start.12 = (bf16[432,128]{1,0:T(8,128)(2,1)S(1)}, bf16[432,128]{1,0:T(8,128)(2,1)S(1)}, u32[]{:S(2)}, u32[]{:S(2)}) collective-permute-start(bf16[432,128]{1,0:T(8,128)(2,1)S(1)} %add_convert_fusion.2), channel_id=1, source_target_pairs={{0,4},{1,5},{2,6},{3,7},{4,0},{5,1},{6,2},{7,3},{8,12},{9,13},{10,... | collective-permute-start | bytes 331784 | tf_op jit(solution)/shard_map/ppermute | solution.py:17
  40.6 1.7 %collective-permute-done.18 = bf16[432,128]{1,0:T(8,128)(2,1)S(1)} collective-permute-done((bf16[432,128]{1,0:T(8,128)(2,1)S(1)}, bf16[432,128]{1,0:T(8,128)(2,1)S(1)}, u32[]{:S(2)}, u32[]{:S(2)}) %collective-permute-start.18) | collective-permute-done | bytes 110624 | tf_op jit(solution)/shard_map/ppermute | solution.py:17
  42.3 7.6 %collective-permute-start.19 = (f32[432,128]{1,0:T(8,128)S(1)}, f32[432,128]{1,0:T(8,128)S(1)}, u32[]{:S(2)}, u32[]{:S(2)}) collective-permute-start(f32[432,128]{1,0:T(8,128)S(1)} %add_multiply_fusion), channel_id=1, source_target_pairs={{0,1},{1,0},{2,3},{3,2},{4,5},{5,4},{6,7},{7,6},{8,9},{9,8},{10,11... | collective-permute-start | bytes 663560 | tf_op jit(solution)/shard_map/ppermute | solution.py:17
  49.8 0.0 collective-permute-done.12
  49.9 1.2 %collective-permute-start.13 = (f32[432,128]{1,0:T(8,128)S(1)}, f32[432,128]{1,0:T(8,128)S(1)}, u32[]{:S(2)}, u32[]{:S(2)}) collective-permute-start(f32[432,128]{1,0:T(8,128)S(1)} %add_multiply_fusion.1), channel_id=1, source_target_pairs={{0,1},{1,0},{2,3},{3,2},{4,5},{5,4},{6,7},{7,6},{8,9},{9,8},{10,11... | collective-permute-start | bytes 663560 | tf_op jit(solution)/shard_map/ppermute | solution.py:17
  51.0 0.0 collective-permute-done.19
  51.0 0.1 broadcast_select_fusion.1
  51.1 0.8 %pad_maximum_fusion.1 = f32[864,128]{1,0:T(8,128)} fusion(f32[432,128]{1,0:T(8,128)S(1)} %get-tuple-element.91, f32[432,128]{1,0:T(8,128)S(1)} %get-tuple-element.90), kind=kLoop, calls=%fused_computation.1 | loop fusion | flops 110592 | bytes 884736 | tf_op jit(solution)/shard_map/concatenate | solution.py:490
  51.9 0.3 collective-permute-done.13
  52.2 0.8 %pad_maximum_fusion = f32[864,128]{1,0:T(8,128)} fusion(f32[432,128]{1,0:T(8,128)S(1)} %get-tuple-element.93, f32[432,128]{1,0:T(8,128)S(1)} %get-tuple-element.92), kind=kLoop, calls=%fused_computation | loop fusion | flops 110592 | bytes 884736 | tf_op jit(solution)/shard_map/concatenate | solution.py:490
  (19 shorter events, 0.2 us)
Async XLA Ops:
  0.6 4.0 %copy-start.1 = (bf16[27,128,128]{2,1,0:T(8,128)(2,1)S(1)}, bf16[27,128,128]{2,1,0:T(8,128)(2,1)}, u32[]{:S(2)}) copy-start(bf16[27,128,128]{2,1,0:T(8,128)(2,1)} %param.10) | copy-start | bytes 2654212
  0.6 4.0 %copy-start.3 = (bf16[256,128]{1,0:T(8,128)(2,1)S(1)}, bf16[256,128]{1,0:T(8,128)(2,1)}, u32[]{:S(2)}) copy-start(bf16[256,128]{1,0:T(8,128)(2,1)} %features.7) | copy-start | bytes 196612
  1.8 4.0 %collective-permute-start = (bf16[144,128]{1,0:T(8,128)(2,1)S(1)}, bf16[144,128]{1,0:T(8,128)(2,1)S(1)}, u32[]{:S(2)}, u32[]{:S(2)}) collective-permute-start(bf16[144,128]{1,0:T(8,128)(2,1)S(1)} %get-tuple-element.48), channel_id=1, source_target_pairs={{0,1},{1,0},{2,3},{3,2},{4,5},{5,4},{6,7},{7,6},{8,9},{9,8},{10,11... | collective-permute-start | bytes 110600 | tf_op jit(solution)/shard_map/ppermute | solution.py:17
  1.9 4.6 %collective-permute-start.1 = (bf16[144,128]{1,0:T(8,128)(2,1)S(1)}, bf16[144,128]{1,0:T(8,128)(2,1)S(1)}, u32[]{:S(2)}, u32[]{:S(2)}) collective-permute-start(bf16[144,128]{1,0:T(8,128)(2,1)S(1)} %get-tuple-element.49), channel_id=1, source_target_pairs={{0,8},{1,2},{2,1},{3,4},{4,3},{5,6},{6,5},{7,15},{8,0},{9,10},{10,... | collective-permute-start | bytes 110600 | tf_op jit(solution)/shard_map/ppermute | solution.py:30
  6.5 3.3 %copy-start = (bf16[27,128,128]{2,1,0:T(8,128)(2,1)S(1)}, bf16[27,128,128]{2,1,0:T(8,128)(2,1)}, u32[]{:S(2)}) copy-start(bf16[27,128,128]{2,1,0:T(8,128)(2,1)} %param.11) | copy-start | bytes 2654212
  7.8 2.7 %collective-permute-start.2 = (bf16[128,128]{1,0:T(8,128)(2,1)S(1)}, bf16[128,128]{1,0:T(8,128)(2,1)S(1)}, u32[]{:S(2)}, u32[]{:S(2)}) collective-permute-start(bf16[128,128]{1,0:T(8,128)(2,1)S(1)} %get-tuple-element.54), channel_id=1, source_target_pairs={{0,1},{1,0},{2,3},{3,2},{4,5},{5,4},{6,7},{7,6},{8,9},{9,8},{10,11... | collective-permute-start | bytes 98312 | tf_op jit(solution)/shard_map/ppermute | solution.py:17
  8.2 3.6 %collective-permute-start.3 = (bf16[128,128]{1,0:T(8,128)(2,1)S(1)}, bf16[128,128]{1,0:T(8,128)(2,1)S(1)}, u32[]{:S(2)}, u32[]{:S(2)}) collective-permute-start(bf16[128,128]{1,0:T(8,128)(2,1)S(1)} %get-tuple-element.55), channel_id=1, source_target_pairs={{0,8},{1,2},{2,1},{3,4},{4,3},{5,6},{6,5},{7,15},{8,0},{9,10},{10,... | collective-permute-start | bytes 98312 | tf_op jit(solution)/shard_map/ppermute | solution.py:30
  9.8 2.1 %copy-start.2 = (bf16[256,128]{1,0:T(8,128)(2,1)S(1)}, bf16[256,128]{1,0:T(8,128)(2,1)}, u32[]{:S(2)}) copy-start(bf16[256,128]{1,0:T(8,128)(2,1)} %cotangent.1) | copy-start | bytes 196612
  15.5 1.9 %collective-permute-start.4 = (bf16[1856,128]{1,0:T(8,128)(2,1)S(1)}, bf16[1856,128]{1,0:T(8,128)(2,1)S(1)}, u32[]{:S(2)}, u32[]{:S(2)}) collective-permute-start(bf16[1856,128]{1,0:T(8,128)(2,1)S(1)} %get-tuple-element.66), channel_id=1, source_target_pairs={{0,1},{1,0},{2,3},{3,2},{4,5},{5,4},{6,7},{7,6},{8,9},{9,8},{10,11... | collective-permute-start | bytes 1425416 | tf_op jit(solution)/shard_map/ppermute | solution.py:17
  16.0 3.6 %collective-permute-start.5 = (bf16[128,128]{1,0:T(8,128)(2,1)S(1)}, bf16[128,128]{1,0:T(8,128)(2,1)S(1)}, u32[]{:S(2)}, u32[]{:S(2)}) collective-permute-start(bf16[128,128]{1,0:T(8,128)(2,1)S(1)} %get-tuple-element.70), channel_id=1, source_target_pairs={{0,8},{1,2},{2,1},{3,4},{4,3},{5,6},{6,5},{7,15},{8,0},{9,10},{10,... | collective-permute-start | bytes 98312 | tf_op jit(solution)/shard_map/ppermute | solution.py:30
  22.2 3.4 %collective-permute-start.6 = (bf16[1856,128]{1,0:T(8,128)(2,1)S(1)}, bf16[1856,128]{1,0:T(8,128)(2,1)S(1)}, u32[]{:S(2)}, u32[]{:S(2)}) collective-permute-start(bf16[1856,128]{1,0:T(8,128)(2,1)S(1)} %get-tuple-element.74), channel_id=1, source_target_pairs={{0,1},{1,0},{2,3},{3,2},{4,5},{5,4},{6,7},{7,6},{8,9},{9,8},{10,11... | collective-permute-start | bytes 1425416 | tf_op jit(solution)/shard_map/ppermute | solution.py:17
  22.6 9.8 %collective-permute-start.16 = (bf16[432,128]{1,0:T(8,128)(2,1)S(1)}, bf16[432,128]{1,0:T(8,128)(2,1)S(1)}, u32[]{:S(2)}, u32[]{:S(2)}) collective-permute-start(bf16[432,128]{1,0:T(8,128)(2,1)S(1)} %get-tuple-element.67), channel_id=1, source_target_pairs={{0,24},{8,16},{16,8},{24,0},{1,25},{9,17},{17,9},{25,1},{2,26},{10... | collective-permute-start | bytes 331784 | tf_op jit(solution)/shard_map/ppermute | solution.py:17
  25.3 5.7 %collective-permute-start.14 = (bf16[432,128]{1,0:T(8,128)(2,1)S(1)}, bf16[432,128]{1,0:T(8,128)(2,1)S(1)}, u32[]{:S(2)}, u32[]{:S(2)}) collective-permute-start(bf16[432,128]{1,0:T(8,128)(2,1)S(1)} %get-tuple-element.84), channel_id=1, source_target_pairs={{0,8},{8,0},{16,24},{24,16},{1,9},{9,1},{17,25},{25,17},{2,10},{10... | collective-permute-start | bytes 331784 | tf_op jit(solution)/shard_map/ppermute | solution.py:17
  25.6 6.9 %collective-permute-start.15 = (bf16[432,128]{1,0:T(8,128)(2,1)S(1)}, bf16[432,128]{1,0:T(8,128)(2,1)S(1)}, u32[]{:S(2)}, u32[]{:S(2)}) collective-permute-start(bf16[432,128]{1,0:T(8,128)(2,1)S(1)} %get-tuple-element.86), channel_id=1, source_target_pairs={{0,16},{8,24},{16,0},{24,8},{1,17},{9,25},{17,1},{25,9},{2,18},{10... | collective-permute-start | bytes 331784 | tf_op jit(solution)/shard_map/ppermute | solution.py:17
  25.7 6.5 %collective-permute-start.7 = (bf16[128,128]{1,0:T(8,128)(2,1)S(1)}, bf16[128,128]{1,0:T(8,128)(2,1)S(1)}, u32[]{:S(2)}, u32[]{:S(2)}) collective-permute-start(bf16[128,128]{1,0:T(8,128)(2,1)S(1)} %get-tuple-element.78), channel_id=1, source_target_pairs={{0,8},{1,2},{2,1},{3,4},{4,3},{5,6},{6,5},{7,15},{8,0},{9,10},{10,... | collective-permute-start | bytes 98312 | tf_op jit(solution)/shard_map/ppermute | solution.py:30
  27.0 6.3 %collective-permute-start.10 = (bf16[432,128]{1,0:T(8,128)(2,1)S(1)}, bf16[432,128]{1,0:T(8,128)(2,1)S(1)}, u32[]{:S(2)}, u32[]{:S(2)}) collective-permute-start(bf16[432,128]{1,0:T(8,128)(2,1)S(1)} %get-tuple-element.76), channel_id=1, source_target_pairs={{0,24},{8,16},{16,8},{24,0},{1,25},{9,17},{17,9},{25,1},{2,26},{10... | collective-permute-start | bytes 331784 | tf_op jit(solution)/shard_map/ppermute | solution.py:17
  31.0 4.2 %collective-permute-start.8 = (bf16[432,128]{1,0:T(8,128)(2,1)S(1)}, bf16[432,128]{1,0:T(8,128)(2,1)S(1)}, u32[]{:S(2)}, u32[]{:S(2)}) collective-permute-start(bf16[432,128]{1,0:T(8,128)(2,1)S(1)} %get-tuple-element.80), channel_id=1, source_target_pairs={{0,8},{8,0},{16,24},{24,16},{1,9},{9,1},{17,25},{25,17},{2,10},{10... | collective-permute-start | bytes 331784 | tf_op jit(solution)/shard_map/ppermute | solution.py:17
  32.2 3.9 %collective-permute-start.9 = (bf16[432,128]{1,0:T(8,128)(2,1)S(1)}, bf16[432,128]{1,0:T(8,128)(2,1)S(1)}, u32[]{:S(2)}, u32[]{:S(2)}) collective-permute-start(bf16[432,128]{1,0:T(8,128)(2,1)S(1)} %get-tuple-element.81), channel_id=1, source_target_pairs={{0,16},{8,24},{16,0},{24,8},{1,17},{9,25},{17,1},{25,9},{2,18},{10... | collective-permute-start | bytes 331784 | tf_op jit(solution)/shard_map/ppermute | solution.py:17
  32.5 4.0 %collective-permute-start.17 = (bf16[432,128]{1,0:T(8,128)(2,1)S(1)}, bf16[432,128]{1,0:T(8,128)(2,1)S(1)}, u32[]{:S(2)}, u32[]{:S(2)}) collective-permute-start(bf16[432,128]{1,0:T(8,128)(2,1)S(1)} %add_convert_fusion.1), channel_id=1, source_target_pairs={{0,2},{1,3},{2,0},{3,1},{4,6},{5,7},{6,4},{7,5},{8,10},{9,11},{10,... | collective-permute-start | bytes 331784 | tf_op jit(solution)/shard_map/ppermute | solution.py:17
  36.2 3.7 %collective-permute-start.11 = (bf16[432,128]{1,0:T(8,128)(2,1)S(1)}, bf16[432,128]{1,0:T(8,128)(2,1)S(1)}, u32[]{:S(2)}, u32[]{:S(2)}) collective-permute-start(bf16[432,128]{1,0:T(8,128)(2,1)S(1)} %add_convert_fusion.3), channel_id=1, source_target_pairs={{0,2},{1,3},{2,0},{3,1},{4,6},{5,7},{6,4},{7,5},{8,10},{9,11},{10,... | collective-permute-start | bytes 331784 | tf_op jit(solution)/shard_map/ppermute | solution.py:17
  36.5 5.7 %collective-permute-start.18 = (bf16[432,128]{1,0:T(8,128)(2,1)S(1)}, bf16[432,128]{1,0:T(8,128)(2,1)S(1)}, u32[]{:S(2)}, u32[]{:S(2)}) collective-permute-start(bf16[432,128]{1,0:T(8,128)(2,1)S(1)} %add_convert_fusion), channel_id=1, source_target_pairs={{0,4},{1,5},{2,6},{3,7},{4,0},{5,1},{6,2},{7,3},{8,12},{9,13},{10,... | collective-permute-start | bytes 331784 | tf_op jit(solution)/shard_map/ppermute | solution.py:17
  39.9 9.9 %collective-permute-start.12 = (bf16[432,128]{1,0:T(8,128)(2,1)S(1)}, bf16[432,128]{1,0:T(8,128)(2,1)S(1)}, u32[]{:S(2)}, u32[]{:S(2)}) collective-permute-start(bf16[432,128]{1,0:T(8,128)(2,1)S(1)} %add_convert_fusion.2), channel_id=1, source_target_pairs={{0,4},{1,5},{2,6},{3,7},{4,0},{5,1},{6,2},{7,3},{8,12},{9,13},{10,... | collective-permute-start | bytes 331784 | tf_op jit(solution)/shard_map/ppermute | solution.py:17
  42.3 8.8 %collective-permute-start.19 = (f32[432,128]{1,0:T(8,128)S(1)}, f32[432,128]{1,0:T(8,128)S(1)}, u32[]{:S(2)}, u32[]{:S(2)}) collective-permute-start(f32[432,128]{1,0:T(8,128)S(1)} %add_multiply_fusion), channel_id=1, source_target_pairs={{0,1},{1,0},{2,3},{3,2},{4,5},{5,4},{6,7},{7,6},{8,9},{9,8},{10,11... | collective-permute-start | bytes 663560 | tf_op jit(solution)/shard_map/ppermute | solution.py:17
  49.9 2.3 %collective-permute-start.13 = (f32[432,128]{1,0:T(8,128)S(1)}, f32[432,128]{1,0:T(8,128)S(1)}, u32[]{:S(2)}, u32[]{:S(2)}) collective-permute-start(f32[432,128]{1,0:T(8,128)S(1)} %add_multiply_fusion.1), channel_id=1, source_target_pairs={{0,1},{1,0},{2,3},{3,2},{4,5},{5,4},{6,7},{7,6},{8,9},{9,8},{10,11... | collective-permute-start | bytes 663560 | tf_op jit(solution)/shard_map/ppermute | solution.py:17

commit v6 on v5

--- a/solution.py
+++ b/solution.py
@@ -175,28 +175,36 @@
             singles_turned[side * per + i] = by_sources(near, at, blk)
 
 
-def pull_back(far_turned, pairs_turned, singles_turned, grads, weights, sources, pulled, wgrad):
+def pull(far_turned, pairs_turned, singles_turned, grads, pulled, kind):
     per, channels = pairs_turned.shape[0], grads.shape[1]
-    sums = []
-    for kind in range(KINDS):
-        base = kind * per * channels
-        for i in range(per):
-            if kind == 1:
-                select = pairs_turned[i]
-            else:
-                side = (kind // 2) * per + i
-                select = jnp.concatenate([far_turned[side], singles_turned[side]], axis=0)
-            got = jnp.dot(select, grads, preferred_element_type=F32)
-            at = base + i * channels
-            pulled[:, at : at + channels] = got.astype(BF16)
-        held = pulled[:, base : base + per * channels]
-        wide = weights_of(weights, kind, per, 1)
-        sums.append(lax.dot_general(held, wide, NT, preferred_element_type=F32))
-        terms = jnp.dot(sources[kind].T, held, preferred_element_type=F32)
-        for i in range(per):
-            at = (i * KINDS + kind) * channels
-            wgrad[at : at + channels, :] = terms[:, i * channels : (i + 1) * channels]
-    return sums
+    for i in range(per):
+        if kind == 1:
+            select = pairs_turned[i]
+        else:
+            side = (kind // 2) * per + i
+            select = jnp.concatenate([far_turned[side], singles_turned[side]], axis=0)
+        got = jnp.dot(select, grads, preferred_element_type=F32)
+        at = (kind * per + i) * channels
+        pulled[:, at : at + channels] = got.astype(BF16)
+
+
+def of_kind_in(pulled, kind):
+    wide = pulled.shape[1] // KINDS
+    return pulled[:, kind * wide : (kind + 1) * wide]
+
+
+def source_sums(pulled, weights, kind):
+    per = weights.shape[0] // weights.shape[1] // KINDS
+    wide = weights_of(weights, kind, per, 1)
+    return lax.dot_general(of_kind_in(pulled, kind), wide, NT, preferred_element_type=F32)
+
+
+def weight_sums(pulled, source, wgrad, kind):
+    channels = wgrad.shape[1]
+    terms = jnp.dot(source.T, of_kind_in(pulled, kind), preferred_element_type=F32)
+    for i in range(terms.shape[1] // channels):
+        at = (i * KINDS + kind) * channels
+        wgrad[at : at + channels, :] = terms[:, i * channels : (i + 1) * channels]
 
 
 def split_sums(sums, both, blk):
@@ -278,9 +286,11 @@
     grads = (cotangent[...].astype(F32) * grad * mask).astype(BF16)
     grads_out[...] = grads
     sources = [low, hidden[...], high]
-    sums = pull_back(
-        far_turned, pairs_turned, singles_turned, grads, weights, sources, pulled, wgrad
-    )
+    sums = []
+    for kind in range(KINDS):
+        pull(far_turned, pairs_turned, singles_turned, grads, pulled, kind)
+        sums.append(source_sums(pulled, weights, kind))
+        weight_sums(pulled, sources[kind], wgrad, kind)
     own, to_next, to_prev = split_sums(sums, both, blk)
     own_out[...] = own
     core, cross = exchange_sides(odd, to_next, to_prev)
@@ -297,9 +307,9 @@
 
 
 def third_kernel(
-    count_ref, features, halo, own, core_in, cross_in, slope, grads_in, weights,
+    count_ref, features, halo, own, core_in, cross_in, slope,
     far_turned, pairs_turned, singles_turned,
-    own_out, keep, core_out, cross_out, pulled, wgrad,
+    pulled, keep, core_out, wgrad,
 ):
     blk = features.shape[0] // 2
     both = count_ref[:1, :] == 2
@@ -312,22 +322,30 @@
         features[...],
         jnp.concatenate([halo[1], features[:blk, :]], axis=0),
     ]
-    sums = pull_back(
-        far_turned, pairs_turned, singles_turned, grads, weights, sources, pulled, wgrad
-    )
-    own_sum, to_next, to_prev = split_sums(sums, both, blk)
-    own_out[...] = own_sum + grads_in[...].astype(F32)
+    for kind in range(KINDS):
+        pull(far_turned, pairs_turned, singles_turned, grads, pulled, kind)
+    for kind in range(KINDS):
+        weight_sums(pulled, sources[kind], wgrad, kind)
+    halves_out(odd, wgrad, keep, core_out, 0)
+
+
+def fourth_kernel(count_ref, pulled, weights, grads_in, own_out, core_out, cross_out):
+    blk = grads_in.shape[0] // 2
+    both = count_ref[:1, :] == 2
+    odd, _, _ = place()
+    sums = [source_sums(pulled, weights, kind) for kind in range(KINDS)]
+    own, to_next, to_prev = split_sums(sums, both, blk)
+    own_out[...] = own + grads_in[...].astype(F32)
     core, cross = exchange_sides(odd, to_next, to_prev)
-    core_out[:blk, :] = core.astype(BF16)
+    core_out[...] = core.astype(BF16)
     cross_out[...] = cross.astype(BF16)
-    halves_out(odd, wgrad, keep, core_out, blk)
 
 
 def last_kernel(count_ref, own, core_in, cross_in, input_grad):
     blk = own.shape[0] // 2
     both = count_ref[:1, :] == 2
     odd, _, _ = place()
-    core, cross = core_in[:blk, :].astype(F32), cross_in[...].astype(F32)
+    core, cross = core_in[...].astype(F32), cross_in[...].astype(F32)
     input_grad[...] = joined(own[...], odd, both, core, cross, blk).astype(BF16)
 
 
@@ -347,6 +365,11 @@
 
 def after(first, later):
     return lax.optimization_barrier((first, later))[1]
+
+
+def either_order(second, mine, other):
+    parts = [jnp.where(second, other, mine), jnp.where(second, mine, other)]
+    return jnp.concatenate(parts, axis=0)
 
 
 def added(value, others):
@@ -451,47 +474,50 @@
     mine_two, *sends_two = call(shards_kernel, shards, keep_two, core_two)
     got_two = [swapped(send, "grp", d + 1) for d, send in enumerate(sends_two)]
     own = after(sends_two[-1], own)
-    own, keep_one, core_one, cross = call(
+    held, keep_one, core_one = call(
         third_kernel,
-        [summed, keep_shape, core_shape, block],
-        count, features, halo, own, core_two, cross, slope, grad_sum, flat_one,
+        [pulled, keep_shape, ((n_grp * slot, channels), BF16)],
+        count, features, halo, own, core_two, cross, slope,
         far_turned, pairs_turned, singles_turned,
-        scratch=[pulled, wgrad],
-        micros=3,
+        scratch=[wgrad],
+        micros=2,
     )
     core_one = swapped(core_one, "tile", 1)
     mine_one, *sends_one = call(shards_kernel, shards, keep_one, core_one)
     got_one = [swapped(send, "grp", d + 1) for d, send in enumerate(sends_one)]
-    cross = crossed(after(sends_one[-1], cross))
-    got_two = [after(cross, got) for got in got_two]
+    own, core, cross = call(
+        fourth_kernel,
+        [summed, block, block],
+        count, after(sends_one[-1], held), flat_one, grad_sum,
+    )
     two = added(mine_two, got_two).astype(BF16)
     steps = [1 << b for b in range(1, (n_tile - 1).bit_length())]
-    other_two = swapped(two, "tile", steps[0])
+    other_two = swapped(two, "tile", steps[-1])
     one = added(mine_one, got_one).astype(BF16)
-    one = after(cross, one)
-    (input_grad,) = call(last_kernel, [field], count, own, core_one, cross)
     for at, bits in enumerate(steps):
         other_one = swapped(one, "tile", bits)
         two = added(two, [other_two])
         if at + 1 < len(steps):
-            two = after(one, two.astype(BF16))
-            other_two = swapped(two, "tile", steps[at + 1])
+            two = two.astype(BF16)
+            two = after(one, two)
+            other_two = swapped(two, "tile", steps[-2 - at])
             one = added(one, [other_one]).astype(BF16)
-        else:
-            one = added(one, [other_one])
-    voxel_total = n_grp * n_tile * rows
-    scale = float(voxel_total) ** (-0.5)
+            if at == 0:
+                one, core, cross = lax.optimization_barrier((one, core, cross))
+    cross, core = crossed(cross), swapped(core, "tile", 1)
+    (input_grad,) = call(last_kernel, [field], count, own, core, cross)
+    scale = float(n_grp * n_tile * rows) ** (-0.5)
     odd = lax.axis_index("tile") % 2 == 1
-    outs = []
-    for half_sum in (one, two):
-        half_sum = half_sum[:half] * scale
-        other = swapped(half_sum, "tile", 1)
-        outs.append(
-            jnp.concatenate(
-                [jnp.where(odd, other, half_sum), jnp.where(odd, half_sum, other)], axis=0
-            )
-        )
-    return (result, input_grad, outs[0], outs[1])
+
+    def finished(part):
+        part = part[:half]
+        other = swapped(part, "tile", 1)
+        return either_order(odd, part.astype(F32) * scale, other.astype(F32) * scale)
+
+    other_one = after(cross, other_one)
+    two = finished(two.astype(BF16))
+    one = finished(added(one, [other_one]).astype(BF16))
+    return (result, input_grad, one, two)
 
 
 def solution(mesh):

time: 53.4 us -> 51.7 us (0.968)
  starting transfers between devices: 25.9 us -> 24.4 us
    ppermute x16 -> x17, starting transfers between devices: 19.3 us -> 15 us  [swapped(): lax.ppermute(value, axis, [(i, i ^ bits) for i in range(count) if i ^ bit...]
    ppermute x4, starting transfers between devices: 6.56 us -> 9.41 us  [crossed(): return lax.ppermute(value, ('grp', 'tile'), pairs)]
    pallas_call x9 -> x10, Pallas kernels: 11.3 us -> 11.1 us  [call(): pl.pallas_call(kernel, out_shape=[jax.ShapeDtypeStruct(shape, kind) for s...]
    ppermute x16 -> x17, waiting for transfers between devices: 8.95 us -> 8.83 us  [swapped(): lax.ppermute(value, axis, [(i, i ^ bits) for i in range(count) if i ^ bit...]
  transfers between devices with their start and end apart: 20 -> 21, of which waited for: 11 -> 11; matrix products, arithmetic and copies ran while one was open for 2% -> 1% of each run, Pallas kernels for 5% -> 6%
where the time goes in v6:
time: 51.7 us; the launch traced here: 51.2 us
  starting transfers between devices  24.4 us (47%)
  waiting for transfers between devices  13 us (25%)
  Pallas kernels  11.1 us (21%)
  other arithmetic  1.95 us (4%)
  between operations  0.78 us (2%)
    ppermute x17, starting transfers between devices, swapped(): lax.ppermute(value, axis, [(i, i ^ bits) for i in range(count) if i ^ bit...  15 us
    pallas_call x10, Pallas kernels, call(): pl.pallas_call(kernel, out_shape=[jax.ShapeDtypeStruct(shape, kind) for s...  11.1 us
    ppermute x4, starting transfers between devices, crossed(): return lax.ppermute(value, ('grp', 'tile'), pairs)  9.41 us
    ppermute x17, waiting for transfers between devices, swapped(): lax.ppermute(value, axis, [(i, i ^ bits) for i in range(count) if i ^ bit...  8.83 us
    ppermute x4, waiting for transfers between devices, crossed(): return lax.ppermute(value, ('grp', 'tile'), pairs)  4.14 us
    concatenate x2, other arithmetic, either_order(): return jnp.concatenate(parts, axis=0)  1.58 us
  transfers between devices with their start and end apart: 21, of which 11 were waited for; matrix products, arithmetic and copies ran while one was open for 1% of the time, Pallas kernels for 6%

profile of v6, /device:TPU:1, one launch (start us, length us, event | category | flops | bytes accessed | tf_op | source)
XLA Modules:
  0.0 51.2 jit_solution(11024067593720187567)
XLA Ops:
  0.7 1.1 %shard_map.93 = (f32[40,128]{1,0:T(8,128)S(1)}, bf16[144,128]{1,0:T(8,128)(2,1)S(1)}, bf16[144,128]{1,0:T(8,128)(2,1)S(1)}, s32[8,128]{1,0:T(8,128)S(1)}) custom-call(bf16[256,128]{1,0:T(8,128)(2,1)} %features.7, s32[27,2,128]{2,1,0:T(2,128)} %rows_in.1, s32[2,27]{1,0:T(2,128)} %bitcast.8), custom_call_target="tpu_custom_call" | custom-call | flops 3000000000 | bytes 9000000 | tf_op jit(solution)/shard_map/pallas_call | solution.py:384
  1.8 0.1 collective-permute-start
  1.9 2.7 %collective-permute-start.1 = (bf16[144,128]{1,0:T(8,128)(2,1)S(1)}, bf16[144,128]{1,0:T(8,128)(2,1)S(1)}, u32[]{:S(2)}, u32[]{:S(2)}) collective-permute-start(bf16[144,128]{1,0:T(8,128)(2,1)S(1)} %get-tuple-element.51), channel_id=1, source_target_pairs={{0,8},{1,2},{2,1},{3,4},{4,3},{5,6},{6,5},{7,15},{8,0},{9,10},{10,... | collective-permute-start | bytes 110600 | tf_op jit(solution)/shard_map/ppermute | solution.py:30
  4.6 1.1 %shard_map.94 = (bf16[9,256,256]{2,1,0:T(8,128)(2,1)S(1)}, bf16[18,256,128]{2,1,0:T(8,128)(2,1)S(1)}, bf16[9,256,256]{2,1,0:T(8,128)(2,1)S(1)}, bf16[18,128,256]{2,1,0:T(8,128)(2,1)S(1)}, f32[256,128]{1,0:T(8,128)S(1)}) custom-call(f32[40,128]{1,0:T(8,128)S(1)} %get-tuple-element.52.near, bf16[256,128]{1,0:T(8,128)(2,1)S(1)} %copy-done.3, ...), custom_call_target="tpu_custom_call" | custom-call | flops 2000000000 | bytes 6000000 | tf_op jit(solution)/shard_map/pallas_call | solution.py:384
  5.7 0.0 collective-permute-done.core_in
  5.8 0.7 %collective-permute-done.1.cross_in = bf16[144,128]{1,0:T(8,128)(2,1)S(1)} collective-permute-done((bf16[144,128]{1,0:T(8,128)(2,1)S(1)}, bf16[144,128]{1,0:T(8,128)(2,1)S(1)}, u32[]{:S(2)}, u32[]{:S(2)}) %collective-permute-start.1) | collective-permute-done | bytes 36896 | tf_op jit(solution)/shard_map/ppermute | solution.py:30
  6.5 1.3 %shard_map.95 = (f32[24,128]{1,0:T(8,128)S(1)}, bf16[18,256,128]{2,1,0:T(8,128)(2,1)S(1)}, bf16[2,128,128]{2,1,0:T(8,128)(2,1)S(1)}, bf16[256,128]{1,0:T(8,128)(...) custom-call(s32[8,128]{1,0:T(8,128)S(1)} %get-tuple-element.49.count_ref, ...), custom_call_target="tpu_custom_call" | custom-call | flops 2000000000 | bytes 6000000 | tf_op jit(solution)/shard_map/pallas_call | solution.py:384
  7.8 0.5 collective-permute-start.2
  8.2 1.6 %collective-permute-start.3 = (bf16[128,128]{1,0:T(8,128)(2,1)S(1)}, bf16[128,128]{1,0:T(8,128)(2,1)S(1)}, u32[]{:S(2)}, u32[]{:S(2)}) collective-permute-start(bf16[128,128]{1,0:T(8,128)(2,1)S(1)} %get-tuple-element.57), channel_id=1, source_target_pairs={{0,8},{1,2},{2,1},{3,4},{4,3},{5,6},{6,5},{7,15},{8,0},{9,10},{10,... | collective-permute-start | bytes 98312 | tf_op jit(solution)/shard_map/ppermute | solution.py:30
  9.8 0.7 %shard_map.96 = (f32[256,128]{1,0:T(8,128)S(1)}, bf16[18,128,256]{2,1,0:T(8,128)(2,1)S(1)}) custom-call(bf16[256,128]{1,0:T(8,128)(2,1)S(1)} %get-tuple-element.55.hidden, bf16[9,256,256]{2,1,0:T(8,128)(2,1)S(1)} %get-tuple-element.59.pairs, f32[24,128]{1,0:T(8,128)S(1)} %get-tuple-element.60.entries, bf16[3456,128]{1,0:T(8,128)(2,1)S(1)} %bitcast.3), custom_call_target="tpu_custom_call" | custom-call | flops 1000000000 | bytes 3000000 | tf_op jit(solution)/shard_map/pallas_call | solution.py:384
  10.5 0.0 collective-permute-done.2.core_in
  10.5 1.4 %collective-permute-done.3.cross_in = bf16[128,128]{1,0:T(8,128)(2,1)S(1)} collective-permute-done((bf16[128,128]{1,0:T(8,128)(2,1)S(1)}, bf16[128,128]{1,0:T(8,128)(2,1)S(1)}, u32[]{:S(2)}, u32[]{:S(2)}) %collective-permute-start.3) | collective-permute-done | bytes 32800 | tf_op jit(solution)/shard_map/ppermute | solution.py:30
  11.9 3.7 %shard_map.97 = (bf16[256,128]{1,0:T(8,128)(2,1)}, bf16[256,128]{1,0:T(8,128)(2,1)S(1)}, f32[256,128]{1,0:T(8,128)S(1)}, f32[4,432,128]{2,1,0:T(8,128)S(1)}, bf1...) custom-call(s32[8,128]{1,0:T(8,128)S(1)} %get-tuple-element.49.count_ref, bf16[256,128]{1,0:T(8,128)(2,1)S(1)} %copy-done.3, ...), custom_call_target="tpu_custom_call" | custom-call | flops 4000000000 | bytes 12000000 | tf_op jit(solution)/shard_map/pallas_call | solution.py:384
  15.6 0.4 collective-permute-start.4
  16.0 1.0 %collective-permute-start.5 = (bf16[128,128]{1,0:T(8,128)(2,1)S(1)}, bf16[128,128]{1,0:T(8,128)(2,1)S(1)}, u32[]{:S(2)}, u32[]{:S(2)}) collective-permute-start(bf16[128,128]{1,0:T(8,128)(2,1)S(1)} %get-tuple-element.72), channel_id=1, source_target_pairs={{0,8},{1,2},{2,1},{3,4},{4,3},{5,6},{6,5},{7,15},{8,0},{9,10},{10,... | collective-permute-start | bytes 98312 | tf_op jit(solution)/shard_map/ppermute | solution.py:30
  17.0 0.4 collective-permute-done.4.core.core_in
  17.5 0.1 shard_map.98
  17.6 2.1 %collective-permute-done.5.cross_in = bf16[128,128]{1,0:T(8,128)(2,1)S(1)} collective-permute-done((bf16[128,128]{1,0:T(8,128)(2,1)S(1)}, bf16[128,128]{1,0:T(8,128)(2,1)S(1)}, u32[]{:S(2)}, u32[]{:S(2)}) %collective-permute-start.5) | collective-permute-done | bytes 32800 | tf_op jit(solution)/shard_map/ppermute | solution.py:30
  19.6 1.7 %shard_map.99 = (bf16[256,3456]{1,0:T(8,128)(2,1)S(1)}, f32[4,432,128]{2,1,0:T(8,128)S(1)}, bf16[1728,128]{1,0:T(8,128)(2,1)S(1)}) custom-call(s32[8,128]{1,0:T(8,128)S(1)} %get-tuple-element.49.count_ref, bf16[256,128]{1,0:T(8,128)(2,1)S(1)} %copy-done.3, bf16[2,128,128]{2,1,0:T(8,128)(2,1)S(1)} %get-tuple-element.66.halo, ...), custom_call_target="tpu_custom_call" | custom-call | flops 2000000000 | bytes 6000000 | tf_op jit(solution)/shard_map/pallas_call | solution.py:384
  21.3 0.5 collective-permute-start.6
  21.8 1.8 %collective-permute-start.15 = (bf16[432,128]{1,0:T(8,128)(2,1)S(1)}, bf16[432,128]{1,0:T(8,128)(2,1)S(1)}, u32[]{:S(2)}, u32[]{:S(2)}) collective-permute-start(bf16[432,128]{1,0:T(8,128)(2,1)S(1)} %get-tuple-element.91), channel_id=1, source_target_pairs={{0,8},{8,0},{16,24},{24,16},{1,9},{9,1},{17,25},{25,17},{2,10},{10... | collective-permute-start | bytes 331784 | tf_op jit(solution)/shard_map/ppermute | solution.py:17
  23.5 1.2 %collective-permute-start.16 = (bf16[432,128]{1,0:T(8,128)(2,1)S(1)}, bf16[432,128]{1,0:T(8,128)(2,1)S(1)}, u32[]{:S(2)}, u32[]{:S(2)}) collective-permute-start(bf16[432,128]{1,0:T(8,128)(2,1)S(1)} %get-tuple-element.92), channel_id=1, source_target_pairs={{0,16},{8,24},{16,0},{24,8},{1,17},{9,25},{17,1},{25,9},{2,18},{10... | collective-permute-start | bytes 331784 | tf_op jit(solution)/shard_map/ppermute | solution.py:17
  24.8 0.1 shard_map.100
  24.9 1.5 %collective-permute-start.7 = (bf16[432,128]{1,0:T(8,128)(2,1)S(1)}, bf16[432,128]{1,0:T(8,128)(2,1)S(1)}, u32[]{:S(2)}, u32[]{:S(2)}) collective-permute-start(bf16[432,128]{1,0:T(8,128)(2,1)S(1)} %get-tuple-element.82), channel_id=1, source_target_pairs={{0,8},{8,0},{16,24},{24,16},{1,9},{9,1},{17,25},{25,17},{2,10},{10... | collective-permute-start | bytes 331784 | tf_op jit(solution)/shard_map/ppermute | solution.py:17
  26.4 1.2 %collective-permute-start.8 = (bf16[432,128]{1,0:T(8,128)(2,1)S(1)}, bf16[432,128]{1,0:T(8,128)(2,1)S(1)}, u32[]{:S(2)}, u32[]{:S(2)}) collective-permute-start(bf16[432,128]{1,0:T(8,128)(2,1)S(1)} %get-tuple-element.83), channel_id=1, source_target_pairs={{0,16},{8,24},{16,0},{24,8},{1,17},{9,25},{17,1},{25,9},{2,18},{10... | collective-permute-start | bytes 331784 | tf_op jit(solution)/shard_map/ppermute | solution.py:17
  27.6 1.5 %collective-permute-start.9 = (bf16[432,128]{1,0:T(8,128)(2,1)S(1)}, bf16[432,128]{1,0:T(8,128)(2,1)S(1)}, u32[]{:S(2)}, u32[]{:S(2)}) collective-permute-start(bf16[432,128]{1,0:T(8,128)(2,1)S(1)} %get-tuple-element.76), channel_id=1, source_target_pairs={{0,24},{8,16},{16,8},{24,0},{1,25},{9,17},{17,9},{25,1},{2,26},{10... | collective-permute-start | bytes 331784 | tf_op jit(solution)/shard_map/ppermute | solution.py:17
  29.1 0.6 %collective-permute-done.17 = bf16[432,128]{1,0:T(8,128)(2,1)S(1)} collective-permute-done((bf16[432,128]{1,0:T(8,128)(2,1)S(1)}, bf16[432,128]{1,0:T(8,128)(2,1)S(1)}, u32[]{:S(2)}, u32[]{:S(2)}) %collective-permute-start.17) | collective-permute-done | bytes 110624 | tf_op jit(solution)/shard_map/ppermute | solution.py:17
  29.7 0.1 add_convert_fusion.2
  29.8 0.6 %collective-permute-start.18 = (bf16[432,128]{1,0:T(8,128)(2,1)S(1)}, bf16[432,128]{1,0:T(8,128)(2,1)S(1)}, u32[]{:S(2)}, u32[]{:S(2)}) collective-permute-start(bf16[432,128]{1,0:T(8,128)(2,1)S(1)} %add_convert_fusion.2), channel_id=1, source_target_pairs={{0,4},{1,5},{2,6},{3,7},{4,0},{5,1},{6,2},{7,3},{8,12},{9,13},{10,... | collective-permute-start | bytes 331784 | tf_op jit(solution)/shard_map/ppermute | solution.py:17
  30.4 0.8 %collective-permute-done.7 = bf16[432,128]{1,0:T(8,128)(2,1)S(1)} collective-permute-done((bf16[432,128]{1,0:T(8,128)(2,1)S(1)}, bf16[432,128]{1,0:T(8,128)(2,1)S(1)}, u32[]{:S(2)}, u32[]{:S(2)}) %collective-permute-start.7) | collective-permute-done | bytes 110624 | tf_op jit(solution)/shard_map/ppermute | solution.py:17
  31.1 2.8 %collective-permute-done.8 = bf16[432,128]{1,0:T(8,128)(2,1)S(1)} collective-permute-done((bf16[432,128]{1,0:T(8,128)(2,1)S(1)}, bf16[432,128]{1,0:T(8,128)(2,1)S(1)}, u32[]{:S(2)}, u32[]{:S(2)}) %collective-permute-start.8) | collective-permute-done | bytes 110624 | tf_op jit(solution)/shard_map/ppermute | solution.py:17
  34.0 0.5 collective-permute-done.9
  34.5 0.1 add_convert_fusion.5
  34.5 0.1 collective-permute-start.10
  34.6 0.5 collective-permute-done.18
  35.1 0.6 %shard_map.101 = (f32[256,128]{1,0:T(8,128)S(1)}, bf16[128,128]{1,0:T(8,128)(2,1)S(1)}, bf16[128,128]{1,0:T(8,128)(2,1)S(1)}) custom-call(s32[8,128]{1,0:T(8,128)S(1)} %get-tuple-element.49.count_ref, bf16[256,3456]{1,0:T(8,128)(2,1)S(1)} %get-tuple-element.78.pulled, bf16[3456,128]{1,0:T(8,128)(2,1)S(1)} %bitcast.7, ...), custom_call_target="tpu_custom_call" | custom-call | flops 1000000000 | bytes 3000000 | tf_op jit(solution)/shard_map/pallas_call | solution.py:384
  35.8 1.0 %collective-permute-start.19 = (bf16[432,128]{1,0:T(8,128)(2,1)S(1)}, bf16[432,128]{1,0:T(8,128)(2,1)S(1)}, u32[]{:S(2)}, u32[]{:S(2)}) collective-permute-start(bf16[432,128]{1,0:T(8,128)(2,1)S(1)} %add_convert_fusion.1), channel_id=1, source_target_pairs={{0,2},{1,3},{2,0},{3,1},{4,6},{5,7},{6,4},{7,5},{8,10},{9,11},{10,... | collective-permute-start | bytes 331784 | tf_op jit(solution)/shard_map/ppermute | solution.py:17
  36.8 2.9 %collective-permute-done.10 = bf16[432,128]{1,0:T(8,128)(2,1)S(1)} collective-permute-done((bf16[432,128]{1,0:T(8,128)(2,1)S(1)}, bf16[432,128]{1,0:T(8,128)(2,1)S(1)}, u32[]{:S(2)}, u32[]{:S(2)}) %collective-permute-start.10) | collective-permute-done | bytes 110624 | tf_op jit(solution)/shard_map/ppermute | solution.py:17
  39.7 0.1 collective-permute-start.13
  39.8 4.1 %collective-permute-start.12 = (bf16[128,128]{1,0:T(8,128)(2,1)S(1)}, bf16[128,128]{1,0:T(8,128)(2,1)S(1)}, u32[]{:S(2)}, u32[]{:S(2)}) collective-permute-start(bf16[128,128]{1,0:T(8,128)(2,1)S(1)} %get-tuple-element.87), channel_id=1, source_target_pairs={{0,8},{1,2},{2,1},{3,4},{4,3},{5,6},{6,5},{7,15},{8,0},{9,10},{10,... | collective-permute-start | bytes 98312 | tf_op jit(solution)/shard_map/ppermute | solution.py:30
  44.0 2.1 %collective-permute-start.20 = (bf16[432,128]{1,0:T(8,128)(2,1)S(1)}, bf16[432,128]{1,0:T(8,128)(2,1)S(1)}, u32[]{:S(2)}, u32[]{:S(2)}) collective-permute-start(bf16[432,128]{1,0:T(8,128)(2,1)S(1)} %add_convert_fusion), channel_id=1, source_target_pairs={{0,1},{1,0},{2,3},{3,2},{4,5},{5,4},{6,7},{7,6},{8,9},{9,8},{10,11... | collective-permute-start | bytes 331784 | tf_op jit(solution)/shard_map/ppermute | solution.py:17
  46.1 0.1 collective-permute-start.11
  46.2 2.3 %collective-permute-start.14 = (bf16[432,128]{1,0:T(8,128)(2,1)S(1)}, bf16[432,128]{1,0:T(8,128)(2,1)S(1)}, u32[]{:S(2)}, u32[]{:S(2)}) collective-permute-start(bf16[432,128]{1,0:T(8,128)(2,1)S(1)} %add_convert_fusion.3), channel_id=1, source_target_pairs={{0,1},{1,0},{2,3},{3,2},{4,5},{5,4},{6,7},{7,6},{8,9},{9,8},{10,11... | collective-permute-start | bytes 331784 | tf_op jit(solution)/shard_map/ppermute | solution.py:17
  48.6 0.7 %shard_map.102 = bf16[256,128]{1,0:T(8,128)(2,1)} custom-call(s32[8,128]{1,0:T(8,128)S(1)} %get-tuple-element.49.count_ref, f32[256,128]{1,0:T(8,128)S(1)} %get-tuple-element.80.own, bf16[128,128]{1,0:T(8,128)(2,1)S(1)} %collective-permute-done.11.core_in, bf16[128,128]{1,0:T(8,128)(2,1)S(1)} %collective-permute-done.12.cross_in), custom_call_target="tpu_custom_call" | custom-call | flops 1000000000 | bytes 3000000 | tf_op jit(solution)/shard_map/pallas_call | solution.py:384
  49.2 0.3 collective-permute-done.14
  49.5 0.1 fusion.1
  49.6 0.8 %pad_maximum_fusion.1 = f32[864,128]{1,0:T(8,128)} fusion(f32[432,128]{1,0:T(8,128)S(1)} %get-tuple-element.95, f32[432,128]{1,0:T(8,128)S(1)} %get-tuple-element.94), kind=kLoop, calls=%fused_computation.1 | loop fusion | flops 110592 | bytes 884736 | tf_op jit(solution)/shard_map/concatenate | solution.py:372
  50.4 0.8 %pad_maximum_fusion = f32[864,128]{1,0:T(8,128)} fusion(f32[432,128]{1,0:T(8,128)S(1)} %get-tuple-element.98, f32[432,128]{1,0:T(8,128)S(1)} %get-tuple-element.99), kind=kLoop, calls=%fused_computation | loop fusion | flops 110592 | bytes 884736 | tf_op jit(solution)/shard_map/concatenate | solution.py:372
  (21 shorter events, 0.2 us)
Async XLA Ops:
  0.6 4.0 %copy-start.1 = (bf16[27,128,128]{2,1,0:T(8,128)(2,1)S(1)}, bf16[27,128,128]{2,1,0:T(8,128)(2,1)}, u32[]{:S(2)}) copy-start(bf16[27,128,128]{2,1,0:T(8,128)(2,1)} %param.10) | copy-start | bytes 2654212
  0.6 4.0 %copy-start.3 = (bf16[256,128]{1,0:T(8,128)(2,1)S(1)}, bf16[256,128]{1,0:T(8,128)(2,1)}, u32[]{:S(2)}) copy-start(bf16[256,128]{1,0:T(8,128)(2,1)} %features.7) | copy-start | bytes 196612
  1.8 4.0 %collective-permute-start = (bf16[144,128]{1,0:T(8,128)(2,1)S(1)}, bf16[144,128]{1,0:T(8,128)(2,1)S(1)}, u32[]{:S(2)}, u32[]{:S(2)}) collective-permute-start(bf16[144,128]{1,0:T(8,128)(2,1)S(1)} %get-tuple-element.50), channel_id=1, source_target_pairs={{0,1},{1,0},{2,3},{3,2},{4,5},{5,4},{6,7},{7,6},{8,9},{9,8},{10,11... | collective-permute-start | bytes 110600 | tf_op jit(solution)/shard_map/ppermute | solution.py:17
  1.9 4.6 %collective-permute-start.1 = (bf16[144,128]{1,0:T(8,128)(2,1)S(1)}, bf16[144,128]{1,0:T(8,128)(2,1)S(1)}, u32[]{:S(2)}, u32[]{:S(2)}) collective-permute-start(bf16[144,128]{1,0:T(8,128)(2,1)S(1)} %get-tuple-element.51), channel_id=1, source_target_pairs={{0,8},{1,2},{2,1},{3,4},{4,3},{5,6},{6,5},{7,15},{8,0},{9,10},{10,... | collective-permute-start | bytes 110600 | tf_op jit(solution)/shard_map/ppermute | solution.py:30
  6.5 3.4 %copy-start = (bf16[27,128,128]{2,1,0:T(8,128)(2,1)S(1)}, bf16[27,128,128]{2,1,0:T(8,128)(2,1)}, u32[]{:S(2)}) copy-start(bf16[27,128,128]{2,1,0:T(8,128)(2,1)} %param.11) | copy-start | bytes 2654212
  7.8 2.7 %collective-permute-start.2 = (bf16[128,128]{1,0:T(8,128)(2,1)S(1)}, bf16[128,128]{1,0:T(8,128)(2,1)S(1)}, u32[]{:S(2)}, u32[]{:S(2)}) collective-permute-start(bf16[128,128]{1,0:T(8,128)(2,1)S(1)} %get-tuple-element.56), channel_id=1, source_target_pairs={{0,1},{1,0},{2,3},{3,2},{4,5},{5,4},{6,7},{7,6},{8,9},{9,8},{10,11... | collective-permute-start | bytes 98312 | tf_op jit(solution)/shard_map/ppermute | solution.py:17
  8.2 3.6 %collective-permute-start.3 = (bf16[128,128]{1,0:T(8,128)(2,1)S(1)}, bf16[128,128]{1,0:T(8,128)(2,1)S(1)}, u32[]{:S(2)}, u32[]{:S(2)}) collective-permute-start(bf16[128,128]{1,0:T(8,128)(2,1)S(1)} %get-tuple-element.57), channel_id=1, source_target_pairs={{0,8},{1,2},{2,1},{3,4},{4,3},{5,6},{6,5},{7,15},{8,0},{9,10},{10,... | collective-permute-start | bytes 98312 | tf_op jit(solution)/shard_map/ppermute | solution.py:30
  9.8 2.1 %copy-start.2 = (bf16[256,128]{1,0:T(8,128)(2,1)S(1)}, bf16[256,128]{1,0:T(8,128)(2,1)}, u32[]{:S(2)}) copy-start(bf16[256,128]{1,0:T(8,128)(2,1)} %cotangent.1) | copy-start | bytes 196612
  15.6 1.9 %collective-permute-start.4 = (bf16[1856,128]{1,0:T(8,128)(2,1)S(1)}, bf16[1856,128]{1,0:T(8,128)(2,1)S(1)}, u32[]{:S(2)}, u32[]{:S(2)}) collective-permute-start(bf16[1856,128]{1,0:T(8,128)(2,1)S(1)} %get-tuple-element.68), channel_id=1, source_target_pairs={{0,1},{1,0},{2,3},{3,2},{4,5},{5,4},{6,7},{7,6},{8,9},{9,8},{10,11... | collective-permute-start | bytes 1425416 | tf_op jit(solution)/shard_map/ppermute | solution.py:17
  16.0 3.6 %collective-permute-start.5 = (bf16[128,128]{1,0:T(8,128)(2,1)S(1)}, bf16[128,128]{1,0:T(8,128)(2,1)S(1)}, u32[]{:S(2)}, u32[]{:S(2)}) collective-permute-start(bf16[128,128]{1,0:T(8,128)(2,1)S(1)} %get-tuple-element.72), channel_id=1, source_target_pairs={{0,8},{1,2},{2,1},{3,4},{4,3},{5,6},{6,5},{7,15},{8,0},{9,10},{10,... | collective-permute-start | bytes 98312 | tf_op jit(solution)/shard_map/ppermute | solution.py:30
  21.3 3.5 %collective-permute-start.6 = (bf16[1728,128]{1,0:T(8,128)(2,1)S(1)}, bf16[1728,128]{1,0:T(8,128)(2,1)S(1)}, u32[]{:S(2)}, u32[]{:S(2)}) collective-permute-start(bf16[1728,128]{1,0:T(8,128)(2,1)S(1)} %get-tuple-element.75), channel_id=1, source_target_pairs={{0,1},{1,0},{2,3},{3,2},{4,5},{5,4},{6,7},{7,6},{8,9},{9,8},{10,11... | collective-permute-start | bytes 1327112 | tf_op jit(solution)/shard_map/ppermute | solution.py:17
  21.8 5.8 %collective-permute-start.15 = (bf16[432,128]{1,0:T(8,128)(2,1)S(1)}, bf16[432,128]{1,0:T(8,128)(2,1)S(1)}, u32[]{:S(2)}, u32[]{:S(2)}) collective-permute-start(bf16[432,128]{1,0:T(8,128)(2,1)S(1)} %get-tuple-element.91), channel_id=1, source_target_pairs={{0,8},{8,0},{16,24},{24,16},{1,9},{9,1},{17,25},{25,17},{2,10},{10... | collective-permute-start | bytes 331784 | tf_op jit(solution)/shard_map/ppermute | solution.py:17
  23.5 5.6 %collective-permute-start.16 = (bf16[432,128]{1,0:T(8,128)(2,1)S(1)}, bf16[432,128]{1,0:T(8,128)(2,1)S(1)}, u32[]{:S(2)}, u32[]{:S(2)}) collective-permute-start(bf16[432,128]{1,0:T(8,128)(2,1)S(1)} %get-tuple-element.92), channel_id=1, source_target_pairs={{0,16},{8,24},{16,0},{24,8},{1,17},{9,25},{17,1},{25,9},{2,18},{10... | collective-permute-start | bytes 331784 | tf_op jit(solution)/shard_map/ppermute | solution.py:17
  24.8 5.0 %collective-permute-start.17 = (bf16[432,128]{1,0:T(8,128)(2,1)S(1)}, bf16[432,128]{1,0:T(8,128)(2,1)S(1)}, u32[]{:S(2)}, u32[]{:S(2)}) collective-permute-start(bf16[432,128]{1,0:T(8,128)(2,1)S(1)} %get-tuple-element.69), channel_id=1, source_target_pairs={{0,24},{8,16},{16,8},{24,0},{1,25},{9,17},{17,9},{25,1},{2,26},{10... | collective-permute-start | bytes 331784 | tf_op jit(solution)/shard_map/ppermute | solution.py:17
  24.9 6.3 %collective-permute-start.7 = (bf16[432,128]{1,0:T(8,128)(2,1)S(1)}, bf16[432,128]{1,0:T(8,128)(2,1)S(1)}, u32[]{:S(2)}, u32[]{:S(2)}) collective-permute-start(bf16[432,128]{1,0:T(8,128)(2,1)S(1)} %get-tuple-element.82), channel_id=1, source_target_pairs={{0,8},{8,0},{16,24},{24,16},{1,9},{9,1},{17,25},{25,17},{2,10},{10... | collective-permute-start | bytes 331784 | tf_op jit(solution)/shard_map/ppermute | solution.py:17
  26.4 7.6 %collective-permute-start.8 = (bf16[432,128]{1,0:T(8,128)(2,1)S(1)}, bf16[432,128]{1,0:T(8,128)(2,1)S(1)}, u32[]{:S(2)}, u32[]{:S(2)}) collective-permute-start(bf16[432,128]{1,0:T(8,128)(2,1)S(1)} %get-tuple-element.83), channel_id=1, source_target_pairs={{0,16},{8,24},{16,0},{24,8},{1,17},{9,25},{17,1},{25,9},{2,18},{10... | collective-permute-start | bytes 331784 | tf_op jit(solution)/shard_map/ppermute | solution.py:17
  27.6 6.9 %collective-permute-start.9 = (bf16[432,128]{1,0:T(8,128)(2,1)S(1)}, bf16[432,128]{1,0:T(8,128)(2,1)S(1)}, u32[]{:S(2)}, u32[]{:S(2)}) collective-permute-start(bf16[432,128]{1,0:T(8,128)(2,1)S(1)} %get-tuple-element.76), channel_id=1, source_target_pairs={{0,24},{8,16},{16,8},{24,0},{1,25},{9,17},{17,9},{25,1},{2,26},{10... | collective-permute-start | bytes 331784 | tf_op jit(solution)/shard_map/ppermute | solution.py:17
  29.8 5.3 %collective-permute-start.18 = (bf16[432,128]{1,0:T(8,128)(2,1)S(1)}, bf16[432,128]{1,0:T(8,128)(2,1)S(1)}, u32[]{:S(2)}, u32[]{:S(2)}) collective-permute-start(bf16[432,128]{1,0:T(8,128)(2,1)S(1)} %add_convert_fusion.2), channel_id=1, source_target_pairs={{0,4},{1,5},{2,6},{3,7},{4,0},{5,1},{6,2},{7,3},{8,12},{9,13},{10,... | collective-permute-start | bytes 331784 | tf_op jit(solution)/shard_map/ppermute | solution.py:17
  34.5 5.2 %collective-permute-start.10 = (bf16[432,128]{1,0:T(8,128)(2,1)S(1)}, bf16[432,128]{1,0:T(8,128)(2,1)S(1)}, u32[]{:S(2)}, u32[]{:S(2)}) collective-permute-start(bf16[432,128]{1,0:T(8,128)(2,1)S(1)} %add_convert_fusion.5), channel_id=1, source_target_pairs={{0,2},{1,3},{2,0},{3,1},{4,6},{5,7},{6,4},{7,5},{8,10},{9,11},{10,... | collective-permute-start | bytes 331784 | tf_op jit(solution)/shard_map/ppermute | solution.py:17
  35.8 8.2 %collective-permute-start.19 = (bf16[432,128]{1,0:T(8,128)(2,1)S(1)}, bf16[432,128]{1,0:T(8,128)(2,1)S(1)}, u32[]{:S(2)}, u32[]{:S(2)}) collective-permute-start(bf16[432,128]{1,0:T(8,128)(2,1)S(1)} %add_convert_fusion.1), channel_id=1, source_target_pairs={{0,2},{1,3},{2,0},{3,1},{4,6},{5,7},{6,4},{7,5},{8,10},{9,11},{10,... | collective-permute-start | bytes 331784 | tf_op jit(solution)/shard_map/ppermute | solution.py:17
  39.7 6.4 %collective-permute-start.13 = (bf16[432,128]{1,0:T(8,128)(2,1)S(1)}, bf16[432,128]{1,0:T(8,128)(2,1)S(1)}, u32[]{:S(2)}, u32[]{:S(2)}) collective-permute-start(bf16[432,128]{1,0:T(8,128)(2,1)S(1)} %add_convert_fusion.4), channel_id=1, source_target_pairs={{0,4},{1,5},{2,6},{3,7},{4,0},{5,1},{6,2},{7,3},{8,12},{9,13},{10,... | collective-permute-start | bytes 331784 | tf_op jit(solution)/shard_map/ppermute | solution.py:17
  39.8 6.4 %collective-permute-start.12 = (bf16[128,128]{1,0:T(8,128)(2,1)S(1)}, bf16[128,128]{1,0:T(8,128)(2,1)S(1)}, u32[]{:S(2)}, u32[]{:S(2)}) collective-permute-start(bf16[128,128]{1,0:T(8,128)(2,1)S(1)} %get-tuple-element.87), channel_id=1, source_target_pairs={{0,8},{1,2},{2,1},{3,4},{4,3},{5,6},{6,5},{7,15},{8,0},{9,10},{10,... | collective-permute-start | bytes 98312 | tf_op jit(solution)/shard_map/ppermute | solution.py:30
  44.0 5.3 %collective-permute-start.20 = (bf16[432,128]{1,0:T(8,128)(2,1)S(1)}, bf16[432,128]{1,0:T(8,128)(2,1)S(1)}, u32[]{:S(2)}, u32[]{:S(2)}) collective-permute-start(bf16[432,128]{1,0:T(8,128)(2,1)S(1)} %add_convert_fusion), channel_id=1, source_target_pairs={{0,1},{1,0},{2,3},{3,2},{4,5},{5,4},{6,7},{7,6},{8,9},{9,8},{10,11... | collective-permute-start | bytes 331784 | tf_op jit(solution)/shard_map/ppermute | solution.py:17
  46.1 2.5 %collective-permute-start.11 = (bf16[128,128]{1,0:T(8,128)(2,1)S(1)}, bf16[128,128]{1,0:T(8,128)(2,1)S(1)}, u32[]{:S(2)}, u32[]{:S(2)}) collective-permute-start(bf16[128,128]{1,0:T(8,128)(2,1)S(1)} %get-tuple-element.86), channel_id=1, source_target_pairs={{0,1},{1,0},{2,3},{3,2},{4,5},{5,4},{6,7},{7,6},{8,9},{9,8},{10,11... | collective-permute-start | bytes 98312 | tf_op jit(solution)/shard_map/ppermute | solution.py:17
  46.2 3.3 %collective-permute-start.14 = (bf16[432,128]{1,0:T(8,128)(2,1)S(1)}, bf16[432,128]{1,0:T(8,128)(2,1)S(1)}, u32[]{:S(2)}, u32[]{:S(2)}) collective-permute-start(bf16[432,128]{1,0:T(8,128)(2,1)S(1)} %add_convert_fusion.3), channel_id=1, source_target_pairs={{0,1},{1,0},{2,3},{3,2},{4,5},{5,4},{6,7},{7,6},{8,9},{9,8},{10,11... | collective-permute-start | bytes 331784 | tf_op jit(solution)/shard_map/ppermute | solution.py:17

commit v7 on v6

--- a/solution.py
+++ b/solution.py
@@ -1,3 +1,5 @@
+import functools
+
 import jax
 import jax.numpy as jnp
 from jax import lax
@@ -175,33 +177,37 @@
             singles_turned[side * per + i] = by_sources(near, at, blk)
 
 
-def pull(far_turned, pairs_turned, singles_turned, grads, pulled, kind):
+def pull_middle(pairs_turned, grads, pulled, base):
     per, channels = pairs_turned.shape[0], grads.shape[1]
     for i in range(per):
-        if kind == 1:
-            select = pairs_turned[i]
-        else:
-            side = (kind // 2) * per + i
-            select = jnp.concatenate([far_turned[side], singles_turned[side]], axis=0)
+        got = jnp.dot(pairs_turned[i], grads, preferred_element_type=F32)
+        at = base + i * channels
+        pulled[:, at : at + channels] = got.astype(BF16)
+
+
+def pull_outer(far_turned, singles_turned, grads, pulled, side, base=0):
+    per, channels = far_turned.shape[0] // 2, grads.shape[1]
+    for i in range(side * per, (side + 1) * per):
+        select = jnp.concatenate([far_turned[i], singles_turned[i]], axis=0)
         got = jnp.dot(select, grads, preferred_element_type=F32)
-        at = (kind * per + i) * channels
+        at = base + i * channels
         pulled[:, at : at + channels] = got.astype(BF16)
 
 
-def of_kind_in(pulled, kind):
-    wide = pulled.shape[1] // KINDS
-    return pulled[:, kind * wide : (kind + 1) * wide]
-
-
-def source_sums(pulled, weights, kind):
+def side_of(pulled, side, sides):
+    wide = pulled.shape[1] // sides
+    return pulled[:, side * wide : (side + 1) * wide]
+
+
+def source_sums(held, weights, kind):
     per = weights.shape[0] // weights.shape[1] // KINDS
     wide = weights_of(weights, kind, per, 1)
-    return lax.dot_general(of_kind_in(pulled, kind), wide, NT, preferred_element_type=F32)
-
-
-def weight_sums(pulled, source, wgrad, kind):
+    return lax.dot_general(held, wide, NT, preferred_element_type=F32)
+
+
+def weight_sums(held, source, wgrad, kind):
     channels = wgrad.shape[1]
-    terms = jnp.dot(source.T, of_kind_in(pulled, kind), preferred_element_type=F32)
+    terms = jnp.dot(source.T, held, preferred_element_type=F32)
     for i in range(terms.shape[1] // channels):
         at = (i * KINDS + kind) * channels
         wgrad[at : at + channels, :] = terms[:, i * channels : (i + 1) * channels]
@@ -265,19 +271,22 @@
         far_turned[at] = by_sources(entries, at, entries.shape[1])
 
 
+def outer_sources(hidden, odd, core_in, cross_in, blk):
+    after, before = halo_sides(odd, core_in[...], cross_in[...])
+    low = jnp.concatenate([after, hidden[blk:, :]], axis=0)
+    return low, jnp.concatenate([before, hidden[:blk, :]], axis=0)
+
+
 def second_kernel(
     count_ref, features, hidden, core_in, cross_in, far, singles, part, weights, cotangent,
-    far_turned, pairs_turned, singles_turned,
-    result, grads_out, own_out, keep, core_out, cross_out, picked, pulled, wgrad,
+    far_turned, singles_turned,
+    result, grads_out, own_out, pulled, core_out, cross_out, picked,
 ):
     blk = features.shape[0] // 2
     count = count_ref[:1, :]
     both = count == 2
     odd, _, _ = place()
-    after, before = halo_sides(odd, core_in[...], cross_in[...])
-    front, back = hidden[:blk, :], hidden[blk:, :]
-    low = jnp.concatenate([after, back], axis=0)
-    high = jnp.concatenate([before, front], axis=0)
+    low, high = outer_sources(hidden, odd, core_in, cross_in, blk)
     total = part[...] + outer_part(far, singles, [low, high], weights, picked)
     total = total + features[...].astype(F32)
     mask = row_mask(2 * blk, blk, count)
@@ -285,18 +294,31 @@
     result[...] = (value * mask).astype(BF16)
     grads = (cotangent[...].astype(F32) * grad * mask).astype(BF16)
     grads_out[...] = grads
-    sources = [low, hidden[...], high]
     sums = []
-    for kind in range(KINDS):
-        pull(far_turned, pairs_turned, singles_turned, grads, pulled, kind)
-        sums.append(source_sums(pulled, weights, kind))
-        weight_sums(pulled, sources[kind], wgrad, kind)
-    own, to_next, to_prev = split_sums(sums, both, blk)
-    own_out[...] = own
-    core, cross = exchange_sides(odd, to_next, to_prev)
-    core_out[:blk, :] = core.astype(BF16)
+    for side, kind in enumerate((0, 2)):
+        pull_outer(far_turned, singles_turned, grads, pulled, side)
+        sums.append(source_sums(side_of(pulled, side, 2), weights, kind))
+    low, high = sums
+    own_out[:blk, :] = jnp.where(both, high[blk:], 0.0)
+    own_out[blk:, :] = low[blk:]
+    core, cross = exchange_sides(odd, low[:blk], high[:blk])
+    core_out[...] = core.astype(BF16)
     cross_out[...] = cross.astype(BF16)
-    halves_out(odd, wgrad, keep, core_out, blk)
+
+
+def second_rest_kernel(
+    hidden, core_in, cross_in, weights, grads, pulled, own_in, pairs_turned,
+    own_out, keep, core_out, middle, wgrad,
+):
+    blk = hidden.shape[0] // 2
+    odd, _, _ = place()
+    pull_middle(pairs_turned, grads[...], middle, 0)
+    own_out[...] = own_in[...] + source_sums(middle[...], weights, 1)
+    low, high = outer_sources(hidden, odd, core_in, cross_in, blk)
+    weight_sums(middle[...], hidden[...], wgrad, 1)
+    weight_sums(side_of(pulled, 0, 2), low, wgrad, 0)
+    weight_sums(side_of(pulled, 1, 2), high, wgrad, 2)
+    halves_out(odd, wgrad, keep, core_out, 0)
 
 
 def joined(own, odd, both, core_in, cross_in, blk):
@@ -314,7 +336,7 @@
     blk = features.shape[0] // 2
     both = count_ref[:1, :] == 2
     odd, _, _ = place()
-    core, cross = core_in[:blk, :].astype(F32), cross_in[...].astype(F32)
+    core, cross = core_in[...].astype(F32), cross_in[...].astype(F32)
     summed = joined(own[...], odd, both, core, cross, blk)
     grads = (summed * slope[...]).astype(BF16)
     sources = [
@@ -322,10 +344,11 @@
         features[...],
         jnp.concatenate([halo[1], features[:blk, :]], axis=0),
     ]
-    for kind in range(KINDS):
-        pull(far_turned, pairs_turned, singles_turned, grads, pulled, kind)
-    for kind in range(KINDS):
-        weight_sums(pulled, sources[kind], wgrad, kind)
+    for side in range(2):
+        pull_outer(far_turned, singles_turned, grads, pulled, side)
+    pull_middle(pairs_turned, grads, pulled, pulled.shape[1] // KINDS * 2)
+    for at, kind in enumerate((0, 2, 1)):
+        weight_sums(side_of(pulled, at, KINDS), sources[kind], wgrad, kind)
     halves_out(odd, wgrad, keep, core_out, 0)
 
 
@@ -333,20 +356,60 @@
     blk = grads_in.shape[0] // 2
     both = count_ref[:1, :] == 2
     odd, _, _ = place()
-    sums = [source_sums(pulled, weights, kind) for kind in range(KINDS)]
-    own, to_next, to_prev = split_sums(sums, both, blk)
+    low, high, middle = [
+        source_sums(side_of(pulled, at, KINDS), weights, kind)
+        for at, kind in enumerate((0, 2, 1))
+    ]
+    own, to_next, to_prev = split_sums([low, middle, high], both, blk)
     own_out[...] = own + grads_in[...].astype(F32)
     core, cross = exchange_sides(odd, to_next, to_prev)
     core_out[...] = core.astype(BF16)
     cross_out[...] = cross.astype(BF16)
 
 
-def last_kernel(count_ref, own, core_in, cross_in, input_grad):
+def both_halves(odd, mine, other, scale, out):
+    half = out.shape[0] // 2
+    mine, other = mine[:half, :].astype(F32) * scale, other[:half, :].astype(F32) * scale
+    out[:half, :] = jnp.where(odd, other, mine)
+    out[half:, :] = jnp.where(odd, mine, other)
+
+
+def last_kernel(
+    scale, count_ref, own, core_in, cross_in, mine, near, far_off, both_off, input_grad, out
+):
     blk = own.shape[0] // 2
     both = count_ref[:1, :] == 2
     odd, _, _ = place()
     core, cross = core_in[...].astype(F32), cross_in[...].astype(F32)
     input_grad[...] = joined(own[...], odd, both, core, cross, blk).astype(BF16)
+    upper = (lax.axis_index("tile") // 2) % 2 == 1
+    half, part = out.shape[0] // 2, mine.shape[0]
+    slot = half + (-half % 16)
+    values = [ref[...].astype(F32) * scale for ref in (mine, far_off, near, both_off)]
+    low = [jnp.where(upper, values[1], values[0]), jnp.where(upper, values[3], values[2])]
+    high = [jnp.where(upper, values[0], values[1]), jnp.where(upper, values[2], values[3])]
+    for side in range(2):
+        at = side * half
+        out[at : at + part, :] = jnp.where(odd, low[1 - side], low[side])
+        rest = jnp.where(odd, high[1 - side], high[side])
+        skip = 2 * part - slot
+        out[at + part : at + half, :] = rest[skip : skip + half - part]
+
+
+def rows_kernel(scale, mine, other, out):
+    odd, _, _ = place()
+    both_halves(odd, mine, other, scale, out)
+
+
+def quarters_kernel(keep, core, kept, send):
+    shards, slot, _ = keep.shape
+    part = kept.shape[1]
+    upper = (lax.axis_index("tile") // 2) % 2 == 1
+    for s in range(shards):
+        value = keep[s] + core[s * slot : (s + 1) * slot, :].astype(F32)
+        low, high = value[:part], value[slot - part :]
+        kept[s] = jnp.where(upper, high, low)
+        send[s * part : (s + 1) * part, :] = jnp.where(upper, low, high).astype(BF16)
 
 
 def shards_kernel(keep, core, own, *sends):
@@ -365,11 +428,6 @@
 
 def after(first, later):
     return lax.optimization_barrier((first, later))[1]
-
-
-def either_order(second, mine, other):
-    parts = [jnp.where(second, other, mine), jnp.where(second, mine, other)]
-    return jnp.concatenate(parts, axis=0)
 
 
 def added(value, others):
@@ -460,29 +518,43 @@
         scratch=[inner],
         micros=1,
     )
-    result, grad_sum, own, keep_two, core_two, cross = call(
+    result, grad_sum, own, held, core_sum, cross_sum = call(
         second_kernel,
-        [field, field, summed, keep_shape, core_shape, block],
+        [field, field, summed, outer, block, block],
         count, features, hidden, core, cross, far, singles, part, flat_two, out_cotangent,
-        far_turned, pairs_turned, singles_turned,
-        scratch=[outer, pulled, wgrad],
-        micros=4,
-    )
-    cross, core_two = crossed(cross), swapped(core_two, "tile", 1)
+        far_turned, singles_turned,
+        scratch=[outer],
+        micros=3,
+    )
+    cross_sum, core_sum = crossed(cross_sum), swapped(core_sum, "tile", 1)
+    own, keep_two, core_two = call(
+        second_rest_kernel,
+        [summed, keep_shape, ((n_grp * slot, channels), BF16)],
+        hidden, core, cross, flat_two, grad_sum, held, own, pairs_turned,
+        scratch=[inner, wgrad],
+        micros=1,
+    )
+    core_two = swapped(core_two, "tile", 1)
     shard = (slot, channels)
     shards = [(shard, F32)] + [(shard, BF16)] * (n_grp - 1)
-    mine_two, *sends_two = call(shards_kernel, shards, keep_two, core_two)
-    got_two = [swapped(send, "grp", d + 1) for d, send in enumerate(sends_two)]
-    own = after(sends_two[-1], own)
+    part = slot // 2 + (-(slot // 2) % 16)
+    quarter = (part, channels)
+    steps = [1 << b for b in range(1, (n_tile - 1).bit_length())]
+    kept_two, send_two = call(
+        quarters_kernel,
+        [((n_grp, part, channels), F32), ((n_grp * part, channels), BF16)],
+        keep_two, core_two,
+    )
     held, keep_one, core_one = call(
         third_kernel,
         [pulled, keep_shape, ((n_grp * slot, channels), BF16)],
-        count, features, halo, own, core_two, cross, slope,
+        count, features, halo, own, core_sum, cross_sum, slope,
         far_turned, pairs_turned, singles_turned,
         scratch=[wgrad],
         micros=2,
     )
     core_one = swapped(core_one, "tile", 1)
+    near_two = swapped(send_two, "tile", steps[0])
     mine_one, *sends_one = call(shards_kernel, shards, keep_one, core_one)
     got_one = [swapped(send, "grp", d + 1) for d, send in enumerate(sends_one)]
     own, core, cross = call(
@@ -490,33 +562,37 @@
         [summed, block, block],
         count, after(sends_one[-1], held), flat_one, grad_sum,
     )
-    two = added(mine_two, got_two).astype(BF16)
-    steps = [1 << b for b in range(1, (n_tile - 1).bit_length())]
-    other_two = swapped(two, "tile", steps[-1])
+    mine_two, *sends_two = call(
+        shards_kernel,
+        [(quarter, F32)] + [(quarter, BF16)] * (n_grp - 1),
+        after(sends_one[-1], kept_two), near_two,
+    )
+    got_two = [swapped(send, "grp", d + 1) for d, send in enumerate(sends_two)]
     one = added(mine_one, got_one).astype(BF16)
+    two = added(mine_two, got_two)
     for at, bits in enumerate(steps):
         other_one = swapped(one, "tile", bits)
-        two = added(two, [other_two])
         if at + 1 < len(steps):
             two = two.astype(BF16)
             two = after(one, two)
-            other_two = swapped(two, "tile", steps[-2 - at])
+            other_two = swapped(two, "tile", steps[at + 1])
+            two = added(two, [other_two])
             one = added(one, [other_one]).astype(BF16)
-            if at == 0:
-                one, core, cross = lax.optimization_barrier((one, core, cross))
+    two = two.astype(BF16)
+    core, cross = lax.optimization_barrier((one, core, cross))[1:]
     cross, core = crossed(cross), swapped(core, "tile", 1)
-    (input_grad,) = call(last_kernel, [field], count, own, core, cross)
+    near, far_off, both_off = [swapped(two, "tile", bits) for bits in (1, steps[0], steps[0] + 1)]
     scale = float(n_grp * n_tile * rows) ** (-0.5)
-    odd = lax.axis_index("tile") % 2 == 1
-
-    def finished(part):
-        part = part[:half]
-        other = swapped(part, "tile", 1)
-        return either_order(odd, part.astype(F32) * scale, other.astype(F32) * scale)
-
-    other_one = after(cross, other_one)
-    two = finished(two.astype(BF16))
-    one = finished(added(one, [other_one]).astype(BF16))
+    shard_out = ((2 * half, channels), F32)
+    input_grad, two = call(
+        functools.partial(last_kernel, scale),
+        [field, shard_out],
+        count, own, core, cross, two, near, far_off, both_off,
+    )
+    one = added(one, [other_one]).astype(BF16)
+    (one,) = call(
+        functools.partial(rows_kernel, scale), [shard_out], one, swapped(one, "tile", 1)
+    )
     return (result, input_grad, one, two)
 
 

time: 51.7 us -> 50.7 us (0.981)
  waiting for transfers between devices: 13 us -> 10.2 us
  starting transfers between devices: 24.4 us -> 26.3 us
  other arithmetic: 1.95 us -> 0.18 us
  Pallas kernels: 11.1 us -> 12.8 us
    ppermute x17 -> x20, starting transfers between devices: 15 us -> 21 us  [swapped(): lax.ppermute(value, axis, [(i, i ^ bits) for i in range(count) if i ^ bit...]
    ppermute x4, starting transfers between devices: 9.41 us -> 5.27 us  [crossed(): return lax.ppermute(value, ('grp', 'tile'), pairs)]
    ppermute x4, waiting for transfers between devices: 4.14 us -> 2.21 us  [crossed(): return lax.ppermute(value, ('grp', 'tile'), pairs)]
    pallas_call x10 -> x13, Pallas kernels: 11.1 us -> 12.8 us  [call(): pl.pallas_call(kernel, out_shape=[jax.ShapeDtypeStruct(shape, kind) for s...]
    concatenate x2 -> x0, other arithmetic: 1.58 us -> none  [either_order(): return jnp.concatenate(parts, axis=0)]
    ppermute x17 -> x20, waiting for transfers between devices: 8.83 us -> 7.95 us  [swapped(): lax.ppermute(value, axis, [(i, i ^ bits) for i in range(count) if i ^ bit...]
  transfers between devices with their start and end apart: 21 -> 24, of which waited for: 11 -> 8; matrix products, arithmetic and copies ran while one was open for 1% -> 0% of each run, Pallas kernels for 6% -> 13%
where the time goes in v7:
time: 50.7 us; the launch traced here: 50.2 us
  starting transfers between devices  26.3 us (52%)
  Pallas kernels  12.8 us (25%)
  waiting for transfers between devices  10.2 us (20%)
  between operations  0.8 us (2%)
    ppermute x20, starting transfers between devices, swapped(): lax.ppermute(value, axis, [(i, i ^ bits) for i in range(count) if i ^ bit...  21 us
    pallas_call x13, Pallas kernels, call(): pl.pallas_call(kernel, out_shape=[jax.ShapeDtypeStruct(shape, kind) for s...  12.8 us
    ppermute x20, waiting for transfers between devices, swapped(): lax.ppermute(value, axis, [(i, i ^ bits) for i in range(count) if i ^ bit...  7.95 us
    ppermute x4, starting transfers between devices, crossed(): return lax.ppermute(value, ('grp', 'tile'), pairs)  5.27 us
    ppermute x4, waiting for transfers between devices, crossed(): return lax.ppermute(value, ('grp', 'tile'), pairs)  2.21 us
  transfers between devices with their start and end apart: 24, of which 8 were waited for; matrix products, arithmetic and copies ran while one was open for 0% of the time, Pallas kernels for 13%

profile of v7, /device:TPU:1, one launch (start us, length us, event | category | flops | bytes accessed | tf_op | source)
XLA Modules:
  0.0 50.2 jit_solution(5058868722144089678)
XLA Ops:
  0.7 1.1 %shard_map.93 = (f32[40,128]{1,0:T(8,128)S(1)}, bf16[144,128]{1,0:T(8,128)(2,1)S(1)}, bf16[144,128]{1,0:T(8,128)(2,1)S(1)}, s32[8,128]{1,0:T(8,128)S(1)}) custom-call(bf16[256,128]{1,0:T(8,128)(2,1)} %features.7, s32[27,2,128]{2,1,0:T(2,128)} %rows_in.1, s32[2,27]{1,0:T(2,128)} %bitcast.9), custom_call_target="tpu_custom_call" | custom-call | flops 3000000000 | bytes 9000000 | tf_op jit(solution)/shard_map/pallas_call | solution.py:442
  1.8 0.1 collective-permute-start
  1.9 2.7 %collective-permute-start.1 = (bf16[144,128]{1,0:T(8,128)(2,1)S(1)}, bf16[144,128]{1,0:T(8,128)(2,1)S(1)}, u32[]{:S(2)}, u32[]{:S(2)}) collective-permute-start(bf16[144,128]{1,0:T(8,128)(2,1)S(1)} %get-tuple-element.56), channel_id=1, source_target_pairs={{0,8},{1,2},{2,1},{3,4},{4,3},{5,6},{6,5},{7,15},{8,0},{9,10},{10,... | collective-permute-start | bytes 110600 | tf_op jit(solution)/shard_map/ppermute | solution.py:32
  4.6 1.1 %shard_map.94 = (bf16[9,256,256]{2,1,0:T(8,128)(2,1)S(1)}, bf16[18,256,128]{2,1,0:T(8,128)(2,1)S(1)}, bf16[9,256,256]{2,1,0:T(8,128)(2,1)S(1)}, bf16[18,128,256]{2,1,0:T(8,128)(2,1)S(1)}, f32[256,128]{1,0:T(8,128)S(1)}) custom-call(f32[40,128]{1,0:T(8,128)S(1)} %get-tuple-element.57.near, bf16[256,128]{1,0:T(8,128)(2,1)S(1)} %copy-done.3, ...), custom_call_target="tpu_custom_call" | custom-call | flops 2000000000 | bytes 6000000 | tf_op jit(solution)/shard_map/pallas_call | solution.py:442
  5.8 0.7 %collective-permute-done.1.cross_in = bf16[144,128]{1,0:T(8,128)(2,1)S(1)} collective-permute-done((bf16[144,128]{1,0:T(8,128)(2,1)S(1)}, bf16[144,128]{1,0:T(8,128)(2,1)S(1)}, u32[]{:S(2)}, u32[]{:S(2)}) %collective-permute-start.1) | collective-permute-done | bytes 36896 | tf_op jit(solution)/shard_map/ppermute | solution.py:32
  6.5 1.3 %shard_map.95 = (f32[24,128]{1,0:T(8,128)S(1)}, bf16[18,256,128]{2,1,0:T(8,128)(2,1)S(1)}, bf16[2,128,128]{2,1,0:T(8,128)(2,1)S(1)}, bf16[256,128]{1,0:T(8,128)(...) custom-call(s32[8,128]{1,0:T(8,128)S(1)} %get-tuple-element.54.count_ref, ...), custom_call_target="tpu_custom_call" | custom-call | flops 2000000000 | bytes 6000000 | tf_op jit(solution)/shard_map/pallas_call | solution.py:442
  7.8 0.5 collective-permute-start.2
  8.2 1.6 %collective-permute-start.3 = (bf16[128,128]{1,0:T(8,128)(2,1)S(1)}, bf16[128,128]{1,0:T(8,128)(2,1)S(1)}, u32[]{:S(2)}, u32[]{:S(2)}) collective-permute-start(bf16[128,128]{1,0:T(8,128)(2,1)S(1)} %get-tuple-element.62), channel_id=1, source_target_pairs={{0,8},{1,2},{2,1},{3,4},{4,3},{5,6},{6,5},{7,15},{8,0},{9,10},{10,... | collective-permute-start | bytes 98312 | tf_op jit(solution)/shard_map/ppermute | solution.py:32
  9.8 0.7 %shard_map.96 = (f32[256,128]{1,0:T(8,128)S(1)}, bf16[18,128,256]{2,1,0:T(8,128)(2,1)S(1)}) custom-call(bf16[256,128]{1,0:T(8,128)(2,1)S(1)} %get-tuple-element.60.hidden, bf16[9,256,256]{2,1,0:T(8,128)(2,1)S(1)} %get-tuple-element.64.pairs, f32[24,128]{1,0:T(8,128)S(1)} %get-tuple-element.65.entries, bf16[3456,128]{1,0:T(8,128)(2,1)S(1)} %bitcast.3), custom_call_target="tpu_custom_call" | custom-call | flops 1000000000 | bytes 3000000 | tf_op jit(solution)/shard_map/pallas_call | solution.py:442
  10.5 0.0 collective-permute-done.2.core_in
  10.5 1.4 %collective-permute-done.3.cross_in = bf16[128,128]{1,0:T(8,128)(2,1)S(1)} collective-permute-done((bf16[128,128]{1,0:T(8,128)(2,1)S(1)}, bf16[128,128]{1,0:T(8,128)(2,1)S(1)}, u32[]{:S(2)}, u32[]{:S(2)}) %collective-permute-start.3) | collective-permute-done | bytes 32800 | tf_op jit(solution)/shard_map/ppermute | solution.py:32
  11.9 3.0 %shard_map.97 = (bf16[256,128]{1,0:T(8,128)(2,1)}, bf16[256,128]{1,0:T(8,128)(2,1)S(1)}, f32[256,128]{1,0:T(8,128)S(1)}, bf16[256,2304]{1,0:T(8,128)(2,1)S(1)}, ...) custom-call(s32[8,128]{1,0:T(8,128)S(1)} %get-tuple-element.54.count_ref, bf16[256,128]{1,0:T(8,128)(2,1)S(1)} %copy-done.3, ...), custom_call_target="tpu_custom_call" | custom-call | flops 3000000000 | bytes 9000000 | tf_op jit(solution)/shard_map/pallas_call | solution.py:442
  14.9 0.4 collective-permute-start.4
  15.3 1.0 %collective-permute-start.5 = (bf16[128,128]{1,0:T(8,128)(2,1)S(1)}, bf16[128,128]{1,0:T(8,128)(2,1)S(1)}, u32[]{:S(2)}, u32[]{:S(2)}) collective-permute-start(bf16[128,128]{1,0:T(8,128)(2,1)S(1)} %get-tuple-element.77), channel_id=1, source_target_pairs={{0,8},{1,2},{2,1},{3,4},{4,3},{5,6},{6,5},{7,15},{8,0},{9,10},{10,... | collective-permute-start | bytes 98312 | tf_op jit(solution)/shard_map/ppermute | solution.py:32
  16.3 1.3 %shard_map.98 = (f32[256,128]{1,0:T(8,128)S(1)}, f32[4,432,128]{2,1,0:T(8,128)S(1)}, bf16[1728,128]{1,0:T(8,128)(2,1)S(1)}) custom-call(bf16[256,128]{1,0:T(8,128)(2,1)S(1)} %get-tuple-element.60.hidden, bf16[128,128]{1,0:T(8,128)(2,1)S(1)} %collective-permute-done.2.core_in, bf16[128,128]{1,0:T(8,128)(2,1)S(1)} %collective-permute-done.3.cross_in, ...), custom_call_target="tpu_custom_call" | custom-call | flops 1000000000 | bytes 3000000 | tf_op jit(solution)/shard_map/pallas_call | solution.py:442
  17.6 1.2 %collective-permute-start.13 = (bf16[1728,128]{1,0:T(8,128)(2,1)S(1)}, bf16[1728,128]{1,0:T(8,128)(2,1)S(1)}, u32[]{:S(2)}, u32[]{:S(2)}) collective-permute-start(bf16[1728,128]{1,0:T(8,128)(2,1)S(1)} %get-tuple-element.93), channel_id=1, source_target_pairs={{0,1},{1,0},{2,3},{3,2},{4,5},{5,4},{6,7},{7,6},{8,9},{9,8},{10,11... | collective-permute-start | bytes 1327112 | tf_op jit(solution)/shard_map/ppermute | solution.py:19
  18.8 0.1 collective-permute-done.5.cross_in
  18.9 1.7 %shard_map.99 = (bf16[256,3456]{1,0:T(8,128)(2,1)S(1)}, f32[4,432,128]{2,1,0:T(8,128)S(1)}, bf16[1728,128]{1,0:T(8,128)(2,1)S(1)}) custom-call(s32[8,128]{1,0:T(8,128)S(1)} %get-tuple-element.54.count_ref, bf16[256,128]{1,0:T(8,128)(2,1)S(1)} %copy-done.3, bf16[2,128,128]{2,1,0:T(8,128)(2,1)S(1)} %get-tuple-element.70.halo, ...), custom_call_target="tpu_custom_call" | custom-call | flops 2000000000 | bytes 6000000 | tf_op jit(solution)/shard_map/pallas_call | solution.py:442
  20.6 0.5 collective-permute-start.6
  21.1 0.0 collective-permute-done.13.core
  21.1 0.1 shard_map.102
  21.2 0.5 collective-permute-start.14
  21.7 0.8 %collective-permute-done.6.core = bf16[1728,128]{1,0:T(8,128)(2,1)S(1)} collective-permute-done((bf16[1728,128]{1,0:T(8,128)(2,1)S(1)}, bf16[1728,128]{1,0:T(8,128)(2,1)S(1)}, u32[]{:S(2)}, u32[]{:S(2)}) %collective-permute-start.6) | collective-permute-done | bytes 442400 | tf_op jit(solution)/shard_map/ppermute | solution.py:19
  22.5 0.1 shard_map.100
  22.6 2.8 %collective-permute-start.9 = (bf16[432,128]{1,0:T(8,128)(2,1)S(1)}, bf16[432,128]{1,0:T(8,128)(2,1)S(1)}, u32[]{:S(2)}, u32[]{:S(2)}) collective-permute-start(bf16[432,128]{1,0:T(8,128)(2,1)S(1)} %get-tuple-element.81), channel_id=1, source_target_pairs={{0,24},{8,16},{16,8},{24,0},{1,25},{9,17},{17,9},{25,1},{2,26},{10... | collective-permute-start | bytes 331784 | tf_op jit(solution)/shard_map/ppermute | solution.py:19
  25.3 0.3 collective-permute-start.7
  25.6 0.1 collective-permute-start.8
  25.7 0.6 %shard_map.101 = (f32[256,128]{1,0:T(8,128)S(1)}, bf16[128,128]{1,0:T(8,128)(2,1)S(1)}, bf16[128,128]{1,0:T(8,128)(2,1)S(1)}) custom-call(s32[8,128]{1,0:T(8,128)S(1)} %get-tuple-element.54.count_ref, bf16[256,3456]{1,0:T(8,128)(2,1)S(1)} %get-tuple-element.83.pulled, bf16[3456,128]{1,0:T(8,128)(2,1)S(1)} %bitcast.8, ...), custom_call_target="tpu_custom_call" | custom-call | flops 1000000000 | bytes 3000000 | tf_op jit(solution)/shard_map/pallas_call | solution.py:442
  26.3 2.0 %collective-permute-done.14.core = bf16[896,128]{1,0:T(8,128)(2,1)S(1)} collective-permute-done((bf16[896,128]{1,0:T(8,128)(2,1)S(1)}, bf16[896,128]{1,0:T(8,128)(2,1)S(1)}, u32[]{:S(2)}, u32[]{:S(2)}) %collective-permute-start.14) | collective-permute-done | bytes 229408 | tf_op jit(solution)/shard_map/ppermute | solution.py:19
  28.4 1.8 %collective-permute-start.15 = (bf16[224,128]{1,0:T(8,128)(2,1)S(1)}, bf16[224,128]{1,0:T(8,128)(2,1)S(1)}, u32[]{:S(2)}, u32[]{:S(2)}) collective-permute-start(bf16[224,128]{1,0:T(8,128)(2,1)S(1)} %get-tuple-element.98), channel_id=1, source_target_pairs={{0,8},{8,0},{16,24},{24,16},{1,9},{9,1},{17,25},{25,17},{2,10},{10... | collective-permute-start | bytes 172040 | tf_op jit(solution)/shard_map/ppermute | solution.py:19
  30.2 1.2 %collective-permute-start.16 = (bf16[224,128]{1,0:T(8,128)(2,1)S(1)}, bf16[224,128]{1,0:T(8,128)(2,1)S(1)}, u32[]{:S(2)}, u32[]{:S(2)}) collective-permute-start(bf16[224,128]{1,0:T(8,128)(2,1)S(1)} %get-tuple-element.99), channel_id=1, source_target_pairs={{0,16},{8,24},{16,0},{24,8},{1,17},{9,25},{17,1},{25,9},{2,18},{10... | collective-permute-start | bytes 172040 | tf_op jit(solution)/shard_map/ppermute | solution.py:19
  31.4 0.0 collective-permute-done.7
  31.4 0.5 %collective-permute-start.17 = (bf16[224,128]{1,0:T(8,128)(2,1)S(1)}, bf16[224,128]{1,0:T(8,128)(2,1)S(1)}, u32[]{:S(2)}, u32[]{:S(2)}) collective-permute-start(bf16[224,128]{1,0:T(8,128)(2,1)S(1)} %get-tuple-element.100), channel_id=1, source_target_pairs={{0,24},{8,16},{16,8},{24,0},{1,25},{9,17},{17,9},{25,1},{2,26},{10... | collective-permute-start | bytes 172040 | tf_op jit(solution)/shard_map/ppermute | solution.py:19
  31.9 0.0 collective-permute-done.8
  31.9 0.1 add_convert_fusion.2
  32.0 0.2 collective-permute-start.10
  32.2 1.0 %collective-permute-done.16 = bf16[224,128]{1,0:T(8,128)(2,1)S(1)} collective-permute-done((bf16[224,128]{1,0:T(8,128)(2,1)S(1)}, bf16[224,128]{1,0:T(8,128)(2,1)S(1)}, u32[]{:S(2)}, u32[]{:S(2)}) %collective-permute-start.16) | collective-permute-done | bytes 57376 | tf_op jit(solution)/shard_map/ppermute | solution.py:19
  33.2 2.2 %collective-permute-done.17 = bf16[224,128]{1,0:T(8,128)(2,1)S(1)} collective-permute-done((bf16[224,128]{1,0:T(8,128)(2,1)S(1)}, bf16[224,128]{1,0:T(8,128)(2,1)S(1)}, u32[]{:S(2)}, u32[]{:S(2)}) %collective-permute-start.17) | collective-permute-done | bytes 57376 | tf_op jit(solution)/shard_map/ppermute | solution.py:19
  35.5 0.8 %collective-permute-start.18 = (bf16[224,128]{1,0:T(8,128)(2,1)S(1)}, bf16[224,128]{1,0:T(8,128)(2,1)S(1)}, u32[]{:S(2)}, u32[]{:S(2)}) collective-permute-start(bf16[224,128]{1,0:T(8,128)(2,1)S(1)} %add_convert_fusion.4), channel_id=1, source_target_pairs={{0,4},{1,5},{2,6},{3,7},{4,0},{5,1},{6,2},{7,3},{8,12},{9,13},{10,... | collective-permute-start | bytes 172040 | tf_op jit(solution)/shard_map/ppermute | solution.py:19
  36.4 1.7 %collective-permute-start.22 = (bf16[432,128]{1,0:T(8,128)(2,1)S(1)}, bf16[432,128]{1,0:T(8,128)(2,1)S(1)}, u32[]{:S(2)}, u32[]{:S(2)}) collective-permute-start(bf16[432,128]{1,0:T(8,128)(2,1)S(1)} %add_convert_fusion.1), channel_id=1, source_target_pairs={{0,4},{1,5},{2,6},{3,7},{4,0},{5,1},{6,2},{7,3},{8,12},{9,13},{10,... | collective-permute-start | bytes 331784 | tf_op jit(solution)/shard_map/ppermute | solution.py:19
  38.0 3.1 %collective-permute-start.11 = (bf16[128,128]{1,0:T(8,128)(2,1)S(1)}, bf16[128,128]{1,0:T(8,128)(2,1)S(1)}, u32[]{:S(2)}, u32[]{:S(2)}) collective-permute-start(bf16[128,128]{1,0:T(8,128)(2,1)S(1)} %get-tuple-element.90), channel_id=1, source_target_pairs={{0,1},{1,0},{2,3},{3,2},{4,5},{5,4},{6,7},{7,6},{8,9},{9,8},{10,11... | collective-permute-start | bytes 98312 | tf_op jit(solution)/shard_map/ppermute | solution.py:19
  41.2 2.3 %collective-permute-start.21 = (bf16[224,128]{1,0:T(8,128)(2,1)S(1)}, bf16[224,128]{1,0:T(8,128)(2,1)S(1)}, u32[]{:S(2)}, u32[]{:S(2)}) collective-permute-start(bf16[224,128]{1,0:T(8,128)(2,1)S(1)} %add_convert_fusion.3.mine), channel_id=1, source_target_pairs={{0,3},{1,2},{2,1},{3,0},{4,7},{5,6},{6,5},{7,4},{8,11},{9,10},{10,... | collective-permute-start | bytes 172040 | tf_op jit(solution)/shard_map/ppermute | solution.py:19
  43.4 2.0 %collective-permute-start.20 = (bf16[224,128]{1,0:T(8,128)(2,1)S(1)}, bf16[224,128]{1,0:T(8,128)(2,1)S(1)}, u32[]{:S(2)}, u32[]{:S(2)}) collective-permute-start(bf16[224,128]{1,0:T(8,128)(2,1)S(1)} %add_convert_fusion.3.mine), channel_id=1, source_target_pairs={{0,2},{1,3},{2,0},{3,1},{4,6},{5,7},{6,4},{7,5},{8,10},{9,11},{10,... | collective-permute-start | bytes 172040 | tf_op jit(solution)/shard_map/ppermute | solution.py:19
  45.5 1.0 %collective-permute-start.19 = (bf16[224,128]{1,0:T(8,128)(2,1)S(1)}, bf16[224,128]{1,0:T(8,128)(2,1)S(1)}, u32[]{:S(2)}, u32[]{:S(2)}) collective-permute-start(bf16[224,128]{1,0:T(8,128)(2,1)S(1)} %add_convert_fusion.3.mine), channel_id=1, source_target_pairs={{0,1},{1,0},{2,3},{3,2},{4,5},{5,4},{6,7},{7,6},{8,9},{9,8},{10,11... | collective-permute-start | bytes 172040 | tf_op jit(solution)/shard_map/ppermute | solution.py:19
  46.5 0.1 collective-permute-start.23
  46.6 1.9 %collective-permute-done.20.far_off = bf16[224,128]{1,0:T(8,128)(2,1)S(1)} collective-permute-done((bf16[224,128]{1,0:T(8,128)(2,1)S(1)}, bf16[224,128]{1,0:T(8,128)(2,1)S(1)}, u32[]{:S(2)}, u32[]{:S(2)}) %collective-permute-start.20) | collective-permute-done | bytes 57376 | tf_op jit(solution)/shard_map/ppermute | solution.py:19
  48.5 0.9 %shard_map.104 = (bf16[256,128]{1,0:T(8,128)(2,1)}, f32[864,128]{1,0:T(8,128)}) custom-call(s32[8,128]{1,0:T(8,128)S(1)} %get-tuple-element.54.count_ref, f32[256,128]{1,0:T(8,128)S(1)} %get-tuple-element.84.own, bf16[128,128]{1,0:T(8,128)(2,1)S(1)} %collective-permute-done.11.core_in, bf16[128,128]{1,0:T(8,128)(2,1)S(1)} %collective-permute-done.12.cross_in, ...), custom_call_target="tpu_custom_call" | custom-call | flops 1000000000 | bytes 3000000 | tf_op jit(solution)/shard_map/pallas_call | solution.py:442
  49.4 0.8 %shard_map.105 = f32[864,128]{1,0:T(8,128)} custom-call(bf16[432,128]{1,0:T(8,128)(2,1)S(1)} %add_convert_fusion.mine, bf16[432,128]{1,0:T(8,128)(2,1)S(1)} %collective-permute-done.23.other), custom_call_target="tpu_custom_call" | custom-call | flops 1000000000 | bytes 3000000 | tf_op jit(solution)/shard_map/pallas_call | solution.py:442
  (26 shorter events, 0.2 us)
Async XLA Ops:
  0.6 4.0 %copy-start.1 = (bf16[27,128,128]{2,1,0:T(8,128)(2,1)S(1)}, bf16[27,128,128]{2,1,0:T(8,128)(2,1)}, u32[]{:S(2)}) copy-start(bf16[27,128,128]{2,1,0:T(8,128)(2,1)} %param.10) | copy-start | bytes 2654212
  0.6 4.0 %copy-start.3 = (bf16[256,128]{1,0:T(8,128)(2,1)S(1)}, bf16[256,128]{1,0:T(8,128)(2,1)}, u32[]{:S(2)}) copy-start(bf16[256,128]{1,0:T(8,128)(2,1)} %features.7) | copy-start | bytes 196612
  1.8 4.0 %collective-permute-start = (bf16[144,128]{1,0:T(8,128)(2,1)S(1)}, bf16[144,128]{1,0:T(8,128)(2,1)S(1)}, u32[]{:S(2)}, u32[]{:S(2)}) collective-permute-start(bf16[144,128]{1,0:T(8,128)(2,1)S(1)} %get-tuple-element.55), channel_id=1, source_target_pairs={{0,1},{1,0},{2,3},{3,2},{4,5},{5,4},{6,7},{7,6},{8,9},{9,8},{10,11... | collective-permute-start | bytes 110600 | tf_op jit(solution)/shard_map/ppermute | solution.py:19
  1.9 4.6 %collective-permute-start.1 = (bf16[144,128]{1,0:T(8,128)(2,1)S(1)}, bf16[144,128]{1,0:T(8,128)(2,1)S(1)}, u32[]{:S(2)}, u32[]{:S(2)}) collective-permute-start(bf16[144,128]{1,0:T(8,128)(2,1)S(1)} %get-tuple-element.56), channel_id=1, source_target_pairs={{0,8},{1,2},{2,1},{3,4},{4,3},{5,6},{6,5},{7,15},{8,0},{9,10},{10,... | collective-permute-start | bytes 110600 | tf_op jit(solution)/shard_map/ppermute | solution.py:32
  6.5 3.3 %copy-start = (bf16[27,128,128]{2,1,0:T(8,128)(2,1)S(1)}, bf16[27,128,128]{2,1,0:T(8,128)(2,1)}, u32[]{:S(2)}) copy-start(bf16[27,128,128]{2,1,0:T(8,128)(2,1)} %param.11) | copy-start | bytes 2654212
  7.8 2.7 %collective-permute-start.2 = (bf16[128,128]{1,0:T(8,128)(2,1)S(1)}, bf16[128,128]{1,0:T(8,128)(2,1)S(1)}, u32[]{:S(2)}, u32[]{:S(2)}) collective-permute-start(bf16[128,128]{1,0:T(8,128)(2,1)S(1)} %get-tuple-element.61), channel_id=1, source_target_pairs={{0,1},{1,0},{2,3},{3,2},{4,5},{5,4},{6,7},{7,6},{8,9},{9,8},{10,11... | collective-permute-start | bytes 98312 | tf_op jit(solution)/shard_map/ppermute | solution.py:19
  8.2 3.6 %collective-permute-start.3 = (bf16[128,128]{1,0:T(8,128)(2,1)S(1)}, bf16[128,128]{1,0:T(8,128)(2,1)S(1)}, u32[]{:S(2)}, u32[]{:S(2)}) collective-permute-start(bf16[128,128]{1,0:T(8,128)(2,1)S(1)} %get-tuple-element.62), channel_id=1, source_target_pairs={{0,8},{1,2},{2,1},{3,4},{4,3},{5,6},{6,5},{7,15},{8,0},{9,10},{10,... | collective-permute-start | bytes 98312 | tf_op jit(solution)/shard_map/ppermute | solution.py:32
  9.8 2.1 %copy-start.2 = (bf16[256,128]{1,0:T(8,128)(2,1)S(1)}, bf16[256,128]{1,0:T(8,128)(2,1)}, u32[]{:S(2)}) copy-start(bf16[256,128]{1,0:T(8,128)(2,1)} %cotangent.1) | copy-start | bytes 196612
  14.9 3.9 %collective-permute-start.4 = (bf16[128,128]{1,0:T(8,128)(2,1)S(1)}, bf16[128,128]{1,0:T(8,128)(2,1)S(1)}, u32[]{:S(2)}, u32[]{:S(2)}) collective-permute-start(bf16[128,128]{1,0:T(8,128)(2,1)S(1)} %get-tuple-element.76), channel_id=1, source_target_pairs={{0,1},{1,0},{2,3},{3,2},{4,5},{5,4},{6,7},{7,6},{8,9},{9,8},{10,11... | collective-permute-start | bytes 98312 | tf_op jit(solution)/shard_map/ppermute | solution.py:19
  15.3 3.6 %collective-permute-start.5 = (bf16[128,128]{1,0:T(8,128)(2,1)S(1)}, bf16[128,128]{1,0:T(8,128)(2,1)S(1)}, u32[]{:S(2)}, u32[]{:S(2)}) collective-permute-start(bf16[128,128]{1,0:T(8,128)(2,1)S(1)} %get-tuple-element.77), channel_id=1, source_target_pairs={{0,8},{1,2},{2,1},{3,4},{4,3},{5,6},{6,5},{7,15},{8,0},{9,10},{10,... | collective-permute-start | bytes 98312 | tf_op jit(solution)/shard_map/ppermute | solution.py:32
  17.6 3.5 %collective-permute-start.13 = (bf16[1728,128]{1,0:T(8,128)(2,1)S(1)}, bf16[1728,128]{1,0:T(8,128)(2,1)S(1)}, u32[]{:S(2)}, u32[]{:S(2)}) collective-permute-start(bf16[1728,128]{1,0:T(8,128)(2,1)S(1)} %get-tuple-element.93), channel_id=1, source_target_pairs={{0,1},{1,0},{2,3},{3,2},{4,5},{5,4},{6,7},{7,6},{8,9},{9,8},{10,11... | collective-permute-start | bytes 1327112 | tf_op jit(solution)/shard_map/ppermute | solution.py:19
  20.6 1.9 %collective-permute-start.6 = (bf16[1728,128]{1,0:T(8,128)(2,1)S(1)}, bf16[1728,128]{1,0:T(8,128)(2,1)S(1)}, u32[]{:S(2)}, u32[]{:S(2)}) collective-permute-start(bf16[1728,128]{1,0:T(8,128)(2,1)S(1)} %get-tuple-element.80), channel_id=1, source_target_pairs={{0,1},{1,0},{2,3},{3,2},{4,5},{5,4},{6,7},{7,6},{8,9},{9,8},{10,11... | collective-permute-start | bytes 1327112 | tf_op jit(solution)/shard_map/ppermute | solution.py:19
  21.2 7.1 %collective-permute-start.14 = (bf16[896,128]{1,0:T(8,128)(2,1)S(1)}, bf16[896,128]{1,0:T(8,128)(2,1)S(1)}, u32[]{:S(2)}, u32[]{:S(2)}) collective-permute-start(bf16[896,128]{1,0:T(8,128)(2,1)S(1)} %get-tuple-element.96), channel_id=1, source_target_pairs={{0,2},{1,3},{2,0},{3,1},{4,6},{5,7},{6,4},{7,5},{8,10},{9,11},{10,... | collective-permute-start | bytes 688136 | tf_op jit(solution)/shard_map/ppermute | solution.py:19
  22.6 9.3 %collective-permute-start.9 = (bf16[432,128]{1,0:T(8,128)(2,1)S(1)}, bf16[432,128]{1,0:T(8,128)(2,1)S(1)}, u32[]{:S(2)}, u32[]{:S(2)}) collective-permute-start(bf16[432,128]{1,0:T(8,128)(2,1)S(1)} %get-tuple-element.81), channel_id=1, source_target_pairs={{0,24},{8,16},{16,8},{24,0},{1,25},{9,17},{17,9},{25,1},{2,26},{10... | collective-permute-start | bytes 331784 | tf_op jit(solution)/shard_map/ppermute | solution.py:19
  25.3 6.1 %collective-permute-start.7 = (bf16[432,128]{1,0:T(8,128)(2,1)S(1)}, bf16[432,128]{1,0:T(8,128)(2,1)S(1)}, u32[]{:S(2)}, u32[]{:S(2)}) collective-permute-start(bf16[432,128]{1,0:T(8,128)(2,1)S(1)} %get-tuple-element.86), channel_id=1, source_target_pairs={{0,8},{8,0},{16,24},{24,16},{1,9},{9,1},{17,25},{25,17},{2,10},{10... | collective-permute-start | bytes 331784 | tf_op jit(solution)/shard_map/ppermute | solution.py:19
  25.6 6.3 %collective-permute-start.8 = (bf16[432,128]{1,0:T(8,128)(2,1)S(1)}, bf16[432,128]{1,0:T(8,128)(2,1)S(1)}, u32[]{:S(2)}, u32[]{:S(2)}) collective-permute-start(bf16[432,128]{1,0:T(8,128)(2,1)S(1)} %get-tuple-element.87), channel_id=1, source_target_pairs={{0,16},{8,24},{16,0},{24,8},{1,17},{9,25},{17,1},{25,9},{2,18},{10... | collective-permute-start | bytes 331784 | tf_op jit(solution)/shard_map/ppermute | solution.py:19
  28.4 3.9 %collective-permute-start.15 = (bf16[224,128]{1,0:T(8,128)(2,1)S(1)}, bf16[224,128]{1,0:T(8,128)(2,1)S(1)}, u32[]{:S(2)}, u32[]{:S(2)}) collective-permute-start(bf16[224,128]{1,0:T(8,128)(2,1)S(1)} %get-tuple-element.98), channel_id=1, source_target_pairs={{0,8},{8,0},{16,24},{24,16},{1,9},{9,1},{17,25},{25,17},{2,10},{10... | collective-permute-start | bytes 172040 | tf_op jit(solution)/shard_map/ppermute | solution.py:19
  30.2 3.0 %collective-permute-start.16 = (bf16[224,128]{1,0:T(8,128)(2,1)S(1)}, bf16[224,128]{1,0:T(8,128)(2,1)S(1)}, u32[]{:S(2)}, u32[]{:S(2)}) collective-permute-start(bf16[224,128]{1,0:T(8,128)(2,1)S(1)} %get-tuple-element.99), channel_id=1, source_target_pairs={{0,16},{8,24},{16,0},{24,8},{1,17},{9,25},{17,1},{25,9},{2,18},{10... | collective-permute-start | bytes 172040 | tf_op jit(solution)/shard_map/ppermute | solution.py:19
  31.4 4.0 %collective-permute-start.17 = (bf16[224,128]{1,0:T(8,128)(2,1)S(1)}, bf16[224,128]{1,0:T(8,128)(2,1)S(1)}, u32[]{:S(2)}, u32[]{:S(2)}) collective-permute-start(bf16[224,128]{1,0:T(8,128)(2,1)S(1)} %get-tuple-element.100), channel_id=1, source_target_pairs={{0,24},{8,16},{16,8},{24,0},{1,25},{9,17},{17,9},{25,1},{2,26},{10... | collective-permute-start | bytes 172040 | tf_op jit(solution)/shard_map/ppermute | solution.py:19
  32.0 4.3 %collective-permute-start.10 = (bf16[432,128]{1,0:T(8,128)(2,1)S(1)}, bf16[432,128]{1,0:T(8,128)(2,1)S(1)}, u32[]{:S(2)}, u32[]{:S(2)}) collective-permute-start(bf16[432,128]{1,0:T(8,128)(2,1)S(1)} %add_convert_fusion.2), channel_id=1, source_target_pairs={{0,2},{1,3},{2,0},{3,1},{4,6},{5,7},{6,4},{7,5},{8,10},{9,11},{10,... | collective-permute-start | bytes 331784 | tf_op jit(solution)/shard_map/ppermute | solution.py:19
  35.5 5.7 %collective-permute-start.18 = (bf16[224,128]{1,0:T(8,128)(2,1)S(1)}, bf16[224,128]{1,0:T(8,128)(2,1)S(1)}, u32[]{:S(2)}, u32[]{:S(2)}) collective-permute-start(bf16[224,128]{1,0:T(8,128)(2,1)S(1)} %add_convert_fusion.4), channel_id=1, source_target_pairs={{0,4},{1,5},{2,6},{3,7},{4,0},{5,1},{6,2},{7,3},{8,12},{9,13},{10,... | collective-permute-start | bytes 172040 | tf_op jit(solution)/shard_map/ppermute | solution.py:19
  36.4 9.1 %collective-permute-start.22 = (bf16[432,128]{1,0:T(8,128)(2,1)S(1)}, bf16[432,128]{1,0:T(8,128)(2,1)S(1)}, u32[]{:S(2)}, u32[]{:S(2)}) collective-permute-start(bf16[432,128]{1,0:T(8,128)(2,1)S(1)} %add_convert_fusion.1), channel_id=1, source_target_pairs={{0,4},{1,5},{2,6},{3,7},{4,0},{5,1},{6,2},{7,3},{8,12},{9,13},{10,... | collective-permute-start | bytes 331784 | tf_op jit(solution)/shard_map/ppermute | solution.py:19
  38.0 8.5 %collective-permute-start.11 = (bf16[128,128]{1,0:T(8,128)(2,1)S(1)}, bf16[128,128]{1,0:T(8,128)(2,1)S(1)}, u32[]{:S(2)}, u32[]{:S(2)}) collective-permute-start(bf16[128,128]{1,0:T(8,128)(2,1)S(1)} %get-tuple-element.90), channel_id=1, source_target_pairs={{0,1},{1,0},{2,3},{3,2},{4,5},{5,4},{6,7},{7,6},{8,9},{9,8},{10,11... | collective-permute-start | bytes 98312 | tf_op jit(solution)/shard_map/ppermute | solution.py:19
  41.1 5.5 %collective-permute-start.12 = (bf16[128,128]{1,0:T(8,128)(2,1)S(1)}, bf16[128,128]{1,0:T(8,128)(2,1)S(1)}, u32[]{:S(2)}, u32[]{:S(2)}) collective-permute-start(bf16[128,128]{1,0:T(8,128)(2,1)S(1)} %get-tuple-element.91), channel_id=1, source_target_pairs={{0,8},{1,2},{2,1},{3,4},{4,3},{5,6},{6,5},{7,15},{8,0},{9,10},{10,... | collective-permute-start | bytes 98312 | tf_op jit(solution)/shard_map/ppermute | solution.py:32
  41.2 5.5 %collective-permute-start.21 = (bf16[224,128]{1,0:T(8,128)(2,1)S(1)}, bf16[224,128]{1,0:T(8,128)(2,1)S(1)}, u32[]{:S(2)}, u32[]{:S(2)}) collective-permute-start(bf16[224,128]{1,0:T(8,128)(2,1)S(1)} %add_convert_fusion.3.mine), channel_id=1, source_target_pairs={{0,3},{1,2},{2,1},{3,0},{4,7},{5,6},{6,5},{7,4},{8,11},{9,10},{10,... | collective-permute-start | bytes 172040 | tf_op jit(solution)/shard_map/ppermute | solution.py:19
  43.4 5.1 %collective-permute-start.20 = (bf16[224,128]{1,0:T(8,128)(2,1)S(1)}, bf16[224,128]{1,0:T(8,128)(2,1)S(1)}, u32[]{:S(2)}, u32[]{:S(2)}) collective-permute-start(bf16[224,128]{1,0:T(8,128)(2,1)S(1)} %add_convert_fusion.3.mine), channel_id=1, source_target_pairs={{0,2},{1,3},{2,0},{3,1},{4,6},{5,7},{6,4},{7,5},{8,10},{9,11},{10,... | collective-permute-start | bytes 172040 | tf_op jit(solution)/shard_map/ppermute | solution.py:19
  45.5 3.1 %collective-permute-start.19 = (bf16[224,128]{1,0:T(8,128)(2,1)S(1)}, bf16[224,128]{1,0:T(8,128)(2,1)S(1)}, u32[]{:S(2)}, u32[]{:S(2)}) collective-permute-start(bf16[224,128]{1,0:T(8,128)(2,1)S(1)} %add_convert_fusion.3.mine), channel_id=1, source_target_pairs={{0,1},{1,0},{2,3},{3,2},{4,5},{5,4},{6,7},{7,6},{8,9},{9,8},{10,11... | collective-permute-start | bytes 172040 | tf_op jit(solution)/shard_map/ppermute | solution.py:19
  46.5 2.9 %collective-permute-start.23 = (bf16[432,128]{1,0:T(8,128)(2,1)S(1)}, bf16[432,128]{1,0:T(8,128)(2,1)S(1)}, u32[]{:S(2)}, u32[]{:S(2)}) collective-permute-start(bf16[432,128]{1,0:T(8,128)(2,1)S(1)} %add_convert_fusion.mine), channel_id=1, source_target_pairs={{0,1},{1,0},{2,3},{3,2},{4,5},{5,4},{6,7},{7,6},{8,9},{9,8},{10,11... | collective-permute-start | bytes 331784 | tf_op jit(solution)/shard_map/ppermute | solution.py:19

commit v8 on v7

--- a/solution.py
+++ b/solution.py
@@ -581,7 +581,7 @@
     two = two.astype(BF16)
     core, cross = lax.optimization_barrier((one, core, cross))[1:]
     cross, core = crossed(cross), swapped(core, "tile", 1)
-    near, far_off, both_off = [swapped(two, "tile", bits) for bits in (1, steps[0], steps[0] + 1)]
+    both_off, far_off, near = [swapped(two, "tile", bits) for bits in (steps[0] + 1, steps[0], 1)]
     scale = float(n_grp * n_tile * rows) ** (-0.5)
     shard_out = ((2 * half, channels), F32)
     input_grad, two = call(

time: 50.7 us -> 50.7 us (level)
  no operation moved by 1% of the time
where the time goes in v8:
time: 50.7 us; the launch traced here: 50.2 us
  starting transfers between devices  26.3 us (52%)
  Pallas kernels  12.8 us (25%)
  waiting for transfers between devices  10.2 us (20%)
  between operations  0.8 us (2%)
    ppermute x20, starting transfers between devices, swapped(): lax.ppermute(value, axis, [(i, i ^ bits) for i in range(count) if i ^ bit...  21 us
    pallas_call x13, Pallas kernels, call(): pl.pallas_call(kernel, out_shape=[jax.ShapeDtypeStruct(shape, kind) for s...  12.8 us
    ppermute x20, waiting for transfers between devices, swapped(): lax.ppermute(value, axis, [(i, i ^ bits) for i in range(count) if i ^ bit...  7.95 us
    ppermute x4, starting transfers between devices, crossed(): return lax.ppermute(value, ('grp', 'tile'), pairs)  5.27 us
    ppermute x4, waiting for transfers between devices, crossed(): return lax.ppermute(value, ('grp', 'tile'), pairs)  2.21 us
  transfers between devices with their start and end apart: 24, of which 8 were waited for; matrix products, arithmetic and copies ran while one was open for 0% of the time, Pallas kernels for 13%

profile of v8, /device:TPU:1, one launch (start us, length us, event | category | flops | bytes accessed | tf_op | source)
XLA Modules:
  0.0 50.2 jit_solution(5058868722144089678)
XLA Ops:
  0.7 1.1 %shard_map.93 = (f32[40,128]{1,0:T(8,128)S(1)}, bf16[144,128]{1,0:T(8,128)(2,1)S(1)}, bf16[144,128]{1,0:T(8,128)(2,1)S(1)}, s32[8,128]{1,0:T(8,128)S(1)}) custom-call(bf16[256,128]{1,0:T(8,128)(2,1)} %features.7, s32[27,2,128]{2,1,0:T(2,128)} %rows_in.1, s32[2,27]{1,0:T(2,128)} %bitcast.9), custom_call_target="tpu_custom_call" | custom-call | flops 3000000000 | bytes 9000000 | tf_op jit(solution)/shard_map/pallas_call | solution.py:442
  1.8 0.1 collective-permute-start
  1.9 2.7 %collective-permute-start.1 = (bf16[144,128]{1,0:T(8,128)(2,1)S(1)}, bf16[144,128]{1,0:T(8,128)(2,1)S(1)}, u32[]{:S(2)}, u32[]{:S(2)}) collective-permute-start(bf16[144,128]{1,0:T(8,128)(2,1)S(1)} %get-tuple-element.56), channel_id=1, source_target_pairs={{0,8},{1,2},{2,1},{3,4},{4,3},{5,6},{6,5},{7,15},{8,0},{9,10},{10,... | collective-permute-start | bytes 110600 | tf_op jit(solution)/shard_map/ppermute | solution.py:32
  4.6 1.1 %shard_map.94 = (bf16[9,256,256]{2,1,0:T(8,128)(2,1)S(1)}, bf16[18,256,128]{2,1,0:T(8,128)(2,1)S(1)}, bf16[9,256,256]{2,1,0:T(8,128)(2,1)S(1)}, bf16[18,128,256]{2,1,0:T(8,128)(2,1)S(1)}, f32[256,128]{1,0:T(8,128)S(1)}) custom-call(f32[40,128]{1,0:T(8,128)S(1)} %get-tuple-element.57.near, bf16[256,128]{1,0:T(8,128)(2,1)S(1)} %copy-done.3, ...), custom_call_target="tpu_custom_call" | custom-call | flops 2000000000 | bytes 6000000 | tf_op jit(solution)/shard_map/pallas_call | solution.py:442
  5.8 0.7 %collective-permute-done.1.cross_in = bf16[144,128]{1,0:T(8,128)(2,1)S(1)} collective-permute-done((bf16[144,128]{1,0:T(8,128)(2,1)S(1)}, bf16[144,128]{1,0:T(8,128)(2,1)S(1)}, u32[]{:S(2)}, u32[]{:S(2)}) %collective-permute-start.1) | collective-permute-done | bytes 36896 | tf_op jit(solution)/shard_map/ppermute | solution.py:32
  6.5 1.3 %shard_map.95 = (f32[24,128]{1,0:T(8,128)S(1)}, bf16[18,256,128]{2,1,0:T(8,128)(2,1)S(1)}, bf16[2,128,128]{2,1,0:T(8,128)(2,1)S(1)}, bf16[256,128]{1,0:T(8,128)(...) custom-call(s32[8,128]{1,0:T(8,128)S(1)} %get-tuple-element.54.count_ref, ...), custom_call_target="tpu_custom_call" | custom-call | flops 2000000000 | bytes 6000000 | tf_op jit(solution)/shard_map/pallas_call | solution.py:442
  7.8 0.5 collective-permute-start.2
  8.2 1.6 %collective-permute-start.3 = (bf16[128,128]{1,0:T(8,128)(2,1)S(1)}, bf16[128,128]{1,0:T(8,128)(2,1)S(1)}, u32[]{:S(2)}, u32[]{:S(2)}) collective-permute-start(bf16[128,128]{1,0:T(8,128)(2,1)S(1)} %get-tuple-element.62), channel_id=1, source_target_pairs={{0,8},{1,2},{2,1},{3,4},{4,3},{5,6},{6,5},{7,15},{8,0},{9,10},{10,... | collective-permute-start | bytes 98312 | tf_op jit(solution)/shard_map/ppermute | solution.py:32
  9.8 0.7 %shard_map.96 = (f32[256,128]{1,0:T(8,128)S(1)}, bf16[18,128,256]{2,1,0:T(8,128)(2,1)S(1)}) custom-call(bf16[256,128]{1,0:T(8,128)(2,1)S(1)} %get-tuple-element.60.hidden, bf16[9,256,256]{2,1,0:T(8,128)(2,1)S(1)} %get-tuple-element.64.pairs, f32[24,128]{1,0:T(8,128)S(1)} %get-tuple-element.65.entries, bf16[3456,128]{1,0:T(8,128)(2,1)S(1)} %bitcast.3), custom_call_target="tpu_custom_call" | custom-call | flops 1000000000 | bytes 3000000 | tf_op jit(solution)/shard_map/pallas_call | solution.py:442
  10.5 0.0 collective-permute-done.2.core_in
  10.5 1.4 %collective-permute-done.3.cross_in = bf16[128,128]{1,0:T(8,128)(2,1)S(1)} collective-permute-done((bf16[128,128]{1,0:T(8,128)(2,1)S(1)}, bf16[128,128]{1,0:T(8,128)(2,1)S(1)}, u32[]{:S(2)}, u32[]{:S(2)}) %collective-permute-start.3) | collective-permute-done | bytes 32800 | tf_op jit(solution)/shard_map/ppermute | solution.py:32
  11.9 3.0 %shard_map.97 = (bf16[256,128]{1,0:T(8,128)(2,1)}, bf16[256,128]{1,0:T(8,128)(2,1)S(1)}, f32[256,128]{1,0:T(8,128)S(1)}, bf16[256,2304]{1,0:T(8,128)(2,1)S(1)}, ...) custom-call(s32[8,128]{1,0:T(8,128)S(1)} %get-tuple-element.54.count_ref, bf16[256,128]{1,0:T(8,128)(2,1)S(1)} %copy-done.3, ...), custom_call_target="tpu_custom_call" | custom-call | flops 3000000000 | bytes 9000000 | tf_op jit(solution)/shard_map/pallas_call | solution.py:442
  14.9 0.4 collective-permute-start.4
  15.3 1.0 %collective-permute-start.5 = (bf16[128,128]{1,0:T(8,128)(2,1)S(1)}, bf16[128,128]{1,0:T(8,128)(2,1)S(1)}, u32[]{:S(2)}, u32[]{:S(2)}) collective-permute-start(bf16[128,128]{1,0:T(8,128)(2,1)S(1)} %get-tuple-element.77), channel_id=1, source_target_pairs={{0,8},{1,2},{2,1},{3,4},{4,3},{5,6},{6,5},{7,15},{8,0},{9,10},{10,... | collective-permute-start | bytes 98312 | tf_op jit(solution)/shard_map/ppermute | solution.py:32
  16.3 1.3 %shard_map.98 = (f32[256,128]{1,0:T(8,128)S(1)}, f32[4,432,128]{2,1,0:T(8,128)S(1)}, bf16[1728,128]{1,0:T(8,128)(2,1)S(1)}) custom-call(bf16[256,128]{1,0:T(8,128)(2,1)S(1)} %get-tuple-element.60.hidden, bf16[128,128]{1,0:T(8,128)(2,1)S(1)} %collective-permute-done.2.core_in, bf16[128,128]{1,0:T(8,128)(2,1)S(1)} %collective-permute-done.3.cross_in, ...), custom_call_target="tpu_custom_call" | custom-call | flops 1000000000 | bytes 3000000 | tf_op jit(solution)/shard_map/pallas_call | solution.py:442
  17.6 1.2 %collective-permute-start.13 = (bf16[1728,128]{1,0:T(8,128)(2,1)S(1)}, bf16[1728,128]{1,0:T(8,128)(2,1)S(1)}, u32[]{:S(2)}, u32[]{:S(2)}) collective-permute-start(bf16[1728,128]{1,0:T(8,128)(2,1)S(1)} %get-tuple-element.93), channel_id=1, source_target_pairs={{0,1},{1,0},{2,3},{3,2},{4,5},{5,4},{6,7},{7,6},{8,9},{9,8},{10,11... | collective-permute-start | bytes 1327112 | tf_op jit(solution)/shard_map/ppermute | solution.py:19
  18.8 0.1 collective-permute-done.5.cross_in
  18.9 1.7 %shard_map.99 = (bf16[256,3456]{1,0:T(8,128)(2,1)S(1)}, f32[4,432,128]{2,1,0:T(8,128)S(1)}, bf16[1728,128]{1,0:T(8,128)(2,1)S(1)}) custom-call(s32[8,128]{1,0:T(8,128)S(1)} %get-tuple-element.54.count_ref, bf16[256,128]{1,0:T(8,128)(2,1)S(1)} %copy-done.3, bf16[2,128,128]{2,1,0:T(8,128)(2,1)S(1)} %get-tuple-element.70.halo, ...), custom_call_target="tpu_custom_call" | custom-call | flops 2000000000 | bytes 6000000 | tf_op jit(solution)/shard_map/pallas_call | solution.py:442
  20.6 0.5 collective-permute-start.6
  21.1 0.0 collective-permute-done.13.core
  21.1 0.1 shard_map.102
  21.2 0.5 collective-permute-start.14
  21.7 0.8 %collective-permute-done.6.core = bf16[1728,128]{1,0:T(8,128)(2,1)S(1)} collective-permute-done((bf16[1728,128]{1,0:T(8,128)(2,1)S(1)}, bf16[1728,128]{1,0:T(8,128)(2,1)S(1)}, u32[]{:S(2)}, u32[]{:S(2)}) %collective-permute-start.6) | collective-permute-done | bytes 442400 | tf_op jit(solution)/shard_map/ppermute | solution.py:19
  22.5 0.1 shard_map.100
  22.6 2.8 %collective-permute-start.9 = (bf16[432,128]{1,0:T(8,128)(2,1)S(1)}, bf16[432,128]{1,0:T(8,128)(2,1)S(1)}, u32[]{:S(2)}, u32[]{:S(2)}) collective-permute-start(bf16[432,128]{1,0:T(8,128)(2,1)S(1)} %get-tuple-element.81), channel_id=1, source_target_pairs={{0,24},{8,16},{16,8},{24,0},{1,25},{9,17},{17,9},{25,1},{2,26},{10... | collective-permute-start | bytes 331784 | tf_op jit(solution)/shard_map/ppermute | solution.py:19
  25.3 0.3 collective-permute-start.7
  25.6 0.1 collective-permute-start.8
  25.7 0.6 %shard_map.101 = (f32[256,128]{1,0:T(8,128)S(1)}, bf16[128,128]{1,0:T(8,128)(2,1)S(1)}, bf16[128,128]{1,0:T(8,128)(2,1)S(1)}) custom-call(s32[8,128]{1,0:T(8,128)S(1)} %get-tuple-element.54.count_ref, bf16[256,3456]{1,0:T(8,128)(2,1)S(1)} %get-tuple-element.83.pulled, bf16[3456,128]{1,0:T(8,128)(2,1)S(1)} %bitcast.8, ...), custom_call_target="tpu_custom_call" | custom-call | flops 1000000000 | bytes 3000000 | tf_op jit(solution)/shard_map/pallas_call | solution.py:442
  26.3 2.0 %collective-permute-done.14.core = bf16[896,128]{1,0:T(8,128)(2,1)S(1)} collective-permute-done((bf16[896,128]{1,0:T(8,128)(2,1)S(1)}, bf16[896,128]{1,0:T(8,128)(2,1)S(1)}, u32[]{:S(2)}, u32[]{:S(2)}) %collective-permute-start.14) | collective-permute-done | bytes 229408 | tf_op jit(solution)/shard_map/ppermute | solution.py:19
  28.4 1.8 %collective-permute-start.15 = (bf16[224,128]{1,0:T(8,128)(2,1)S(1)}, bf16[224,128]{1,0:T(8,128)(2,1)S(1)}, u32[]{:S(2)}, u32[]{:S(2)}) collective-permute-start(bf16[224,128]{1,0:T(8,128)(2,1)S(1)} %get-tuple-element.98), channel_id=1, source_target_pairs={{0,8},{8,0},{16,24},{24,16},{1,9},{9,1},{17,25},{25,17},{2,10},{10... | collective-permute-start | bytes 172040 | tf_op jit(solution)/shard_map/ppermute | solution.py:19
  30.2 1.2 %collective-permute-start.16 = (bf16[224,128]{1,0:T(8,128)(2,1)S(1)}, bf16[224,128]{1,0:T(8,128)(2,1)S(1)}, u32[]{:S(2)}, u32[]{:S(2)}) collective-permute-start(bf16[224,128]{1,0:T(8,128)(2,1)S(1)} %get-tuple-element.99), channel_id=1, source_target_pairs={{0,16},{8,24},{16,0},{24,8},{1,17},{9,25},{17,1},{25,9},{2,18},{10... | collective-permute-start | bytes 172040 | tf_op jit(solution)/shard_map/ppermute | solution.py:19
  31.4 0.0 collective-permute-done.7
  31.4 0.5 %collective-permute-start.17 = (bf16[224,128]{1,0:T(8,128)(2,1)S(1)}, bf16[224,128]{1,0:T(8,128)(2,1)S(1)}, u32[]{:S(2)}, u32[]{:S(2)}) collective-permute-start(bf16[224,128]{1,0:T(8,128)(2,1)S(1)} %get-tuple-element.100), channel_id=1, source_target_pairs={{0,24},{8,16},{16,8},{24,0},{1,25},{9,17},{17,9},{25,1},{2,26},{10... | collective-permute-start | bytes 172040 | tf_op jit(solution)/shard_map/ppermute | solution.py:19
  31.9 0.0 collective-permute-done.8
  31.9 0.1 add_convert_fusion.2
  32.0 0.2 collective-permute-start.10
  32.2 1.0 %collective-permute-done.16 = bf16[224,128]{1,0:T(8,128)(2,1)S(1)} collective-permute-done((bf16[224,128]{1,0:T(8,128)(2,1)S(1)}, bf16[224,128]{1,0:T(8,128)(2,1)S(1)}, u32[]{:S(2)}, u32[]{:S(2)}) %collective-permute-start.16) | collective-permute-done | bytes 57376 | tf_op jit(solution)/shard_map/ppermute | solution.py:19
  33.2 2.2 %collective-permute-done.17 = bf16[224,128]{1,0:T(8,128)(2,1)S(1)} collective-permute-done((bf16[224,128]{1,0:T(8,128)(2,1)S(1)}, bf16[224,128]{1,0:T(8,128)(2,1)S(1)}, u32[]{:S(2)}, u32[]{:S(2)}) %collective-permute-start.17) | collective-permute-done | bytes 57376 | tf_op jit(solution)/shard_map/ppermute | solution.py:19
  35.5 0.8 %collective-permute-start.18 = (bf16[224,128]{1,0:T(8,128)(2,1)S(1)}, bf16[224,128]{1,0:T(8,128)(2,1)S(1)}, u32[]{:S(2)}, u32[]{:S(2)}) collective-permute-start(bf16[224,128]{1,0:T(8,128)(2,1)S(1)} %add_convert_fusion.4), channel_id=1, source_target_pairs={{0,4},{1,5},{2,6},{3,7},{4,0},{5,1},{6,2},{7,3},{8,12},{9,13},{10,... | collective-permute-start | bytes 172040 | tf_op jit(solution)/shard_map/ppermute | solution.py:19
  36.4 1.7 %collective-permute-start.22 = (bf16[432,128]{1,0:T(8,128)(2,1)S(1)}, bf16[432,128]{1,0:T(8,128)(2,1)S(1)}, u32[]{:S(2)}, u32[]{:S(2)}) collective-permute-start(bf16[432,128]{1,0:T(8,128)(2,1)S(1)} %add_convert_fusion.1), channel_id=1, source_target_pairs={{0,4},{1,5},{2,6},{3,7},{4,0},{5,1},{6,2},{7,3},{8,12},{9,13},{10,... | collective-permute-start | bytes 331784 | tf_op jit(solution)/shard_map/ppermute | solution.py:19
  38.0 3.1 %collective-permute-start.11 = (bf16[128,128]{1,0:T(8,128)(2,1)S(1)}, bf16[128,128]{1,0:T(8,128)(2,1)S(1)}, u32[]{:S(2)}, u32[]{:S(2)}) collective-permute-start(bf16[128,128]{1,0:T(8,128)(2,1)S(1)} %get-tuple-element.90), channel_id=1, source_target_pairs={{0,1},{1,0},{2,3},{3,2},{4,5},{5,4},{6,7},{7,6},{8,9},{9,8},{10,11... | collective-permute-start | bytes 98312 | tf_op jit(solution)/shard_map/ppermute | solution.py:19
  41.2 2.3 %collective-permute-start.21 = (bf16[224,128]{1,0:T(8,128)(2,1)S(1)}, bf16[224,128]{1,0:T(8,128)(2,1)S(1)}, u32[]{:S(2)}, u32[]{:S(2)}) collective-permute-start(bf16[224,128]{1,0:T(8,128)(2,1)S(1)} %add_convert_fusion.3.mine), channel_id=1, source_target_pairs={{0,3},{1,2},{2,1},{3,0},{4,7},{5,6},{6,5},{7,4},{8,11},{9,10},{10,... | collective-permute-start | bytes 172040 | tf_op jit(solution)/shard_map/ppermute | solution.py:19
  43.4 2.0 %collective-permute-start.20 = (bf16[224,128]{1,0:T(8,128)(2,1)S(1)}, bf16[224,128]{1,0:T(8,128)(2,1)S(1)}, u32[]{:S(2)}, u32[]{:S(2)}) collective-permute-start(bf16[224,128]{1,0:T(8,128)(2,1)S(1)} %add_convert_fusion.3.mine), channel_id=1, source_target_pairs={{0,2},{1,3},{2,0},{3,1},{4,6},{5,7},{6,4},{7,5},{8,10},{9,11},{10,... | collective-permute-start | bytes 172040 | tf_op jit(solution)/shard_map/ppermute | solution.py:19
  45.5 1.0 %collective-permute-start.19 = (bf16[224,128]{1,0:T(8,128)(2,1)S(1)}, bf16[224,128]{1,0:T(8,128)(2,1)S(1)}, u32[]{:S(2)}, u32[]{:S(2)}) collective-permute-start(bf16[224,128]{1,0:T(8,128)(2,1)S(1)} %add_convert_fusion.3.mine), channel_id=1, source_target_pairs={{0,1},{1,0},{2,3},{3,2},{4,5},{5,4},{6,7},{7,6},{8,9},{9,8},{10,11... | collective-permute-start | bytes 172040 | tf_op jit(solution)/shard_map/ppermute | solution.py:19
  46.5 0.1 collective-permute-start.23
  46.6 1.9 %collective-permute-done.20.far_off = bf16[224,128]{1,0:T(8,128)(2,1)S(1)} collective-permute-done((bf16[224,128]{1,0:T(8,128)(2,1)S(1)}, bf16[224,128]{1,0:T(8,128)(2,1)S(1)}, u32[]{:S(2)}, u32[]{:S(2)}) %collective-permute-start.20) | collective-permute-done | bytes 57376 | tf_op jit(solution)/shard_map/ppermute | solution.py:19
  48.5 0.9 %shard_map.104 = (bf16[256,128]{1,0:T(8,128)(2,1)}, f32[864,128]{1,0:T(8,128)}) custom-call(s32[8,128]{1,0:T(8,128)S(1)} %get-tuple-element.54.count_ref, f32[256,128]{1,0:T(8,128)S(1)} %get-tuple-element.84.own, bf16[128,128]{1,0:T(8,128)(2,1)S(1)} %collective-permute-done.11.core_in, bf16[128,128]{1,0:T(8,128)(2,1)S(1)} %collective-permute-done.12.cross_in, ...), custom_call_target="tpu_custom_call" | custom-call | flops 1000000000 | bytes 3000000 | tf_op jit(solution)/shard_map/pallas_call | solution.py:442
  49.4 0.8 %shard_map.105 = f32[864,128]{1,0:T(8,128)} custom-call(bf16[432,128]{1,0:T(8,128)(2,1)S(1)} %add_convert_fusion.mine, bf16[432,128]{1,0:T(8,128)(2,1)S(1)} %collective-permute-done.23.other), custom_call_target="tpu_custom_call" | custom-call | flops 1000000000 | bytes 3000000 | tf_op jit(solution)/shard_map/pallas_call | solution.py:442
  (26 shorter events, 0.2 us)
Async XLA Ops:
  0.6 4.0 %copy-start.1 = (bf16[27,128,128]{2,1,0:T(8,128)(2,1)S(1)}, bf16[27,128,128]{2,1,0:T(8,128)(2,1)}, u32[]{:S(2)}) copy-start(bf16[27,128,128]{2,1,0:T(8,128)(2,1)} %param.10) | copy-start | bytes 2654212
  0.6 4.0 %copy-start.3 = (bf16[256,128]{1,0:T(8,128)(2,1)S(1)}, bf16[256,128]{1,0:T(8,128)(2,1)}, u32[]{:S(2)}) copy-start(bf16[256,128]{1,0:T(8,128)(2,1)} %features.7) | copy-start | bytes 196612
  1.8 4.0 %collective-permute-start = (bf16[144,128]{1,0:T(8,128)(2,1)S(1)}, bf16[144,128]{1,0:T(8,128)(2,1)S(1)}, u32[]{:S(2)}, u32[]{:S(2)}) collective-permute-start(bf16[144,128]{1,0:T(8,128)(2,1)S(1)} %get-tuple-element.55), channel_id=1, source_target_pairs={{0,1},{1,0},{2,3},{3,2},{4,5},{5,4},{6,7},{7,6},{8,9},{9,8},{10,11... | collective-permute-start | bytes 110600 | tf_op jit(solution)/shard_map/ppermute | solution.py:19
  1.9 4.6 %collective-permute-start.1 = (bf16[144,128]{1,0:T(8,128)(2,1)S(1)}, bf16[144,128]{1,0:T(8,128)(2,1)S(1)}, u32[]{:S(2)}, u32[]{:S(2)}) collective-permute-start(bf16[144,128]{1,0:T(8,128)(2,1)S(1)} %get-tuple-element.56), channel_id=1, source_target_pairs={{0,8},{1,2},{2,1},{3,4},{4,3},{5,6},{6,5},{7,15},{8,0},{9,10},{10,... | collective-permute-start | bytes 110600 | tf_op jit(solution)/shard_map/ppermute | solution.py:32
  6.5 3.3 %copy-start = (bf16[27,128,128]{2,1,0:T(8,128)(2,1)S(1)}, bf16[27,128,128]{2,1,0:T(8,128)(2,1)}, u32[]{:S(2)}) copy-start(bf16[27,128,128]{2,1,0:T(8,128)(2,1)} %param.11) | copy-start | bytes 2654212
  7.8 2.7 %collective-permute-start.2 = (bf16[128,128]{1,0:T(8,128)(2,1)S(1)}, bf16[128,128]{1,0:T(8,128)(2,1)S(1)}, u32[]{:S(2)}, u32[]{:S(2)}) collective-permute-start(bf16[128,128]{1,0:T(8,128)(2,1)S(1)} %get-tuple-element.61), channel_id=1, source_target_pairs={{0,1},{1,0},{2,3},{3,2},{4,5},{5,4},{6,7},{7,6},{8,9},{9,8},{10,11... | collective-permute-start | bytes 98312 | tf_op jit(solution)/shard_map/ppermute | solution.py:19
  8.2 3.6 %collective-permute-start.3 = (bf16[128,128]{1,0:T(8,128)(2,1)S(1)}, bf16[128,128]{1,0:T(8,128)(2,1)S(1)}, u32[]{:S(2)}, u32[]{:S(2)}) collective-permute-start(bf16[128,128]{1,0:T(8,128)(2,1)S(1)} %get-tuple-element.62), channel_id=1, source_target_pairs={{0,8},{1,2},{2,1},{3,4},{4,3},{5,6},{6,5},{7,15},{8,0},{9,10},{10,... | collective-permute-start | bytes 98312 | tf_op jit(solution)/shard_map/ppermute | solution.py:32
  9.8 2.1 %copy-start.2 = (bf16[256,128]{1,0:T(8,128)(2,1)S(1)}, bf16[256,128]{1,0:T(8,128)(2,1)}, u32[]{:S(2)}) copy-start(bf16[256,128]{1,0:T(8,128)(2,1)} %cotangent.1) | copy-start | bytes 196612
  14.9 3.9 %collective-permute-start.4 = (bf16[128,128]{1,0:T(8,128)(2,1)S(1)}, bf16[128,128]{1,0:T(8,128)(2,1)S(1)}, u32[]{:S(2)}, u32[]{:S(2)}) collective-permute-start(bf16[128,128]{1,0:T(8,128)(2,1)S(1)} %get-tuple-element.76), channel_id=1, source_target_pairs={{0,1},{1,0},{2,3},{3,2},{4,5},{5,4},{6,7},{7,6},{8,9},{9,8},{10,11... | collective-permute-start | bytes 98312 | tf_op jit(solution)/shard_map/ppermute | solution.py:19
  15.3 3.6 %collective-permute-start.5 = (bf16[128,128]{1,0:T(8,128)(2,1)S(1)}, bf16[128,128]{1,0:T(8,128)(2,1)S(1)}, u32[]{:S(2)}, u32[]{:S(2)}) collective-permute-start(bf16[128,128]{1,0:T(8,128)(2,1)S(1)} %get-tuple-element.77), channel_id=1, source_target_pairs={{0,8},{1,2},{2,1},{3,4},{4,3},{5,6},{6,5},{7,15},{8,0},{9,10},{10,... | collective-permute-start | bytes 98312 | tf_op jit(solution)/shard_map/ppermute | solution.py:32
  17.6 3.5 %collective-permute-start.13 = (bf16[1728,128]{1,0:T(8,128)(2,1)S(1)}, bf16[1728,128]{1,0:T(8,128)(2,1)S(1)}, u32[]{:S(2)}, u32[]{:S(2)}) collective-permute-start(bf16[1728,128]{1,0:T(8,128)(2,1)S(1)} %get-tuple-element.93), channel_id=1, source_target_pairs={{0,1},{1,0},{2,3},{3,2},{4,5},{5,4},{6,7},{7,6},{8,9},{9,8},{10,11... | collective-permute-start | bytes 1327112 | tf_op jit(solution)/shard_map/ppermute | solution.py:19
  20.6 1.9 %collective-permute-start.6 = (bf16[1728,128]{1,0:T(8,128)(2,1)S(1)}, bf16[1728,128]{1,0:T(8,128)(2,1)S(1)}, u32[]{:S(2)}, u32[]{:S(2)}) collective-permute-start(bf16[1728,128]{1,0:T(8,128)(2,1)S(1)} %get-tuple-element.80), channel_id=1, source_target_pairs={{0,1},{1,0},{2,3},{3,2},{4,5},{5,4},{6,7},{7,6},{8,9},{9,8},{10,11... | collective-permute-start | bytes 1327112 | tf_op jit(solution)/shard_map/ppermute | solution.py:19
  21.2 7.1 %collective-permute-start.14 = (bf16[896,128]{1,0:T(8,128)(2,1)S(1)}, bf16[896,128]{1,0:T(8,128)(2,1)S(1)}, u32[]{:S(2)}, u32[]{:S(2)}) collective-permute-start(bf16[896,128]{1,0:T(8,128)(2,1)S(1)} %get-tuple-element.96), channel_id=1, source_target_pairs={{0,2},{1,3},{2,0},{3,1},{4,6},{5,7},{6,4},{7,5},{8,10},{9,11},{10,... | collective-permute-start | bytes 688136 | tf_op jit(solution)/shard_map/ppermute | solution.py:19
  22.6 9.3 %collective-permute-start.9 = (bf16[432,128]{1,0:T(8,128)(2,1)S(1)}, bf16[432,128]{1,0:T(8,128)(2,1)S(1)}, u32[]{:S(2)}, u32[]{:S(2)}) collective-permute-start(bf16[432,128]{1,0:T(8,128)(2,1)S(1)} %get-tuple-element.81), channel_id=1, source_target_pairs={{0,24},{8,16},{16,8},{24,0},{1,25},{9,17},{17,9},{25,1},{2,26},{10... | collective-permute-start | bytes 331784 | tf_op jit(solution)/shard_map/ppermute | solution.py:19
  25.3 6.1 %collective-permute-start.7 = (bf16[432,128]{1,0:T(8,128)(2,1)S(1)}, bf16[432,128]{1,0:T(8,128)(2,1)S(1)}, u32[]{:S(2)}, u32[]{:S(2)}) collective-permute-start(bf16[432,128]{1,0:T(8,128)(2,1)S(1)} %get-tuple-element.86), channel_id=1, source_target_pairs={{0,8},{8,0},{16,24},{24,16},{1,9},{9,1},{17,25},{25,17},{2,10},{10... | collective-permute-start | bytes 331784 | tf_op jit(solution)/shard_map/ppermute | solution.py:19
  25.6 6.3 %collective-permute-start.8 = (bf16[432,128]{1,0:T(8,128)(2,1)S(1)}, bf16[432,128]{1,0:T(8,128)(2,1)S(1)}, u32[]{:S(2)}, u32[]{:S(2)}) collective-permute-start(bf16[432,128]{1,0:T(8,128)(2,1)S(1)} %get-tuple-element.87), channel_id=1, source_target_pairs={{0,16},{8,24},{16,0},{24,8},{1,17},{9,25},{17,1},{25,9},{2,18},{10... | collective-permute-start | bytes 331784 | tf_op jit(solution)/shard_map/ppermute | solution.py:19
  28.4 3.9 %collective-permute-start.15 = (bf16[224,128]{1,0:T(8,128)(2,1)S(1)}, bf16[224,128]{1,0:T(8,128)(2,1)S(1)}, u32[]{:S(2)}, u32[]{:S(2)}) collective-permute-start(bf16[224,128]{1,0:T(8,128)(2,1)S(1)} %get-tuple-element.98), channel_id=1, source_target_pairs={{0,8},{8,0},{16,24},{24,16},{1,9},{9,1},{17,25},{25,17},{2,10},{10... | collective-permute-start | bytes 172040 | tf_op jit(solution)/shard_map/ppermute | solution.py:19
  30.2 3.0 %collective-permute-start.16 = (bf16[224,128]{1,0:T(8,128)(2,1)S(1)}, bf16[224,128]{1,0:T(8,128)(2,1)S(1)}, u32[]{:S(2)}, u32[]{:S(2)}) collective-permute-start(bf16[224,128]{1,0:T(8,128)(2,1)S(1)} %get-tuple-element.99), channel_id=1, source_target_pairs={{0,16},{8,24},{16,0},{24,8},{1,17},{9,25},{17,1},{25,9},{2,18},{10... | collective-permute-start | bytes 172040 | tf_op jit(solution)/shard_map/ppermute | solution.py:19
  31.4 4.0 %collective-permute-start.17 = (bf16[224,128]{1,0:T(8,128)(2,1)S(1)}, bf16[224,128]{1,0:T(8,128)(2,1)S(1)}, u32[]{:S(2)}, u32[]{:S(2)}) collective-permute-start(bf16[224,128]{1,0:T(8,128)(2,1)S(1)} %get-tuple-element.100), channel_id=1, source_target_pairs={{0,24},{8,16},{16,8},{24,0},{1,25},{9,17},{17,9},{25,1},{2,26},{10... | collective-permute-start | bytes 172040 | tf_op jit(solution)/shard_map/ppermute | solution.py:19
  32.0 4.3 %collective-permute-start.10 = (bf16[432,128]{1,0:T(8,128)(2,1)S(1)}, bf16[432,128]{1,0:T(8,128)(2,1)S(1)}, u32[]{:S(2)}, u32[]{:S(2)}) collective-permute-start(bf16[432,128]{1,0:T(8,128)(2,1)S(1)} %add_convert_fusion.2), channel_id=1, source_target_pairs={{0,2},{1,3},{2,0},{3,1},{4,6},{5,7},{6,4},{7,5},{8,10},{9,11},{10,... | collective-permute-start | bytes 331784 | tf_op jit(solution)/shard_map/ppermute | solution.py:19
  35.5 5.7 %collective-permute-start.18 = (bf16[224,128]{1,0:T(8,128)(2,1)S(1)}, bf16[224,128]{1,0:T(8,128)(2,1)S(1)}, u32[]{:S(2)}, u32[]{:S(2)}) collective-permute-start(bf16[224,128]{1,0:T(8,128)(2,1)S(1)} %add_convert_fusion.4), channel_id=1, source_target_pairs={{0,4},{1,5},{2,6},{3,7},{4,0},{5,1},{6,2},{7,3},{8,12},{9,13},{10,... | collective-permute-start | bytes 172040 | tf_op jit(solution)/shard_map/ppermute | solution.py:19
  36.4 9.1 %collective-permute-start.22 = (bf16[432,128]{1,0:T(8,128)(2,1)S(1)}, bf16[432,128]{1,0:T(8,128)(2,1)S(1)}, u32[]{:S(2)}, u32[]{:S(2)}) collective-permute-start(bf16[432,128]{1,0:T(8,128)(2,1)S(1)} %add_convert_fusion.1), channel_id=1, source_target_pairs={{0,4},{1,5},{2,6},{3,7},{4,0},{5,1},{6,2},{7,3},{8,12},{9,13},{10,... | collective-permute-start | bytes 331784 | tf_op jit(solution)/shard_map/ppermute | solution.py:19
  38.0 8.5 %collective-permute-start.11 = (bf16[128,128]{1,0:T(8,128)(2,1)S(1)}, bf16[128,128]{1,0:T(8,128)(2,1)S(1)}, u32[]{:S(2)}, u32[]{:S(2)}) collective-permute-start(bf16[128,128]{1,0:T(8,128)(2,1)S(1)} %get-tuple-element.90), channel_id=1, source_target_pairs={{0,1},{1,0},{2,3},{3,2},{4,5},{5,4},{6,7},{7,6},{8,9},{9,8},{10,11... | collective-permute-start | bytes 98312 | tf_op jit(solution)/shard_map/ppermute | solution.py:19
  41.1 5.5 %collective-permute-start.12 = (bf16[128,128]{1,0:T(8,128)(2,1)S(1)}, bf16[128,128]{1,0:T(8,128)(2,1)S(1)}, u32[]{:S(2)}, u32[]{:S(2)}) collective-permute-start(bf16[128,128]{1,0:T(8,128)(2,1)S(1)} %get-tuple-element.91), channel_id=1, source_target_pairs={{0,8},{1,2},{2,1},{3,4},{4,3},{5,6},{6,5},{7,15},{8,0},{9,10},{10,... | collective-permute-start | bytes 98312 | tf_op jit(solution)/shard_map/ppermute | solution.py:32
  41.2 5.5 %collective-permute-start.21 = (bf16[224,128]{1,0:T(8,128)(2,1)S(1)}, bf16[224,128]{1,0:T(8,128)(2,1)S(1)}, u32[]{:S(2)}, u32[]{:S(2)}) collective-permute-start(bf16[224,128]{1,0:T(8,128)(2,1)S(1)} %add_convert_fusion.3.mine), channel_id=1, source_target_pairs={{0,3},{1,2},{2,1},{3,0},{4,7},{5,6},{6,5},{7,4},{8,11},{9,10},{10,... | collective-permute-start | bytes 172040 | tf_op jit(solution)/shard_map/ppermute | solution.py:19
  43.4 5.1 %collective-permute-start.20 = (bf16[224,128]{1,0:T(8,128)(2,1)S(1)}, bf16[224,128]{1,0:T(8,128)(2,1)S(1)}, u32[]{:S(2)}, u32[]{:S(2)}) collective-permute-start(bf16[224,128]{1,0:T(8,128)(2,1)S(1)} %add_convert_fusion.3.mine), channel_id=1, source_target_pairs={{0,2},{1,3},{2,0},{3,1},{4,6},{5,7},{6,4},{7,5},{8,10},{9,11},{10,... | collective-permute-start | bytes 172040 | tf_op jit(solution)/shard_map/ppermute | solution.py:19
  45.5 3.1 %collective-permute-start.19 = (bf16[224,128]{1,0:T(8,128)(2,1)S(1)}, bf16[224,128]{1,0:T(8,128)(2,1)S(1)}, u32[]{:S(2)}, u32[]{:S(2)}) collective-permute-start(bf16[224,128]{1,0:T(8,128)(2,1)S(1)} %add_convert_fusion.3.mine), channel_id=1, source_target_pairs={{0,1},{1,0},{2,3},{3,2},{4,5},{5,4},{6,7},{7,6},{8,9},{9,8},{10,11... | collective-permute-start | bytes 172040 | tf_op jit(solution)/shard_map/ppermute | solution.py:19
  46.5 2.9 %collective-permute-start.23 = (bf16[432,128]{1,0:T(8,128)(2,1)S(1)}, bf16[432,128]{1,0:T(8,128)(2,1)S(1)}, u32[]{:S(2)}, u32[]{:S(2)}) collective-permute-start(bf16[432,128]{1,0:T(8,128)(2,1)S(1)} %add_convert_fusion.mine), channel_id=1, source_target_pairs={{0,1},{1,0},{2,3},{3,2},{4,5},{5,4},{6,7},{7,6},{8,9},{9,8},{10,11... | collective-permute-start | bytes 331784 | tf_op jit(solution)/shard_map/ppermute | solution.py:19
